TPU v7x, 512 devices: a whole 4x8x8 slice. The times are simulated.
512 devices in a mesh: mem: 8 (over y_lo, x), grid: 64 (over z, y_hi, core).
Axes of the slice: x: 4, y: 8 (y_hi: 4, y_lo: 2; y = y_hi * 2 + y_lo), z: 8, core: 2. Of those that a mesh axis runs over, the one named last changes fastest.
Arguments:
- hidden: bfloat16 [8, 28672, 1024], P('mem', 'grid'), may hold values from -16 to 16
- predictions: bfloat16 [8, 100, 28672], P('mem', None, 'grid'), may hold values from -6 to 6
- target: bfloat16 [100, 28672], P(None, 'grid'), may hold values from -6 to 6
- area: float32 [28672], P('grid'), may hold values from 1 to 10
- var_weight: float32 [100], replicated, may hold values from 0.5 to 4
- interior: int32 [28672], P('grid'), may hold values 0 or 1
- sources: int32 [8, 28672], P(None, 'grid'), may hold values from 0 to 575
- edge_weight: float32 [8, 28672], P(None, 'grid'), may hold values from 0.05 to 0.25
- w_node: bfloat16 [1024, 1024], P('grid'), may hold values from -0.1875 to 0.1875
- w_dec: bfloat16 [1024, 100], replicated, may hold values from -0.1875 to 0.1875
Outputs:
- hidden_grad: bfloat16 [8, 28672, 1024], P('mem', 'grid')
- weight_grad: float32 [1024, 1024], P('grid')
- decoder_grad: float32 [1024, 100], replicated
All inputs are finite; a program needn't handle non-finite values. No bound on the sum of `interior` on one device may be relied on, other than what follows from the above.
Results may differ from a plain program's by a relative error of at most 0.018.
Values may be sent and summed in bfloat16 or wider, within the bound.
No kernel may reach another device: no remote copies, remote signals or barrier semaphores. Data moves between devices by JAX's collectives and lax.ppermute only.
A program may use at most 64 MiB of HBM per device.

v0:
```python
import math

import jax
import jax.numpy as jnp
from jax import lax
from jax.sharding import PartitionSpec as P

K = 64
KNB = 8


norm_eps = 1e-05
alpha_fair = 0.95
root_half = 1.0 / math.sqrt(2.0)
inv_root_two_pi = 1.0 / math.sqrt(2.0 * math.pi)


def padded_2(block, sides, width):
    for axis, dim in sides:
        count = lax.axis_size(axis)
        forward = [(i, i + 1) for i in range(count - 1)]
        backward = [(target, source) for source, target in forward]
        low = lax.ppermute(
            lax.slice_in_dim(block, block.shape[dim] - width, None, axis=dim), axis, forward
        )
        high = lax.ppermute(lax.slice_in_dim(block, 0, width, axis=dim), axis, backward)
        block = jnp.concatenate([low, block, high], axis=dim)
    return block


def passed_along(shard, axis, by):
    size = lax.axis_size(axis)
    pairs = [(i, i + by) for i in range(size) if 0 <= i + by < size]
    return lax.ppermute(shard, axis, pairs)


def on_device(
    hidden, predictions, target, area, var_weight, interior, sources, edge_weight, w_node, w_dec
):
    members = lax.axis_size("mem")
    node_rows = hidden.shape[1]
    width = w_dec.shape[0]
    coef_pair = (1.0 - (1.0 - alpha_fair) / members) / (members * (members - 1))
    own_hidden = hidden[0]
    padded = padded_2(own_hidden, (("grid", 0),), K)
    aggregate = jnp.zeros((node_rows, width), jnp.float32)
    for slot in range(KNB):
        aggregate = aggregate + edge_weight[slot][:, None] * padded[sources[slot]].astype(
            jnp.float32
        )
    layer_input = own_hidden.astype(jnp.float32) + aggregate
    centre = jnp.mean(layer_input, axis=-1, keepdims=True)
    spread = jnp.mean((layer_input - centre) ** 2, axis=-1, keepdims=True)
    inv_std = lax.rsqrt(spread + norm_eps)
    unit = (layer_input - centre) * inv_std
    normed = unit.astype(jnp.bfloat16)
    full_weight = lax.all_gather(w_node, "grid", axis=0, tiled=True)
    pre_act = jnp.dot(normed, full_weight, preferred_element_type=jnp.float32)
    cdf_val = 0.5 * (1.0 + jax.scipy.special.erf(pre_act * root_half))
    layer_out = (layer_input + pre_act * cdf_val).astype(jnp.bfloat16)
    loss_weight = var_weight[:, None] * (area * interior.astype(jnp.float32))[None, :]
    every_pred = lax.all_gather(predictions, "mem", axis=0, tiled=True).astype(jnp.float32)
    own_pred = predictions[0].astype(jnp.float32)
    pair_sum = jnp.sum(jnp.sign(own_pred[None] - every_pred), axis=0)
    target_f = target.astype(jnp.float32)
    grad_f = loss_weight * (jnp.sign(own_pred - target_f) / members - coef_pair * pair_sum)
    pred_grad = grad_f.astype(jnp.bfloat16)
    out_grad = lax.dot_general(
        pred_grad, w_dec, (((0,), (1,)), ((), ())), preferred_element_type=jnp.float32
    )
    pdf_val = jnp.exp(-0.5 * pre_act * pre_act) * inv_root_two_pi
    pre_grad = (out_grad * (cdf_val + pre_act * pdf_val)).astype(jnp.bfloat16)
    normed_grad = lax.dot_general(
        pre_grad, full_weight, (((1,), (1,)), ((), ())), preferred_element_type=jnp.float32
    )
    mean_grad = jnp.mean(normed_grad, axis=-1, keepdims=True)
    mean_cross = jnp.mean(normed_grad * unit, axis=-1, keepdims=True)
    input_grad = out_grad + inv_std * (normed_grad - mean_grad - unit * mean_cross)
    padded_grad = jnp.zeros((node_rows + 2 * K, width), jnp.float32)
    for slot in range(KNB):
        padded_grad = padded_grad.at[sources[slot]].add(edge_weight[slot][:, None] * input_grad)
    core_grad = input_grad + padded_grad[K : K + node_rows]
    from_next = passed_along(padded_grad[:K].astype(jnp.bfloat16), "grid", -1).astype(jnp.float32)
    from_prev = passed_along(padded_grad[K + node_rows :].astype(jnp.bfloat16), "grid", 1).astype(
        jnp.float32
    )
    core_grad = core_grad.at[:K].add(from_prev)
    core_grad = core_grad.at[node_rows - K :].add(from_next)
    hidden_grad = core_grad.astype(jnp.bfloat16)[None]
    block_grad = lax.psum_scatter(
        lax.dot_general(
            normed, pre_grad, (((0,), (0,)), ((), ())), preferred_element_type=jnp.float32
        ),
        "grid",
        scatter_dimension=0,
        tiled=True,
    )
    weight_grad = lax.psum(block_grad, "mem")
    decoder_part = lax.dot_general(
        layer_out, pred_grad, (((0,), (1,)), ((), ())), preferred_element_type=jnp.float32
    )
    decoder_grad = lax.psum(decoder_part, ("mem", "grid"))
    return (hidden_grad, weight_grad, decoder_grad)


def solution(mesh):
    placed = (
        P("mem", "grid", None),
        P("mem", None, "grid"),
        P(None, "grid"),
        P("grid"),
        P(),
        P("grid"),
        P(None, "grid"),
        P(None, "grid"),
        P("grid", None),
        P(),
    )
    return jax.shard_map(
        on_device,
        mesh=mesh,
        in_specs=placed,
        out_specs=(P("mem", "grid", None), P("grid", None), P()),
        check_vma=False,
    )
```

profile of v0, /device:TPU:16, one launch (start us, length us, event | category | flops | bytes accessed | tf_op | source)
XLA Modules:
  0.0 624.7 jit_solution(8255171621078374530)
XLA Ops:
  15.5 31.1 %all_gather.6 = bf16[8,100,448]{2,1,0:T(8,128)(2,1)S(1)} all-gather(bf16[1,100,448]{2,1,0:T(8,128)(2,1)} %param.15), channel_id=1, replica_groups=mesh['mem'=8,'grid'=64] {'mem'}, dimensions={0}, use_global_device_ids=true | all-gather | bytes 806400 | tf_op jit(solution)/shard_map/all_gather | solution.py:62
  47.5 2.7 gather_fusion.7
  50.2 2.7 gather_fusion.6
  52.9 2.7 gather_fusion.5
  61.1 2.7 gather_fusion.2
  63.9 2.7 gather_fusion.1
  69.3 4.7 fusion.40
  74.4 25.5 %all-gather.2.cloned.1.call-done = bf16[1024,1024]{1,0:T(8,128)(2,1)} async-done(((bf16[16,1024]{1,0:T(8,128)(2,1)}), bf16[1024,1024]{1,0:T(8,128)(2,1)}) %all-gather.2.cloned.1.call-update) | async-done | bytes 2097168 | tf_op jit(solution)/shard_map/all_gather | solution.py:57
  99.9 2.8 fusion.37
  105.6 3.4 fusion.35
  109.6 3.3 fusion.39
  115.0 5.9 scatter_custom_fusion
  120.9 7.6 %scatter_custom_fusion.1 = f32[576,1024]{1,0:T(8,128)} fusion(f32[576,1024]{1,0:T(8,128)} %scatter_custom_fusion, s32[448]{0:T(512)S(1)} %bitcast.83, f32[448,1024]{1,0:T(8,128)S(1)} %multiply_add_fusion, f32[448]{0:T(512)S(1)} %bitcast.67), kind=kCustom, calls=%fused_computation.37 | custom fusion | flops 917504 | bytes 4196352 | tf_op jit(solution)/shard_map/scatter-add | solution.py:81
  128.5 7.5 %scatter_custom_fusion.2 = f32[576,1024]{1,0:T(8,128)} fusion(f32[576,1024]{1,0:T(8,128)} %scatter_custom_fusion.1, s32[448]{0:T(512)S(1)} %bitcast.81, f32[448,1024]{1,0:T(8,128)S(1)} %multiply_add_fusion, f32[448]{0:T(512)S(1)} %bitcast.65), kind=kCustom, calls=%fused_computation.35 | custom fusion | flops 917504 | bytes 4196352 | tf_op jit(solution)/shard_map/scatter-add | solution.py:81
  136.0 7.5 %scatter_custom_fusion.3 = f32[576,1024]{1,0:T(8,128)} fusion(f32[576,1024]{1,0:T(8,128)} %scatter_custom_fusion.2, s32[448]{0:T(512)S(1)} %bitcast.79, f32[448,1024]{1,0:T(8,128)S(1)} %multiply_add_fusion, f32[448]{0:T(512)S(1)} %bitcast.63), kind=kCustom, calls=%fused_computation.33 | custom fusion | flops 917504 | bytes 4196352 | tf_op jit(solution)/shard_map/scatter-add | solution.py:81
  143.5 7.7 %scatter_custom_fusion.4 = f32[576,1024]{1,0:T(8,128)} fusion(f32[576,1024]{1,0:T(8,128)} %scatter_custom_fusion.3, s32[448]{0:T(512)S(1)} %bitcast.77, f32[448,1024]{1,0:T(8,128)S(1)} %multiply_add_fusion, f32[448]{0:T(512)S(1)} %bitcast.61), kind=kCustom, calls=%fused_computation.31 | custom fusion | flops 917504 | bytes 4196352 | tf_op jit(solution)/shard_map/scatter-add | solution.py:81
  151.2 7.5 %scatter_custom_fusion.5 = f32[576,1024]{1,0:T(8,128)} fusion(f32[576,1024]{1,0:T(8,128)} %scatter_custom_fusion.4, s32[448]{0:T(512)S(1)} %bitcast.75, f32[448,1024]{1,0:T(8,128)S(1)} %multiply_add_fusion, f32[448]{0:T(512)S(1)} %bitcast.59), kind=kCustom, calls=%fused_computation.29 | custom fusion | flops 917504 | bytes 4196352 | tf_op jit(solution)/shard_map/scatter-add | solution.py:81
  158.6 7.5 %scatter_custom_fusion.6 = f32[576,1024]{1,0:T(8,128)} fusion(f32[576,1024]{1,0:T(8,128)} %scatter_custom_fusion.5, s32[448]{0:T(512)S(1)} %bitcast.73, f32[448,1024]{1,0:T(8,128)S(1)} %multiply_add_fusion, f32[448]{0:T(512)S(1)} %bitcast.57), kind=kCustom, calls=%fused_computation.27 | custom fusion | flops 917504 | bytes 4196352 | tf_op jit(solution)/shard_map/scatter-add | solution.py:81
  166.1 7.5 %scatter_custom_fusion.7 = f32[576,1024]{1,0:T(8,128)} fusion(f32[576,1024]{1,0:T(8,128)} %scatter_custom_fusion.6, s32[448]{0:T(512)S(1)} %bitcast.71, f32[448,1024]{1,0:T(8,128)S(1)} %multiply_add_fusion, f32[448]{0:T(512)S(1)} %bitcast.55), kind=kCustom, calls=%fused_computation.25 | custom fusion | flops 917504 | bytes 4196352 | tf_op jit(solution)/shard_map/scatter-add | solution.py:81
  181.1 4.3 collective-permute-start.3
  185.6 5.1 collective-permute-done.3
  190.7 72.2 %reduce-scatter.2.cloned.1.call-done = f32[16,1024]{1,0:T(8,128)} async-done(((f32[1024,1024]{1,0:T(8,128)}), f32[16,1024]{1,0:T(8,128)}) %reduce-scatter.2.cloned.1.call-update) | async-done | bytes 65552 | tf_op jit(solution)/shard_map/reduce_scatter | solution.py:90
  264.0 268.6 %all-reduce.5.cloned.1.call-done = f32[1024,100]{0,1:T(8,128)} async-done(((f32[1024,100]{0,1:T(8,128)}), f32[1024,100]{0,1:T(8,128)}) %all-reduce.5.cloned.1.call-update) | async-done | bytes 409616 | tf_op jit(solution)/shard_map/psum | solution.py:102
  532.6 82.1 %all-reduce.3.cloned.1.call-done = f32[16,1024]{1,0:T(8,128)} async-done(((f32[16,1024]{1,0:T(8,128)}), f32[16,1024]{1,0:T(8,128)}) %all-reduce.3.cloned.1.call-update) | async-done | bytes 65552 | tf_op jit(solution)/shard_map/psum | solution.py:98
  (80 shorter events, 35.1 us)
Async XLA Ops:
  7.2 95.5 %copy-start = (bf16[1024,100]{0,1:T(8,128)(2,1)S(1)}, bf16[1024,100]{0,1:T(8,128)(2,1)}, u32[]{:S(2)}) copy-start(bf16[1024,100]{0,1:T(8,128)(2,1)} %param.23) | copy-start | bytes 614404
  7.2 40.0 %copy-start.9 = (bf16[1,100,448]{2,1,0:T(8,128)(2,1)S(1)}, bf16[1,100,448]{2,1,0:T(8,128)(2,1)}, u32[]{:S(2)}) copy-start(bf16[1,100,448]{2,1,0:T(8,128)(2,1)} %param.15) | copy-start | bytes 268804
  7.2 39.9 %copy-start.12 = (f32[448]{0:T(512)S(1)}, f32[448]{0:T(512)}, u32[]{:S(2)}) copy-start(f32[448]{0:T(512)} %param.17) | copy-start | bytes 5380
  7.2 39.9 %copy-start.13 = (s32[448]{0:T(512)S(1)}, s32[448]{0:T(512)}, u32[]{:S(2)}) copy-start(s32[448]{0:T(512)} %param.19) | copy-start | bytes 5380
  7.2 39.9 %copy-start.11 = (f32[8,448]{1,0:T(8,128)S(1)}, f32[8,448]{1,0:T(8,128)}, u32[]{:S(2)}) copy-start(f32[8,448]{1,0:T(8,128)} %param.21) | copy-start | bytes 43012
  7.2 40.0 %copy-start.10 = (bf16[100,448]{1,0:T(8,128)(2,1)S(1)}, bf16[100,448]{1,0:T(8,128)(2,1)}, u32[]{:S(2)}) copy-start(bf16[100,448]{1,0:T(8,128)(2,1)} %param.16) | copy-start | bytes 268804
  7.2 40.0 %copy-start.14 = (f32[100]{0:T(128)S(1)}, f32[100]{0:T(128)}, u32[]{:S(2)}) copy-start(f32[100]{0:T(128)} %param.18) | copy-start | bytes 1204
  7.2 92.6 %all-gather.2.cloned.1.call-start = ((), (), s32[]{:S(2)}) async-start(), calls=%async_computation.1 | async-start | bytes 2129920 | tf_op jit(solution)/shard_map/all_gather | solution.py:57
  8.0 39.4 %copy-start.5 = (bf16[1,448,1024]{2,1,0:T(8,128)(2,1)S(1)}, bf16[1,448,1024]{2,1,0:T(8,128)(2,1)}, u32[]{:S(2)}) copy-start(bf16[1,448,1024]{2,1,0:T(8,128)(2,1)} %param.14) | copy-start | bytes 2752516
  8.0 254.9 %reduce-scatter.2.cloned.1.call-start = ((), (), s32[]{:S(2)}) async-start(), calls=%async_computation.2 | async-start | bytes 4259840 | tf_op jit(solution)/shard_map/reduce_scatter | solution.py:90
  9.1 38.3 %collective-permute-start.1 = (bf16[64,1024]{1,0:T(8,128)(2,1)S(1)}, bf16[64,1024]{1,0:T(8,128)(2,1)S(1)}, u32[]{:S(2)}, u32[]{:S(2)}) collective-permute-start(bf16[64,1024]{1,0:T(8,128)(2,1)S(1)} %get-tuple-element.34), channel_id=1, source_target_pairs={{1,0},{2,1},{3,2},{4,3},{5,4},{6,5},{7,6},{8,7},{9,8},{10,9},{11,1... | collective-permute-start | bytes 393224 | tf_op jit(solution)/shard_map/ppermute | solution.py:26
  11.0 36.3 %collective-permute-start = (bf16[64,1024]{1,0:T(8,128)(2,1)S(1)}, bf16[64,1024]{1,0:T(8,128)(2,1)S(1)}, u32[]{:S(2)}, u32[]{:S(2)}) collective-permute-start(bf16[64,1024]{1,0:T(8,128)(2,1)S(1)} %get-tuple-element.33), channel_id=1, source_target_pairs={{0,1},{1,2},{2,3},{3,4},{4,5},{5,6},{6,7},{7,8},{8,9},{9,10},{10,1... | collective-permute-start | bytes 393224 | tf_op jit(solution)/shard_map/ppermute | solution.py:23
  74.1 35.5 %copy-start.1 = (f32[448,1024]{1,0:T(8,128)}, f32[448,1024]{1,0:T(8,128)S(1)}, u32[]{:S(2)}) copy-start(f32[448,1024]{1,0:T(8,128)S(1)} %get-tuple-element.30) | copy-start | bytes 5505028
  102.7 2.1 copy-start.6
  104.7 0.9 copy-start.15
  109.0 423.5 %all-reduce.5.cloned.1.call-start = ((), (), s32[]{:S(2)}) async-start(), calls=%async_computation.4 | async-start | bytes 851968 | tf_op jit(solution)/shard_map/psum | solution.py:102
  109.6 3.4 copy-start.8
  173.6 4.5 copy-start.3
  175.6 4.1 copy-start.2
  175.6 4.1 copy-start.7
  175.6 9.9 %collective-permute-start.2 = (bf16[64,1024]{1,0:T(8,128)(2,1)S(1)}, bf16[64,1024]{1,0:T(8,128)(2,1)S(1)}, u32[]{:S(2)}, u32[]{:S(2)}) collective-permute-start(bf16[64,1024]{1,0:T(8,128)(2,1)S(1)} %get-tuple-element.32), channel_id=1, source_target_pairs={{0,1},{1,2},{2,3},{3,4},{4,5},{5,6},{6,7},{7,8},{8,9},{9,10},{10,1... | collective-permute-start | bytes 393224 | tf_op jit(solution)/shard_map/ppermute | solution.py:34
  179.7 5.8 copy-start.4
  181.1 9.5 %collective-permute-start.3 = (bf16[64,1024]{1,0:T(8,128)(2,1)S(1)}, bf16[64,1024]{1,0:T(8,128)(2,1)S(1)}, u32[]{:S(2)}, u32[]{:S(2)}) collective-permute-start(bf16[64,1024]{1,0:T(8,128)(2,1)S(1)} %get-tuple-element.31), channel_id=1, source_target_pairs={{1,0},{2,1},{3,2},{4,3},{5,4},{6,5},{7,6},{8,7},{9,8},{10,9},{11,1... | collective-permute-start | bytes 393224 | tf_op jit(solution)/shard_map/ppermute | solution.py:34
  185.4 429.3 %all-reduce.3.cloned.1.call-start = ((), (), s32[]{:S(2)}) async-start(), calls=%async_computation.3 | async-start | bytes 131072 | tf_op jit(solution)/shard_map/psum | solution.py:98
Sparse Core Ops, SparseCore 0:
  11.4 88.4 all-gather.1
  109.2 153.6 reduce-scatter.1
  269.2 263.2 all-reduce.4
  535.3 79.3 all-reduce.2
where the time goes:
time: 634 us; the launch traced here: 625 us
  waiting for transfers between devices  454 us (72%)
  other arithmetic  73.3 us (12%)
  blocking collectives  31.1 us (5%)
  local copies, waits for them, and re-layouts  27.2 us (4%)
  between operations  14.4 us (2%)
  matrix products  12.9 us (2%)
  starting transfers between devices  11.7 us (2%)
    psum x1, waiting for transfers between devices, on_device(): decoder_grad = lax.psum(decoder_part, ('mem', 'grid'))  269 us
    psum x1, waiting for transfers between devices, on_device(): weight_grad = lax.psum(block_grad, 'mem')  82.1 us
    reduce_scatter x1, waiting for transfers between devices, on_device(): lax.psum_scatter(lax.dot_general(normed, pre_grad, (((0,), (0,)), ((), ()...  72.2 us
    scatter-add x8, other arithmetic, on_device(): padded_grad.at[sources[slot]].add(edge_weight[slot][:, None] * input_grad)  58.6 us
    all_gather x1, blocking collectives, on_device(): lax.all_gather(predictions, 'mem', axis=0, tiled=True).astype(jnp.float32)  31.1 us
    all_gather x1, waiting for transfers between devices, on_device(): full_weight = lax.all_gather(w_node, 'grid', axis=0, tiled=True)  25.5 us
    gather x8, local copies, waits for them, and re-layouts, on_device(): padded[sources[slot]].astype(jnp.float32)  21.8 us
  transfers between devices with their start and end apart: 8, of which 5 were waited for; matrix products, arithmetic and copies ran while one was open for 16% of the time, Pallas kernels for 0%

commit v1 on v0

v1 whole, which is shorter than its diff:
```python
import math

import jax
import jax.numpy as jnp
from jax import lax
from jax.experimental import pallas as pl
from jax.experimental.pallas import tpu as pltpu
from jax.sharding import PartitionSpec as P

K = 64
KNB = 8
LANES = 128

norm_eps = 1e-05
alpha_fair = 0.95
root_half = 1.0 / math.sqrt(2.0)
inv_root_two_pi = 1.0 / math.sqrt(2.0 * math.pi)

f32 = jnp.float32
bf16 = jnp.bfloat16
VMEM = pl.BlockSpec(memory_space=pltpu.VMEM)
SMEM = pl.BlockSpec(memory_space=pltpu.SMEM)


def call(body, out, args, specs, scratch=(), flops=0, trans=0, mib=32, aliases=None):
    moved = sum(a.size * a.dtype.itemsize for a in args)
    moved += sum(math.prod(o.shape) * jnp.dtype(o.dtype).itemsize for o in out)
    return pl.pallas_call(
        body,
        out_shape=out,
        in_specs=specs,
        out_specs=[VMEM] * len(out),
        scratch_shapes=list(scratch),
        input_output_aliases=aliases or {},
        cost_estimate=pl.CostEstimate(flops=flops, bytes_accessed=moved, transcendentals=trans),
        compiler_params=pltpu.CompilerParams(vmem_limit_bytes=mib * 2**20),
    )(*args)


def shape(dims, dtype):
    return jax.ShapeDtypeStruct(dims, dtype)


def dot(a, b, ca=1, cb=0):
    return lax.dot_general(a, b, (((ca,), (cb,)), ((), ())), preferred_element_type=f32)


def edges_body(src_ref, ew_ref, at_ref):
    rows = at_ref.shape[0]
    nodes = at_ref.shape[1]
    step = 64
    for r in range(0, rows, step):
        j = lax.broadcasted_iota(jnp.int32, (step, nodes), 0) + r
        acc = jnp.zeros((step, nodes), f32)
        for s in range(KNB):
            acc += jnp.where(src_ref[s : s + 1, :] == j, ew_ref[s : s + 1, :], 0.0)
        at_ref[r : r + step, :] = acc.astype(bf16)


def norm_body(core_ref, own_ref, low_ref, high_ref, at_ref, normed_ref, rstd_ref, keep_ref, send_ref):
    core = core_ref[0]
    nodes, width = own_ref.shape
    half = width // 2
    agg = dot(at_ref[0:K, :], low_ref[...], 0, 0)
    agg += dot(at_ref[K : K + nodes, :], own_ref[...], 0, 0)
    agg += dot(at_ref[K + nodes :, :], high_ref[...], 0, 0)
    li = own_ref[...].astype(f32) + agg
    mean = jnp.mean(li, axis=-1, keepdims=True)
    dev = li - mean
    rstd = lax.rsqrt(jnp.mean(dev * dev, axis=-1, keepdims=True) + norm_eps)
    normed = (dev * rstd).astype(bf16)
    normed_ref[...] = normed
    rstd_ref[...] = jnp.broadcast_to(rstd, rstd_ref.shape)
    send_ref[:, 0:width] = normed
    lo = li[:, 0:half].astype(bf16)
    hi = li[:, half:].astype(bf16)

    @pl.when(core == 0)
    def _():
        keep_ref[...] = lo
        send_ref[:, width:] = hi

    @pl.when(core != 0)
    def _():
        keep_ref[...] = hi
        send_ref[:, width:] = lo


def fill_weight(wg_ref, w_ref):
    groups = w_ref.shape[0] // 32
    cols = w_ref.shape[1] // LANES
    for g in range(groups):
        for c in range(2):
            for x in range(cols):
                w_ref[g * 32 + c * 16 : g * 32 + c * 16 + 16, x * LANES : (x + 1) * LANES] = wg_ref[
                    c * cols + x, g * 16 : g * 16 + 16, :
                ]


def main_body(core_ref, wg_ref, no_ref, got_ref, keep_ref, po_ref, pp_ref, wd_ref, send_ref, pre_ref, w_ref, lo_ref):
    core = core_ref[0]
    nodes, width = no_ref.shape
    half = width // 2
    fill_weight(wg_ref, w_ref)
    wd = wd_ref[pl.ds(pl.multiple_of(core * half, half), half), :]
    step = nodes // 2
    for part in range(2):
        p_ref = (po_ref, pp_ref)[part]
        for r in range(0, nodes, step):
            n = no_ref[r : r + step, :] if part == 0 else got_ref[r : r + step, 0:width]
            li = keep_ref[r : r + step, :] if part == 0 else got_ref[r : r + step, width:]
            pre = dot(n, w_ref[...])
            og = dot(p_ref[r : r + step, :], wd, 1, 1)
            cdf = 0.5 * (1.0 + lax.erf(pre * root_half))
            pdf = jnp.exp(-0.5 * pre * pre) * inv_root_two_pi
            at = part * nodes + r
            lo_ref[at : at + step, :] = (li.astype(f32) + pre * cdf).astype(bf16)
            pre_ref[at : at + step, :] = (og * (cdf + pre * pdf)).astype(bf16)
    cols = half // LANES
    rows = 256
    groups = width // 32
    for q in range(0, width, rows):
        res = dot(no_ref[:, q : q + rows], pre_ref[0:nodes, :], 0, 0)
        res += dot(got_ref[:, q : q + rows], pre_ref[nodes:, :], 0, 0)
        res = res.astype(bf16)
        for g in range(rows // 32):
            for c in range(2):
                for x in range(cols):
                    at = (q // 32 + g) * 16
                    send_ref[c * cols + x, at : at + 16, :] = res[
                        g * 32 + c * 16 : g * 32 + c * 16 + 16, x * LANES : (x + 1) * LANES
                    ]
    dec = dot(lo_ref[0:nodes, :], po_ref[...], 0, 0) + dot(lo_ref[nodes:, :], pp_ref[...], 0, 0)
    dec = dec.astype(bf16)
    per = half // 8
    for m in range(8):
        send_ref[m, groups * 16 : groups * 16 + per, :] = dec[m * per : (m + 1) * per, :]
        send_ref[m, groups * 16 + per :, :] = jnp.zeros((send_ref.shape[1] - groups * 16 - per, LANES), bf16)


def sum_mem_body(got_ref, out_ref):
    groups = out_ref.shape[0]
    per = out_ref.shape[1] - 16
    total = got_ref[0, 0 : groups * 16 + per, :].astype(f32)
    for m in range(1, 8):
        total += got_ref[m, 0 : groups * 16 + per, :].astype(f32)
    total = total.astype(bf16)
    for g in range(groups):
        out_ref[g, 0:16, :] = total[g * 16 : g * 16 + 16, :]
        out_ref[g, 16:, :] = total[groups * 16 :, :]


def sum_grid_body(got_ref, out_ref):
    total = got_ref[0].astype(f32)
    for g in range(1, got_ref.shape[0]):
        total += got_ref[g].astype(f32)
    total = total.astype(bf16)
    for m in range(out_ref.shape[0]):
        out_ref[m] = total


def final_body(core_ref, got_ref, weight_ref, dec_ref):
    core = core_ref[0]
    per = got_ref.shape[1] - 16
    cols = weight_ref.shape[1] // 2 // LANES
    vars_ = dec_ref.shape[1]
    half = dec_ref.shape[0] // 2
    for c in range(2):
        for x in range(cols):
            lane = c * half + x * LANES
            weight_ref[:, lane : lane + LANES] = got_ref[(core * cols + x) * 2 + c, 0:16, :].astype(f32)
        for m in range(8):
            at = c * half + m * per
            dec_ref[at : at + per, :] = got_ref[m * 2 + c, 16:, 0:vars_].astype(f32)


def back_body(wg_ref, pre_ref, own_ref, send_ref, w_ref):
    nodes = own_ref.shape[0]
    fill_weight(wg_ref, w_ref)
    own_ref[...] = dot(pre_ref[0:nodes, :], w_ref[...], 1, 1)
    send_ref[...] = dot(pre_ref[nodes:, :], w_ref[...], 1, 1).astype(bf16)


def scatter_body(ng_ref, got_ref, no_ref, rstd_ref, po_ref, wd_ref, at_ref, mid_ref, edge_ref, prev_ref, next_ref):
    nodes = ng_ref.shape[0]
    ng = ng_ref[...] + got_ref[...].astype(f32)
    unit = no_ref[...].astype(f32)
    og = dot(po_ref[...], wd_ref[...], 1, 1)
    mean_g = jnp.mean(ng, axis=-1, keepdims=True)
    mean_c = jnp.mean(ng * unit, axis=-1, keepdims=True)
    ig = og + rstd_ref[:, 0:1] * (ng - mean_g - unit * mean_c)
    ib = ig.astype(bf16)
    prev_ref[...] = dot(at_ref[0:K, :], ib).astype(bf16)
    next_ref[...] = dot(at_ref[K + nodes :, :], ib).astype(bf16)
    core = ig + dot(at_ref[K : K + nodes, :], ib)
    mid_ref[...] = core.astype(bf16)
    edge_ref[0:K, :] = core[0:K, :]
    edge_ref[K:, :] = core[nodes - K :, :]


def join_body(mid_ref, edge_ref, prev_ref, next_ref, out_ref):
    nodes = mid_ref.shape[0]
    out_ref[0, 0:K, :] = (edge_ref[0:K, :] + prev_ref[...].astype(f32)).astype(bf16)
    out_ref[0, K : nodes - K, :] = mid_ref[K : nodes - K, :]
    out_ref[0, nodes - K :, :] = (edge_ref[K:, :] + next_ref[...].astype(f32)).astype(bf16)


def passed_along(shard, by):
    size = lax.axis_size(("pair", "core"))
    pairs = [(i, i + by) for i in range(size) if 0 <= i + by < size]
    return lax.ppermute(shard, ("pair", "core"), pairs)


def on_device(
    hidden, predictions, target, area, var_weight, interior, sources, edge_weight, w_node, w_dec
):
    members = lax.axis_size("mem")
    groups = lax.axis_size("pair")
    nodes, width = hidden.shape[1:]
    half = width // 2
    cols = half // LANES
    variables = w_dec.shape[1]
    coef_pair = (1.0 - (1.0 - alpha_fair) / members) / (members * (members - 1))
    core = lax.axis_index("core")
    member = lax.axis_index("mem")
    core_arg = core.astype(jnp.int32).reshape(1)
    own = hidden[0]
    def other_core(a):
        return lax.ppermute(a, "core", [(0, 1), (1, 0)])

    def over_grid(a):
        return lax.all_to_all(a, "pair", 0, 0, tiled=True)

    def over_mem(a):
        return lax.all_to_all(a, "mem", 0, 0, tiled=True)

    row_half, col_block = member // cols, member % cols
    tile_own = lax.dynamic_slice(w_node, (0, core * half + col_block * LANES), (16, LANES))
    tile_out = lax.dynamic_slice(w_node, (0, (1 - core) * half + col_block * LANES), (16, LANES))
    tile_got = other_core(tile_out)
    tile = jnp.where(core == row_half, tile_own, tile_got)
    shards = over_grid(jnp.broadcast_to(tile[None], (groups, 16, LANES)))
    weight = over_mem(jnp.broadcast_to(shards.reshape(1, groups * 16, LANES), (members, groups * 16, LANES)))

    low = passed_along(own[nodes - K :], 1)
    high = passed_along(own[:K], -1)
    every_pred = over_mem(jnp.broadcast_to(predictions, (members,) + predictions.shape[1:]))

    (at,) = call(
        edges_body, [shape((nodes + 2 * K, nodes), bf16)], (sources, edge_weight), [VMEM] * 2,
    )
    normed, rstd, keep, send = call(
        norm_body,
        [shape((nodes, width), bf16), shape((nodes, LANES), f32), shape((nodes, half), bf16),
         shape((nodes, width + half), bf16)],
        (core_arg, own, low, high, at),
        [SMEM] + [VMEM] * 4,
        flops=2 * nodes * (nodes + 2 * K) * width,
    )
    got = other_core(send)

    own_pred = predictions[0].astype(f32)
    loss_weight = var_weight[:, None] * (area * interior.astype(f32))[None, :]
    pair_sum = jnp.sum(jnp.sign(own_pred[None] - every_pred.astype(f32)), axis=0)
    grad_f = loss_weight * (jnp.sign(own_pred - target.astype(f32)) / members - coef_pair * pair_sum)
    pred_grad = jnp.pad(grad_f.astype(bf16), ((0, LANES - variables), (0, 0))).T
    pred_got = other_core(pred_grad)
    dec_pad = jnp.pad(w_dec, ((0, 0), (0, LANES - variables)))

    per = half // members
    sent_rows = groups * 16 + 2 * per
    parts, pre_grad = call(
        main_body,
        [shape((members, sent_rows, LANES), bf16), shape((2 * nodes, half), bf16)],
        (core_arg, weight, normed, got, keep, pred_grad, pred_got, dec_pad),
        [SMEM] + [VMEM] * 7,
        scratch=[pltpu.VMEM((width, half), bf16), pltpu.VMEM((2 * nodes, half), bf16)],
        flops=4 * 2 * nodes * width * half,
        trans=4 * nodes * half,
    )
    mem_parts = over_mem(parts)
    (grid_out,) = call(
        sum_mem_body, [shape((groups, 16 + per, LANES), bf16)], (mem_parts,), [VMEM],
    )
    grid_parts = over_grid(grid_out)
    (last_out,) = call(
        sum_grid_body, [shape((2 * members, 16 + per, LANES), bf16)], (grid_parts,), [VMEM],
    )
    last = lax.all_to_all(last_out, ("mem", "core"), 0, 0, tiled=True)
    weight_grad, decoder_grad = call(
        final_body,
        [shape((16, width), f32), shape((width, variables), f32)],
        (core_arg, last),
        [SMEM, VMEM],
    )

    ng_own, ng_send = call(
        back_body,
        [shape((nodes, width), f32), shape((nodes, width), bf16)],
        (weight, pre_grad),
        [VMEM] * 2,
        scratch=[pltpu.VMEM((width, half), bf16)],
        flops=4 * nodes * width * half,
    )
    ng_got = other_core(ng_send)
    mid, edge, to_prev, to_next = call(
        scatter_body,
        [shape((nodes, width), bf16), shape((2 * K, width), f32), shape((K, width), bf16),
         shape((K, width), bf16)],
        (ng_own, ng_got, normed, rstd, pred_grad, dec_pad, at),
        [VMEM] * 7,
        flops=2 * nodes * (nodes + 2 * K) * width,
    )
    from_next = passed_along(to_prev, -1)
    from_prev = passed_along(to_next, 1)
    (hidden_grad,) = call(
        join_body, [shape((1, nodes, width), bf16)], (mid, edge, from_prev, from_next), [VMEM] * 4,
    )
    return (hidden_grad, weight_grad, decoder_grad)


def solution(mesh):
    members, blocks = mesh.shape["mem"], mesh.shape["grid"]
    split = jax.sharding.Mesh(
        mesh.devices.reshape(members, blocks // 2, 2), ("mem", "pair", "core")
    )
    grid = ("pair", "core")
    placed = (
        P("mem", grid, None),
        P("mem", None, grid),
        P(None, grid),
        P(grid),
        P(),
        P(grid),
        P(None, grid),
        P(None, grid),
        P(grid, None),
        P(),
    )
    return jax.shard_map(
        on_device,
        mesh=split,
        in_specs=placed,
        out_specs=(P("mem", grid, None), P(grid, None), P()),
        check_vma=False,
    )
```

time: 634 us -> 170 us (0.27)
  the two profiles are of different devices: /device:TPU:16 before, /device:TPU:1 now
where the time goes in v1:
time: 170 us; the launch traced here: 167 us
  blocking collectives  63.4 us (37%)
  starting transfers between devices  51.6 us (30%)
  waiting for transfers between devices  17.5 us (10%)
  Pallas kernels  17.1 us (10%)
  local copies, waits for them, and re-layouts  14.2 us (8%)
  other arithmetic  2.59 us (2%)
    all_to_all x2, blocking collectives, over_mem(): return lax.all_to_all(a, 'mem', 0, 0, tiled=True)  41.9 us
    all_to_all x1, blocking collectives, over_grid(): return lax.all_to_all(a, 'pair', 0, 0, tiled=True)  21.4 us
    ppermute x4, starting transfers between devices, other_core(): return lax.ppermute(a, 'core', [(0, 1), (1, 0)])  17.4 us
    pallas_call x9, Pallas kernels, call(): pl.pallas_call(body, out_shape=out, in_specs=specs, out_specs=[VMEM] * le...  17.1 us
    ppermute x4, starting transfers between devices, passed_along(): return lax.ppermute(shard, ('pair', 'core'), pairs)  12.3 us
    all_to_all x1, starting transfers between devices, on_device(): last = lax.all_to_all(last_out, ('mem', 'core'), 0, 0, tiled=True)  11.9 us
    unnamed x38, local copies, waits for them, and re-layouts  11 us
    all_to_all x1, waiting for transfers between devices, over_grid(): return lax.all_to_all(a, 'pair', 0, 0, tiled=True)  9.42 us
  transfers between devices with their start and end apart: 11, of which 4 were waited for; matrix products, arithmetic and copies ran while one was open for 2% of the time, Pallas kernels for 6%

profile of v1, /device:TPU:1, one launch (start us, length us, event | category | flops | bytes accessed | tf_op | source)
XLA Modules:
  0.0 167.4 jit_solution(4161085411206574773)
XLA Ops:
  1.3 8.8 %collective-permute-start = (bf16[16,128]{1,0:T(8,128)(2,1)S(1)}, bf16[16,128]{1,0:T(8,128)(2,1)S(1)}, u32[]{:S(2)}, u32[]{:S(2)}) collective-permute-start(bf16[16,128]{1,0:T(8,128)(2,1)S(1)} %constant_dynamic-slice_fusion), channel_id=1, source_target_pairs={{0,1},{1,0},{2,3},{3,2},{4,5},{5,4},{6,7},{7,6},{8,9},{9,8},{10,11... | collective-permute-start | bytes 12296 | tf_op jit(solution)/shard_map/ppermute | solution.py:229
  11.6 21.4 %all_to_all.30 = bf16[32,16,128]{2,1,0:T(8,128)(2,1)S(1)} all-to-all(bf16[32,16,128]{2,1,0:T(8,128)(2,1)S(1)} %broadcast_in_dim.8), channel_id=1, replica_groups=mesh['mem'=8,'pair'=32,'core'=2] {'pair'}, dimensions={0} | all-to-all | bytes 262144 | tf_op jit(solution)/shard_map/all_to_all | solution.py:232
  34.0 15.4 %all_to_all.31 = bf16[8,100,448]{2,1,0:T(8,128)(2,1)} all-to-all(bf16[8,100,448]{2,1,0:T(8,128)(2,1)S(1)} %broadcast_in_dim.11), channel_id=1, replica_groups=mesh['mem'=8,'pair'=32,'core'=2] {'mem'}, dimensions={0} | all-to-all | bytes 1433600 | tf_op jit(solution)/shard_map/all_to_all | solution.py:235
  50.5 3.6 %all-to-all-start.1 = ((bf16[8,512,128]{2,1,0:T(8,128)(2,1)}), bf16[8,512,128]{2,1,0:T(8,128)(2,1)S(1)}, u32[]{:S(2)}, u32[]{:S(2)}) async-start(bf16[8,512,128]{2,1,0:T(8,128)(2,1)} %broadcast_in_dim.10), calls=%async_computation.1 | async-start | bytes 2097152 | tf_op jit(solution)/shard_map/all_to_all | solution.py:235
  54.1 5.5 %collective-permute-start.2 = (bf16[64,1024]{1,0:T(8,128)(2,1)S(1)}, bf16[64,1024]{1,0:T(8,128)(2,1)S(1)}, u32[]{:S(2)}, u32[]{:S(2)}) collective-permute-start(bf16[64,1024]{1,0:T(8,128)(2,1)S(1)} %get-tuple-element.43), channel_id=1, source_target_pairs={{1,0},{2,1},{3,2},{4,3},{5,4},{6,5},{7,6},{8,7},{9,8},{10,9},{11,1... | collective-permute-start | bytes 393224 | tf_op jit(solution)/shard_map/ppermute | solution.py:211
  59.6 2.5 %collective-permute-start.1 = (bf16[64,1024]{1,0:T(8,128)(2,1)S(1)}, bf16[64,1024]{1,0:T(8,128)(2,1)S(1)}, u32[]{:S(2)}, u32[]{:S(2)}) collective-permute-start(bf16[64,1024]{1,0:T(8,128)(2,1)S(1)} %get-tuple-element.44), channel_id=1, source_target_pairs={{0,1},{1,2},{2,3},{3,4},{4,5},{5,6},{6,7},{7,8},{8,9},{9,10},{10,1... | collective-permute-start | bytes 393224 | tf_op jit(solution)/shard_map/ppermute | solution.py:211
  63.2 2.3 %collective-permute-done.1.low_ref = bf16[64,1024]{1,0:T(8,128)(2,1)S(1)} collective-permute-done((bf16[64,1024]{1,0:T(8,128)(2,1)S(1)}, bf16[64,1024]{1,0:T(8,128)(2,1)S(1)}, u32[]{:S(2)}, u32[]{:S(2)}) %collective-permute-start.1) | collective-permute-done | bytes 131104 | tf_op jit(solution)/shard_map/ppermute | solution.py:211
  65.5 2.7 %shard_map.122 = (bf16[448,1024]{1,0:T(8,128)(2,1)S(1)}, f32[448,128]{1,0:T(8,128)S(1)}, bf16[448,512]{1,0:T(8,128)(2,1)S(1)}, bf16[448,1536]{1,0:T(8,128)(2,1)}) custom-call(s32[1]{0:T(128)} %bitcast.1.core_ref, bf16[448,1024]{1,0:T(8,128)(2,1)S(1)} %bitcast.14, bf16[64,1024]{1,0:T(8,128)(2,1)S(1)} %collective-permute-done.1.low_ref, ...), custom_call_target="tpu_custom_call" | custom-call | flops 528482304 | bytes 4677636 | tf_op jit(solution)/shard_map/pallas_call | solution.py:28
  69.8 2.0 %collective-permute-start.3 = (bf16[448,1536]{1,0:T(8,128)(2,1)}, bf16[448,1536]{1,0:T(8,128)(2,1)}, u32[]{:S(2)}, u32[]{:S(2)}) collective-permute-start(bf16[448,1536]{1,0:T(8,128)(2,1)} %get-tuple-element.18), channel_id=1, source_target_pairs={{0,1},{1,0},{2,3},{3,2},{4,5},{5,4},{6,7},{7,6},{8,9},{9,8},{10,11... | collective-permute-start | bytes 4128776 | tf_op jit(solution)/shard_map/ppermute | solution.py:229
  72.4 1.7 %sign_reduce_fusion = f32[100,448]{1,0:T(8,128)S(1)} fusion(bf16[8,100,448]{2,1,0:T(8,128)(2,1)} %all_to_all.31, f32[100,448]{1,0:T(8,128)S(1)} %copy.37), kind=kLoop, calls=%fused_computation | loop fusion | flops 1388800 | bytes 1075200 | tf_op jit(solution)/shard_map/reduce_sum | solution.py:264
  74.4 2.4 %collective-permute-start.4 = (bf16[448,128]{1,0:T(8,128)(2,1)S(1)}, bf16[448,128]{1,0:T(8,128)(2,1)S(1)}, u32[]{:S(2)}, u32[]{:S(2)}) collective-permute-start(bf16[448,128]{1,0:T(8,128)(2,1)S(1)} %pad_bitcast_fusion.po_ref), channel_id=1, source_target_pairs={{0,1},{1,0},{2,3},{3,2},{4,5},{5,4},{6,7},{7,6},{8,9},{9,8},{10,11... | collective-permute-start | bytes 344072 | tf_op jit(solution)/shard_map/ppermute | solution.py:229
  78.1 1.5 copy-done.3
  79.6 4.8 %shard_map.123 = (bf16[8,640,128]{2,1,0:T(8,128)(2,1)S(1)}, bf16[896,512]{1,0:T(8,128)(2,1)S(1)}) custom-call(s32[1]{0:T(128)} %bitcast.1.core_ref, bf16[8,512,128]{2,1,0:T(8,128)(2,1)S(1)} %all-to-all-done.1.wg_ref, bf16[448,1024]{1,0:T(8,128)(2,1)S(1)} %copy-done.3, bf16[448,1536]{1,0:T(8,128)(2,1)} %collective-permute-done.3.got_ref, ...), custom_call_target="tpu_custom_call" | custom-call | flops 1879048192 | bytes 6520836 | tf_op jit(solution)/shard_map/pallas_call | solution.py:28
  85.4 26.6 %all_to_all.32.got_ref = bf16[8,640,128]{2,1,0:T(8,128)(2,1)S(1)} all-to-all(bf16[8,640,128]{2,1,0:T(8,128)(2,1)S(1)} %get-tuple-element.28), channel_id=1, replica_groups=mesh['mem'=8,'pair'=32,'core'=2] {'mem'}, dimensions={0} | all-to-all | bytes 2621440 | tf_op jit(solution)/shard_map/all_to_all | solution.py:235
  112.9 6.4 %all-to-all-start.4 = ((bf16[32,80,128]{2,1,0:T(8,128)(2,1)}), bf16[32,80,128]{2,1,0:T(8,128)(2,1)S(1)}, u32[]{:S(2)}, u32[]{:S(2)}) async-start(bf16[32,80,128]{2,1,0:T(8,128)(2,1)} %shard_map.127), calls=%async_computation.4 | async-start | bytes 1310720 | tf_op jit(solution)/shard_map/all_to_all | solution.py:232
  119.4 1.2 copy-done.1
  121.8 2.1 %shard_map.124 = (f32[448,1024]{1,0:T(8,128)S(1)}, bf16[448,1024]{1,0:T(8,128)(2,1)}) custom-call(bf16[8,512,128]{2,1,0:T(8,128)(2,1)S(1)} %copy-done.1, bf16[896,512]{1,0:T(8,128)(2,1)S(1)} %copy-done.11), custom_call_target="tpu_custom_call" | custom-call | flops 939524096 | bytes 4718592 | tf_op jit(solution)/shard_map/pallas_call | solution.py:28
  123.9 4.2 %collective-permute-start.5 = (bf16[448,1024]{1,0:T(8,128)(2,1)}, bf16[448,1024]{1,0:T(8,128)(2,1)}, u32[]{:S(2)}, u32[]{:S(2)}) collective-permute-start(bf16[448,1024]{1,0:T(8,128)(2,1)} %get-tuple-element.22), channel_id=1, source_target_pairs={{0,1},{1,0},{2,3},{3,2},{4,5},{5,4},{6,7},{7,6},{8,9},{9,8},{10,11... | collective-permute-start | bytes 2752520 | tf_op jit(solution)/shard_map/ppermute | solution.py:229
  128.1 9.4 %all-to-all-done.4.got_ref = bf16[32,80,128]{2,1,0:T(8,128)(2,1)S(1)} async-done(((bf16[32,80,128]{2,1,0:T(8,128)(2,1)}), bf16[32,80,128]{2,1,0:T(8,128)(2,1)S(1)}, u32[]{:S(2)}, u32[]{:S(2)}) %all-to-all-start.4) | async-done | bytes 655392 | tf_op jit(solution)/shard_map/all_to_all | solution.py:232
  138.4 11.9 %all-to-all-start.5 = ((bf16[16,80,128]{2,1,0:T(8,128)(2,1)}), bf16[16,80,128]{2,1,0:T(8,128)(2,1)S(1)}, u32[]{:S(2)}, u32[]{:S(2)}) async-start(bf16[16,80,128]{2,1,0:T(8,128)(2,1)} %shard_map.128), calls=%async_computation.5 | async-start | bytes 655360 | tf_op jit(solution)/shard_map/all_to_all | solution.py:289
  152.4 3.0 %shard_map.125 = (bf16[448,1024]{1,0:T(8,128)(2,1)S(1)}, f32[128,1024]{1,0:T(8,128)S(1)}, bf16[64,1024]{1,0:T(8,128)(2,1)S(1)}, bf16[64,1024]{1,0:T(8,128)(2,1)S(1)}) custom-call(f32[448,1024]{1,0:T(8,128)S(1)} %get-tuple-element.21.ng_ref, bf16[448,1024]{1,0:T(8,128)(2,1)} %collective-permute-done.5.got_ref, bf16[448,1024]{1,0:T(8,128)(2,1)S(1)} %copy-done.4, ...), custom_call_target="tpu_custom_call" | custom-call | flops 528482304 | bytes 6496256 | tf_op jit(solution)/shard_map/pallas_call | solution.py:28
  155.4 1.9 %collective-permute-start.6 = (bf16[64,1024]{1,0:T(8,128)(2,1)S(1)}, bf16[64,1024]{1,0:T(8,128)(2,1)S(1)}, u32[]{:S(2)}, u32[]{:S(2)}) collective-permute-start(bf16[64,1024]{1,0:T(8,128)(2,1)S(1)} %get-tuple-element.26), channel_id=1, source_target_pairs={{0,1},{1,2},{2,3},{3,4},{4,5},{5,6},{6,7},{7,8},{8,9},{9,10},{10,1... | collective-permute-start | bytes 393224 | tf_op jit(solution)/shard_map/ppermute | solution.py:211
  157.3 2.4 %collective-permute-start.7 = (bf16[64,1024]{1,0:T(8,128)(2,1)S(1)}, bf16[64,1024]{1,0:T(8,128)(2,1)S(1)}, u32[]{:S(2)}, u32[]{:S(2)}) collective-permute-start(bf16[64,1024]{1,0:T(8,128)(2,1)S(1)} %get-tuple-element.27), channel_id=1, source_target_pairs={{1,0},{2,1},{3,2},{4,3},{5,4},{6,5},{7,6},{8,7},{9,8},{10,9},{11,1... | collective-permute-start | bytes 393224 | tf_op jit(solution)/shard_map/ppermute | solution.py:211
  159.8 5.0 %collective-permute-done.7.next_ref = bf16[64,1024]{1,0:T(8,128)(2,1)S(1)} collective-permute-done((bf16[64,1024]{1,0:T(8,128)(2,1)S(1)}, bf16[64,1024]{1,0:T(8,128)(2,1)S(1)}, u32[]{:S(2)}, u32[]{:S(2)}) %collective-permute-start.7) | collective-permute-done | bytes 131104 | tf_op jit(solution)/shard_map/ppermute | solution.py:211
  (62 shorter events, 17.5 us)
Async XLA Ops:
  1.3 9.6 %collective-permute-start = (bf16[16,128]{1,0:T(8,128)(2,1)S(1)}, bf16[16,128]{1,0:T(8,128)(2,1)S(1)}, u32[]{:S(2)}, u32[]{:S(2)}) collective-permute-start(bf16[16,128]{1,0:T(8,128)(2,1)S(1)} %constant_dynamic-slice_fusion), channel_id=1, source_target_pairs={{0,1},{1,0},{2,3},{3,2},{4,5},{5,4},{6,7},{7,6},{8,9},{9,8},{10,11... | collective-permute-start | bytes 12296 | tf_op jit(solution)/shard_map/ppermute | solution.py:229
  49.4 4.7 %copy-start.7 = (bf16[1,448,1024]{2,1,0:T(8,128)(2,1)S(1)}, bf16[1,448,1024]{2,1,0:T(8,128)(2,1)}, u32[]{:S(2)}) copy-start(bf16[1,448,1024]{2,1,0:T(8,128)(2,1)} %param.10) | copy-start | bytes 2752516
  49.4 12.7 %copy-start.8 = (s32[8,448]{1,0:T(8,128)S(1)}, s32[8,448]{1,0:T(8,128)}, u32[]{:S(2)}) copy-start(s32[8,448]{1,0:T(8,128)} %src_ref.1) | copy-start | bytes 43012
  49.4 12.7 %copy-start.9 = (f32[8,448]{1,0:T(8,128)S(1)}, f32[8,448]{1,0:T(8,128)}, u32[]{:S(2)}) copy-start(f32[8,448]{1,0:T(8,128)} %ew_ref.1) | copy-start | bytes 43012
  50.5 27.5 %all-to-all-start.1 = ((bf16[8,512,128]{2,1,0:T(8,128)(2,1)}), bf16[8,512,128]{2,1,0:T(8,128)(2,1)S(1)}, u32[]{:S(2)}, u32[]{:S(2)}) async-start(bf16[8,512,128]{2,1,0:T(8,128)(2,1)} %broadcast_in_dim.10), calls=%async_computation.1 | async-start | bytes 2097152 | tf_op jit(solution)/shard_map/all_to_all | solution.py:235
  54.1 17.8 %copy-start.12 = (bf16[1,100,448]{2,1,0:T(8,128)(2,1)S(1)}, bf16[1,100,448]{2,1,0:T(8,128)(2,1)}, u32[]{:S(2)}) copy-start(bf16[1,100,448]{2,1,0:T(8,128)(2,1)} %param.11) | copy-start | bytes 268804
  54.1 17.9 %copy-start.13 = (bf16[100,448]{1,0:T(8,128)(2,1)S(1)}, bf16[100,448]{1,0:T(8,128)(2,1)}, u32[]{:S(2)}) copy-start(bf16[100,448]{1,0:T(8,128)(2,1)} %param.12) | copy-start | bytes 268804
  54.1 9.0 %collective-permute-start.2 = (bf16[64,1024]{1,0:T(8,128)(2,1)S(1)}, bf16[64,1024]{1,0:T(8,128)(2,1)S(1)}, u32[]{:S(2)}, u32[]{:S(2)}) collective-permute-start(bf16[64,1024]{1,0:T(8,128)(2,1)S(1)} %get-tuple-element.43), channel_id=1, source_target_pairs={{1,0},{2,1},{3,2},{4,3},{5,4},{6,5},{7,6},{8,7},{9,8},{10,9},{11,1... | collective-permute-start | bytes 393224 | tf_op jit(solution)/shard_map/ppermute | solution.py:211
  59.6 5.8 %collective-permute-start.1 = (bf16[64,1024]{1,0:T(8,128)(2,1)S(1)}, bf16[64,1024]{1,0:T(8,128)(2,1)S(1)}, u32[]{:S(2)}, u32[]{:S(2)}) collective-permute-start(bf16[64,1024]{1,0:T(8,128)(2,1)S(1)} %get-tuple-element.44), channel_id=1, source_target_pairs={{0,1},{1,2},{2,3},{3,4},{4,5},{5,6},{6,7},{7,8},{8,9},{9,10},{10,1... | collective-permute-start | bytes 393224 | tf_op jit(solution)/shard_map/ppermute | solution.py:211
  63.1 9.2 %copy-start.14 = (f32[448]{0:T(512)S(1)}, f32[448]{0:T(512)}, u32[]{:S(2)}) copy-start(f32[448]{0:T(512)} %param.13) | copy-start | bytes 5380
  63.1 9.2 %copy-start.15 = (s32[448]{0:T(512)S(1)}, s32[448]{0:T(512)}, u32[]{:S(2)}) copy-start(s32[448]{0:T(512)} %param.15) | copy-start | bytes 5380
  69.8 4.4 %copy-start.16 = (f32[100]{0:T(128)S(1)}, f32[100]{0:T(128)}, u32[]{:S(2)}) copy-start(f32[100]{0:T(128)} %param.14) | copy-start | bytes 1204
  69.8 8.2 %collective-permute-start.3 = (bf16[448,1536]{1,0:T(8,128)(2,1)}, bf16[448,1536]{1,0:T(8,128)(2,1)}, u32[]{:S(2)}, u32[]{:S(2)}) collective-permute-start(bf16[448,1536]{1,0:T(8,128)(2,1)} %get-tuple-element.18), channel_id=1, source_target_pairs={{0,1},{1,0},{2,3},{3,2},{4,5},{5,4},{6,7},{7,6},{8,9},{9,8},{10,11... | collective-permute-start | bytes 4128776 | tf_op jit(solution)/shard_map/ppermute | solution.py:229
  74.4 3.6 %collective-permute-start.4 = (bf16[448,128]{1,0:T(8,128)(2,1)S(1)}, bf16[448,128]{1,0:T(8,128)(2,1)S(1)}, u32[]{:S(2)}, u32[]{:S(2)}) collective-permute-start(bf16[448,128]{1,0:T(8,128)(2,1)S(1)} %pad_bitcast_fusion.po_ref), channel_id=1, source_target_pairs={{0,1},{1,0},{2,3},{3,2},{4,5},{5,4},{6,7},{7,6},{8,9},{9,8},{10,11... | collective-permute-start | bytes 344072 | tf_op jit(solution)/shard_map/ppermute | solution.py:229
  78.1 6.3 %copy-start = (bf16[8,512,128]{2,1,0:T(8,128)(2,1)}, bf16[8,512,128]{2,1,0:T(8,128)(2,1)S(1)}, u32[]{:S(2)}) copy-start(bf16[8,512,128]{2,1,0:T(8,128)(2,1)S(1)} %all-to-all-done.1.wg_ref) | copy-start | bytes 3145732
  78.1 1.6 copy-start.3
  112.9 24.6 %all-to-all-start.4 = ((bf16[32,80,128]{2,1,0:T(8,128)(2,1)}), bf16[32,80,128]{2,1,0:T(8,128)(2,1)S(1)}, u32[]{:S(2)}, u32[]{:S(2)}) async-start(bf16[32,80,128]{2,1,0:T(8,128)(2,1)} %shard_map.127), calls=%async_computation.4 | async-start | bytes 1310720 | tf_op jit(solution)/shard_map/all_to_all | solution.py:232
  119.4 1.2 copy-start.1
  120.6 1.2 copy-start.11
  123.9 26.4 %collective-permute-start.5 = (bf16[448,1024]{1,0:T(8,128)(2,1)}, bf16[448,1024]{1,0:T(8,128)(2,1)}, u32[]{:S(2)}, u32[]{:S(2)}) collective-permute-start(bf16[448,1024]{1,0:T(8,128)(2,1)} %get-tuple-element.22), channel_id=1, source_target_pairs={{0,1},{1,0},{2,3},{3,2},{4,5},{5,4},{6,7},{7,6},{8,9},{9,8},{10,11... | collective-permute-start | bytes 2752520 | tf_op jit(solution)/shard_map/ppermute | solution.py:229
  138.4 27.4 %all-to-all-start.5 = ((bf16[16,80,128]{2,1,0:T(8,128)(2,1)}), bf16[16,80,128]{2,1,0:T(8,128)(2,1)S(1)}, u32[]{:S(2)}, u32[]{:S(2)}) async-start(bf16[16,80,128]{2,1,0:T(8,128)(2,1)} %shard_map.128), calls=%async_computation.5 | async-start | bytes 655360 | tf_op jit(solution)/shard_map/all_to_all | solution.py:289
  150.3 1.2 copy-start.4
  155.4 4.3 %collective-permute-start.6 = (bf16[64,1024]{1,0:T(8,128)(2,1)S(1)}, bf16[64,1024]{1,0:T(8,128)(2,1)S(1)}, u32[]{:S(2)}, u32[]{:S(2)}) collective-permute-start(bf16[64,1024]{1,0:T(8,128)(2,1)S(1)} %get-tuple-element.26), channel_id=1, source_target_pairs={{0,1},{1,2},{2,3},{3,4},{4,5},{5,6},{6,7},{7,8},{8,9},{9,10},{10,1... | collective-permute-start | bytes 393224 | tf_op jit(solution)/shard_map/ppermute | solution.py:211
  157.3 7.4 %collective-permute-start.7 = (bf16[64,1024]{1,0:T(8,128)(2,1)S(1)}, bf16[64,1024]{1,0:T(8,128)(2,1)S(1)}, u32[]{:S(2)}, u32[]{:S(2)}) collective-permute-start(bf16[64,1024]{1,0:T(8,128)(2,1)S(1)} %get-tuple-element.27), channel_id=1, source_target_pairs={{1,0},{2,1},{3,2},{4,3},{5,4},{6,5},{7,6},{8,7},{9,8},{10,9},{11,1... | collective-permute-start | bytes 393224 | tf_op jit(solution)/shard_map/ppermute | solution.py:211
  (4 other events, 3.5 us)

commit v2 on v0

v2 whole, which is shorter than its diff:
```python
import math

import jax
import jax.numpy as jnp
from jax import lax
from jax.experimental import pallas as pl
from jax.experimental.pallas import tpu as pltpu
from jax.sharding import PartitionSpec as P

K = 64
KNB = 8
LANES = 128
TILE = 16
MEMBERS = 8

norm_eps = 1e-05
alpha_fair = 0.95
root_half = 1.0 / math.sqrt(2.0)
inv_root_two_pi = 1.0 / math.sqrt(2.0 * math.pi)

f32 = jnp.float32
bf16 = jnp.bfloat16


def shape(dims, dtype):
    return jax.ShapeDtypeStruct(dims, dtype)


def dot(a, b, ca=1, cb=0):
    return lax.dot_general(a, b, (((ca,), (cb,)), ((), ())), preferred_element_type=f32)


class Copies:
    def __init__(self, sems):
        self.sems, self.used = sems, 0

    def start(self, src, dst):
        copy = pltpu.make_async_copy(src, dst, self.sems.at[self.used])
        self.used += 1
        copy.start()
        return copy


def after(x, *first):
    return lax.optimization_barrier((x,) + first)[0]


def sent(dims, dtype):
    return pltpu.HBM(dims, dtype)


def call(body, out, args, scratch=(), core=None, sems=0, hbm_args=(), flops=0, trans=0, mib=24):
    hbm_args = tuple(pltpu.with_memory_space_constraint(a, pltpu.HBM) for a in hbm_args)
    args = tuple(args) + hbm_args
    moved = sum(a.size * a.dtype.itemsize for a in args)
    moved += sum(math.prod(o.shape) * jnp.dtype(o.dtype).itemsize for o in out)
    first = [] if core is None else [core]

    def kernel(*refs):
        if sems:
            body(*refs[:-1], Copies(refs[-1]))
        else:
            body(*refs)

    vmem = pl.BlockSpec(memory_space=pltpu.VMEM)
    hbm = pl.BlockSpec(memory_space=pltpu.HBM)
    return pl.pallas_call(
        kernel,
        out_shape=out,
        in_specs=[pl.BlockSpec(memory_space=pltpu.SMEM)] * len(first) + [vmem] * (len(args) - len(hbm_args))
        + [hbm] * len(hbm_args),
        out_specs=[hbm if getattr(o, "memory_space", None) == pltpu.HBM else vmem for o in out],
        scratch_shapes=list(scratch) + ([pltpu.SemaphoreType.DMA((sems,))] if sems else []),
        cost_estimate=pl.CostEstimate(flops=flops, bytes_accessed=moved, transcendentals=trans),
        compiler_params=pltpu.CompilerParams(vmem_limit_bytes=mib * 2**20),
    )(*first, *args)


def widen_body(pred_ref, out_hbm, wide_ref, copies):
    variables, nodes = pred_ref.shape[1:]
    pad = jnp.zeros((wide_ref.shape[0] - variables, nodes), f32)
    wide_ref[...] = jnp.concatenate([pred_ref[0].astype(f32), pad], axis=0).astype(bf16)
    for c in [copies.start(wide_ref, out_hbm.at[m]) for m in range(MEMBERS)]:
        c.wait()


def tile_body(pick_ref, own_ref, got_ref, out_hbm, out_ref, copies):
    tile = jnp.where(pick_ref[0] == 1, own_ref[...].astype(f32), got_ref[...].astype(f32)).astype(bf16)
    out_ref[...] = jnp.broadcast_to(tile[None], out_ref.shape)
    copies.start(out_ref, out_hbm).wait()


def edges_body(src_ref, ew_ref, at_hbm, at_ref, copies):
    rows, nodes = at_ref.shape
    for r in range(0, rows, K):
        j = lax.broadcasted_iota(jnp.int32, (K, nodes), 0) + r
        acc = jnp.zeros((K, nodes), f32)
        for s in range(KNB):
            acc += jnp.where(src_ref[s : s + 1, :] == j, ew_ref[s : s + 1, :], 0.0)
        at_ref[r : r + K, :] = acc.astype(bf16)
    copies.start(at_ref, at_hbm).wait()


def norm_body(
    core_ref, own_ref, near_ref, far_ref, at_hbm, rstd_hbm, keep_hbm, send_hbm, at_ref, li_ref, normed_ref, rstd_ref, copies
):
    copies.start(at_hbm, at_ref).wait()
    core = core_ref[0]
    nodes, width = own_ref.shape
    half = width // 2
    near_at = pl.multiple_of((1 - core) * (K + nodes), K)
    far_at = pl.multiple_of(core * (K + nodes), K)
    agg = dot(at_ref[pl.ds(near_at, K), :], near_ref[...], 0, 0)
    agg += dot(at_ref[K : K + nodes, :], own_ref[...], 0, 0)
    agg += dot(at_ref[pl.ds(far_at, K), :], far_ref[...], 0, 0)
    li = own_ref[...].astype(f32) + agg
    li_ref[...] = li.astype(bf16)
    mine = pl.multiple_of(core * half, half)
    theirs = pl.multiple_of((1 - core) * half, half)
    stores = [
        copies.start(li_ref.at[:, pl.ds(theirs, half)], send_hbm.at[:, pl.ds(width, half)]),
        copies.start(li_ref.at[:, pl.ds(mine, half)], keep_hbm),
    ]
    mean = jnp.mean(li, axis=-1, keepdims=True)
    dev = li - mean
    rstd = lax.rsqrt(jnp.mean(dev * dev, axis=-1, keepdims=True) + norm_eps)
    normed_ref[...] = (dev * rstd).astype(bf16)
    stores.append(copies.start(normed_ref, send_hbm.at[:, pl.ds(0, width)]))
    rstd_ref[...] = jnp.broadcast_to(rstd, rstd_ref.shape)
    stores.append(copies.start(rstd_ref, rstd_hbm))
    for c in stores:
        c.wait()


def pred_body(all_ref, own_ref, target_ref, lw_ref, out_ref):
    members = all_ref.shape[0]
    variables = out_ref.shape[0]
    coef_pair = (1.0 - (1.0 - alpha_fair) / members) / (members * (members - 1))

    def sign(a):
        return jnp.where(a > 0.0, 1.0, jnp.where(a < 0.0, -1.0, 0.0))

    own = own_ref[0].astype(f32)
    pair_sum = jnp.zeros(own.shape, f32)
    for k in range(members):
        pair_sum += sign(own - all_ref[k].astype(f32)[0:variables])
    to_target = sign(own - target_ref[...].astype(f32))
    out_ref[...] = (lw_ref[...] * (to_target / members - coef_pair * pair_sum)).astype(bf16)


def share_body(got_ref, out_hbm, copies):
    for c in [copies.start(got_ref, out_hbm.at[m]) for m in range(out_hbm.shape[0])]:
        c.wait()


def fill_weight(wg_ref, w_ref):
    cols = w_ref.shape[1] // LANES
    for g in range(wg_ref.shape[1]):
        for c in range(2):
            for x in range(cols):
                at = (2 * g + c) * TILE
                w_ref[at : at + TILE, x * LANES : (x + 1) * LANES] = wg_ref[c * cols + x, g]


def main_body(
    core_ref, wg_ref, own_hbm, keep_hbm, po_hbm, wd_hbm, got_hbm, pp_hbm, send_hbm, pre_hbm, ng_hbm,
    no_ref, keep_ref, po_ref, wd_ref, got_ref, pp_ref, w_ref, lo_ref, pre_ref, parts_ref, ng_ref, copies,
):
    core = core_ref[0]
    nodes, width = no_ref.shape
    half = width // 2
    cols = half // LANES
    pairs = parts_ref.shape[1] - cols
    loads = [
        [copies.start(own_hbm.at[:, pl.ds(0, width)], no_ref), copies.start(keep_hbm, keep_ref),
         copies.start(po_hbm, po_ref), copies.start(wd_hbm, wd_ref)],
        [copies.start(got_hbm, got_ref), copies.start(pp_hbm, pp_ref)],
    ]
    fill_weight(wg_ref, w_ref)
    stores = []
    for part in range(2):
        p_ref = (po_ref, pp_ref)[part]
        for c in loads[part]:
            c.wait()
        wd = wd_ref[:, pl.ds(pl.multiple_of(core * half, half), half)]
        for r in range(0, nodes, 128):
            step = min(128, nodes - r)
            n = no_ref[r : r + step, :] if part == 0 else got_ref[r : r + step, 0:width]
            li = keep_ref[r : r + step, :] if part == 0 else got_ref[r : r + step, width:]
            pre = dot(n, w_ref[...])
            og = dot(p_ref[:, r : r + step], wd, 0, 0)
            cdf = 0.5 * (1.0 + lax.erf(pre * root_half))
            pdf = jnp.exp(-0.5 * pre * pre) * inv_root_two_pi
            at = part * nodes + r
            lo_ref[at : at + step, :] = (li.astype(f32) + pre * cdf).astype(bf16)
            pre_ref[at : at + step, :] = (og * (cdf + pre * pdf)).astype(bf16)
    stores.append(copies.start(pre_ref.at[pl.ds(0, nodes)], pre_hbm))
    ng_ref[...] = dot(pre_ref[nodes:, :], w_ref[...], 1, 1).astype(bf16)
    stores.append(copies.start(ng_ref, ng_hbm))
    dec = dot(po_ref[...], lo_ref[0:nodes, :]) + dot(pp_ref[...], lo_ref[nodes:, :])
    dec = jnp.concatenate([dec, jnp.zeros((MEMBERS * TILE - dec.shape[0], half), f32)], axis=0).astype(bf16)
    for m in range(MEMBERS):
        for x in range(cols):
            parts_ref[m, pairs + x] = dec[m * TILE : (m + 1) * TILE, x * LANES : (x + 1) * LANES]
    rows = 256
    for q in range(0, width, rows):
        res = dot(no_ref[:, q : q + rows], pre_ref[0:nodes, :], 0, 0)
        res += dot(got_ref[:, q : q + rows], pre_ref[nodes:, :], 0, 0)
        res = res.astype(bf16)
        first, count = q // (2 * TILE), rows // (2 * TILE)
        for g in range(count):
            for c in range(2):
                for x in range(cols):
                    at = (2 * g + c) * TILE
                    parts_ref[c * cols + x, first + g] = res[at : at + TILE, x * LANES : (x + 1) * LANES]
        last = q + rows == width
        tiles = pl.ds(first, count + (cols if last else 0))
        stores.append(copies.start(parts_ref.at[:, tiles], send_hbm.at[:, tiles]))
    for c in stores:
        c.wait()


def scatter_body(
    core_ref, wg_ref, got_ref, rstd_hbm, po_hbm, wd_hbm, pre_hbm, own_hbm, at_hbm, mid_hbm, edge_hbm, near_ref, far_ref,
    w_ref, rstd_ref, po_ref, wd_ref, pre_ref, no_ref, at_ref, ib_ref, mid_ref, edge_ref, copies,
):
    core = core_ref[0]
    nodes, width = no_ref.shape
    first = copies.start(pre_hbm, pre_ref)
    loads = [
        copies.start(po_hbm, po_ref),
        copies.start(wd_hbm, wd_ref),
        copies.start(own_hbm.at[:, pl.ds(0, width)], no_ref),
        copies.start(rstd_hbm, rstd_ref),
        copies.start(at_hbm, at_ref),
    ]
    fill_weight(wg_ref, w_ref)
    first.wait()
    ng = dot(pre_ref[...], w_ref[...], 1, 1) + got_ref[...].astype(f32)
    for c in loads:
        c.wait()
    unit = no_ref[...].astype(f32)
    og = dot(po_ref[...], wd_ref[...], 0, 0)
    mean_g = jnp.mean(ng, axis=-1, keepdims=True)
    mean_c = jnp.mean(ng * unit, axis=-1, keepdims=True)
    ig = og + rstd_ref[:, 0:1] * (ng - mean_g - unit * mean_c)
    ib_ref[...] = ig.astype(bf16)
    near_at = pl.multiple_of((1 - core) * (K + nodes), K)
    far_at = pl.multiple_of(core * (K + nodes), K)
    near_ref[...] = dot(at_ref[pl.ds(near_at, K), :], ib_ref[...]).astype(bf16)
    far_ref[...] = dot(at_ref[pl.ds(far_at, K), :], ib_ref[...]).astype(bf16)
    total = ig + dot(at_ref[K : K + nodes, :], ib_ref[...])
    mid_ref[...] = total.astype(bf16)
    edge_ref[0:K, :] = total[0:K, :]
    edge_ref[K:, :] = total[nodes - K :, :]
    for c in [copies.start(mid_ref, mid_hbm), copies.start(edge_ref, edge_hbm)]:
        c.wait()


def join_body(core_ref, near_ref, far_ref, mid_hbm, edge_hbm, out_hbm, mid_ref, edge_ref, copies):
    core = core_ref[0]
    nodes = mid_ref.shape[0]
    loads = [copies.start(mid_hbm, mid_ref), copies.start(edge_hbm, edge_ref)]
    for c in loads:
        c.wait()
    for ref, end in ((near_ref, 1 - core), (far_ref, core)):
        edge = edge_ref[pl.ds(pl.multiple_of(end * K, K), K), :] + ref[...].astype(f32)
        mid_ref[pl.ds(pl.multiple_of(end * (nodes - K), K), K), :] = edge.astype(bf16)
    copies.start(mid_ref, out_hbm.at[0]).wait()


def sum_mem_body(got_ref, out_hbm, out_ref, copies):
    pairs, tiles = out_ref.shape[:2]
    total = got_ref[0].astype(f32)
    for m in range(1, MEMBERS):
        total += got_ref[m].astype(f32)
    total = total.astype(bf16)
    out_ref[:, 0] = total[0:pairs]
    out_ref[:, 1:] = jnp.broadcast_to(total[pairs:][None], (pairs, tiles - 1, TILE, LANES))
    copies.start(out_ref, out_hbm).wait()


def sum_grid_body(got_ref, out_hbm, out_ref, copies):
    total = got_ref[0].astype(f32)
    for g in range(1, got_ref.shape[0]):
        total += got_ref[g].astype(f32)
    out_ref[...] = total.astype(bf16)
    for c in [copies.start(out_ref, out_hbm.at[m]) for m in range(out_hbm.shape[0])]:
        c.wait()


def final_body(core_ref, got_ref, weight_ref, dec_ref):
    core = core_ref[0]
    half = weight_ref.shape[1] // 2
    cols = half // LANES
    variables = dec_ref.shape[0]
    for c in range(2):
        for x in range(cols):
            lane = c * half + x * LANES
            weight_ref[:, lane : lane + LANES] = got_ref[(core * cols + x) * 2 + c, 0].astype(f32)
            for m in range(MEMBERS):
                rows = min(TILE, variables - m * TILE)
                if rows > 0:
                    tile = got_ref[m * 2 + c, 1 + x].astype(f32)
                    dec_ref[m * TILE : m * TILE + rows, lane : lane + LANES] = tile[0:rows, :]


def other_pair(a):
    size = lax.axis_size(("pair", "core"))
    pairs = [(i, i + (1 if i % 2 else -1)) for i in range(1, size - 1)]
    return lax.ppermute(a, ("pair", "core"), pairs)


def other_core(a):
    return lax.ppermute(a, "core", [(0, 1), (1, 0)])


def over_pairs(a):
    return lax.all_to_all(a, "pair", 0, 0, tiled=True)


def over_mem(a):
    return lax.all_to_all(a, "mem", 0, 0, tiled=True)


def on_device(
    hidden, predictions, target, area, var_weight, interior, sources, edge_weight, w_node, w_dec
):
    pairs = lax.axis_size("pair")
    nodes, width = hidden.shape[1:]
    half = width // 2
    cols = half // LANES
    variables = w_dec.shape[1]
    rows = -(-variables // TILE) * TILE
    core = lax.axis_index("core")
    member = lax.axis_index("mem")
    core_arg = core.astype(jnp.int32).reshape(1)
    own = hidden[0]
    vmem = pltpu.VMEM

    row_half, col_block = member // cols, member % cols
    tile_own = lax.dynamic_slice(w_node, (0, core * half + col_block * LANES), (TILE, LANES))
    tile_out = lax.dynamic_slice(w_node, (0, (1 - core) * half + col_block * LANES), (TILE, LANES))
    tile_got = other_core(tile_out)
    own_half = (core == row_half).astype(jnp.int32).reshape(1)
    (tiles,) = call(
        tile_body,
        [sent((pairs, TILE, LANES), bf16)],
        (tile_own, tile_got),
        [vmem((pairs, TILE, LANES), bf16)],
        core=own_half,
        sems=1,
    )

    (spread_pred,) = call(
        widen_body,
        [sent((MEMBERS, rows, nodes), bf16)],
        (predictions,),
        [vmem((rows, nodes), bf16)],
        sems=MEMBERS,
    )
    every_pred = over_mem(spread_pred)
    near = other_core(lax.dynamic_slice(own, ((1 - core) * (nodes - K), 0), (K, width)))
    far = other_pair(lax.dynamic_slice(own, (core * (nodes - K), 0), (K, width)))
    (at,) = call(
        edges_body, [sent((nodes + 2 * K, nodes), bf16)], (sources, edge_weight),
        [vmem((nodes + 2 * K, nodes), bf16)], sems=1,
    )
    shards = over_pairs(after(tiles, every_pred, far))
    rstd, keep, send = call(
        norm_body,
        [sent((nodes, LANES), f32), sent((nodes, half), bf16), sent((nodes, width + half), bf16)],
        (after(own, shards), near, far),
        [vmem((nodes + 2 * K, nodes), bf16), vmem((nodes, width), bf16), vmem((nodes, width), bf16),
         vmem((nodes, LANES), f32)],
        core=core_arg,
        hbm_args=(at,),
        sems=5,
        flops=2 * nodes * (nodes + 2 * K) * width,
    )
    got = other_core(send)
    loss_weight = var_weight[:, None] * (area * interior.astype(f32))[None, :]
    (pred_grad,) = call(
        pred_body,
        [shape((variables, nodes), bf16)],
        (every_pred, predictions, target, loss_weight),
    )
    pred_got = other_core(pred_grad)
    dec_t = w_dec.T

    (spread,) = call(
        share_body,
        [sent((MEMBERS, pairs, TILE, LANES), bf16)],
        (after(shards, pred_got, near, at),),
        sems=MEMBERS,
    )
    weight = over_mem(spread)

    weight_shape = vmem((width, half), bf16)
    part_shape = (MEMBERS, pairs + cols, TILE, LANES)
    parts, pre_grad, ng_send = call(
        main_body,
        [sent(part_shape, bf16), sent((nodes, half), bf16), sent((nodes, width), bf16)],
        (weight,),
        [vmem((nodes, width), bf16), vmem((nodes, half), bf16), vmem((variables, nodes), bf16),
         vmem((variables, width), bf16), vmem((nodes, width + half), bf16), vmem((variables, nodes), bf16), weight_shape, vmem((2 * nodes, half), bf16),
         vmem((2 * nodes, half), bf16), vmem(part_shape, bf16), vmem((nodes, width), bf16)],
        core=core_arg,
        hbm_args=(send, keep, pred_grad, dec_t, got, pred_got),
        sems=16,
        flops=5 * 2 * nodes * width * half,
        trans=4 * nodes * half,
    )
    mem_parts = over_mem(parts)

    ng_got = other_core(ng_send)
    mid, edge, to_near, to_far = call(
        scatter_body,
        [sent((nodes, width), bf16), sent((2 * K, width), f32), shape((K, width), bf16), shape((K, width), bf16)],
        (weight, ng_got),
        [weight_shape, vmem((nodes, LANES), f32), vmem((variables, nodes), bf16), vmem((variables, width), bf16),
         vmem((nodes, half), bf16), vmem((nodes, width), bf16), vmem((nodes + 2 * K, nodes), bf16),
         vmem((nodes, width), bf16), vmem((nodes, width), bf16), vmem((2 * K, width), f32)],
        core=core_arg,
        hbm_args=(rstd, pred_grad, dec_t, pre_grad, send, at),
        sems=8,
        flops=2 * nodes * (nodes + 2 * K) * width,
    )
    from_near = other_core(to_near)
    from_far = other_pair(to_far)
    (grid_out,) = call(
        sum_mem_body,
        [sent((pairs, 1 + cols, TILE, LANES), bf16)],
        (after(mem_parts, to_near),),
        [vmem((pairs, 1 + cols, TILE, LANES), bf16)],
        sems=1,
    )
    grid_parts = over_pairs(grid_out)
    (hidden_grad,) = call(
        join_body,
        [sent((1, nodes, width), bf16)],
        (from_near, from_far),
        [vmem((nodes, width), bf16), vmem((2 * K, width), f32)],
        core=core_arg,
        hbm_args=(mid, edge),
        sems=3,
    )
    (last_out,) = call(
        sum_grid_body,
        [sent((2 * MEMBERS, 1 + cols, TILE, LANES), bf16)],
        (after(grid_parts, from_near, from_far),),
        [vmem((1 + cols, TILE, LANES), bf16)],
        sems=2 * MEMBERS,
    )
    last = lax.all_to_all(last_out, ("mem", "core"), 0, 0, tiled=True)
    weight_grad, decoder_grad = call(
        final_body,
        [shape((TILE, width), f32), shape((variables, width), f32)],
        (last,),
        core=core_arg,
    )
    return (hidden_grad, weight_grad, decoder_grad.T)


def solution(mesh):
    members, blocks = mesh.shape["mem"], mesh.shape["grid"]
    split = jax.sharding.Mesh(
        mesh.devices.reshape(members, blocks // 2, 2), ("mem", "pair", "core")
    )
    grid = ("pair", "core")
    placed = (
        P("mem", grid, None),
        P("mem", None, grid),
        P(None, grid),
        P(grid),
        P(),
        P(grid),
        P(None, grid),
        P(None, grid),
        P(grid, None),
        P(),
    )
    return jax.shard_map(
        on_device,
        mesh=split,
        in_specs=placed,
        out_specs=(P("mem", grid, None), P(grid, None), P()),
        check_vma=False,
    )
```

time: 634 us -> 145 us (0.23)
  the two profiles are of different devices: /device:TPU:16 before, /device:TPU:1 now
where the time goes in v2:
time: 145 us; the launch traced here: 144 us
  starting transfers between devices  77.6 us (54%)
  waiting for transfers between devices  38.4 us (26%)
  Pallas kernels  24.3 us (17%)
  local copies, waits for them, and re-layouts  2.79 us (2%)
    pallas_call x12, Pallas kernels, call(): pl.pallas_call(kernel, out_shape=out, in_specs=[pl.BlockSpec(memory_space...  24.3 us
    ppermute x6, starting transfers between devices, other_core(): return lax.ppermute(a, 'core', [(0, 1), (1, 0)])  22.9 us
    all_to_all x2, starting transfers between devices, over_pairs(): return lax.all_to_all(a, 'pair', 0, 0, tiled=True)  18.7 us
    all_to_all x3, starting transfers between devices, over_mem(): return lax.all_to_all(a, 'mem', 0, 0, tiled=True)  18.3 us
    ppermute x2, waiting for transfers between devices, other_pair(): return lax.ppermute(a, ('pair', 'core'), pairs)  17.4 us
    all_to_all x1, starting transfers between devices, on_device(): last = lax.all_to_all(last_out, ('mem', 'core'), 0, 0, tiled=True)  10.5 us
    ppermute x2, starting transfers between devices, other_pair(): return lax.ppermute(a, ('pair', 'core'), pairs)  7.22 us
    all_to_all x3, waiting for transfers between devices, over_mem(): return lax.all_to_all(a, 'mem', 0, 0, tiled=True)  6.47 us
  transfers between devices with their start and end apart: 14, of which 7 were waited for; matrix products, arithmetic and copies ran while one was open for 1% of the time, Pallas kernels for 9%

profile of v2, /device:TPU:1, one launch (start us, length us, event | category | flops | bytes accessed | tf_op | source)
XLA Modules:
  0.0 144.2 jit_solution(6614707815188050461)
XLA Ops:
  2.6 6.0 %all-to-all-start = ((bf16[8,112,448]{2,1,0:T(8,128)(2,1)}), bf16[8,112,448]{2,1,0:T(8,128)(2,1)S(1)}, u32[]{:S(2)}, u32[]{:S(2)}) async-start(bf16[8,112,448]{2,1,0:T(8,128)(2,1)} %shard_map.122), calls=%async_computation | async-start | bytes 1835008 | tf_op jit(solution)/shard_map/all_to_all | solution.py:323
  9.3 6.5 %collective-permute-start = (bf16[16,128]{1,0:T(8,128)(2,1)S(1)}, bf16[16,128]{1,0:T(8,128)(2,1)S(1)}, u32[]{:S(2)}, u32[]{:S(2)}) collective-permute-start(bf16[16,128]{1,0:T(8,128)(2,1)S(1)} %get-tuple-element.39), channel_id=1, source_target_pairs={{0,1},{1,0},{2,3},{3,2},{4,5},{5,4},{6,7},{7,6},{8,9},{9,8},{10,11... | collective-permute-start | bytes 12296 | tf_op jit(solution)/shard_map/ppermute | solution.py:315
  15.9 1.9 %collective-permute-start.3 = (bf16[64,1024]{1,0:T(8,128)(2,1)S(1)}, bf16[64,1024]{1,0:T(8,128)(2,1)S(1)}, u32[]{:S(2)}, u32[]{:S(2)}) collective-permute-start(bf16[64,1024]{1,0:T(8,128)(2,1)S(1)} %get-tuple-element.37), channel_id=1, source_target_pairs={{0,1},{1,0},{2,3},{3,2},{4,5},{5,4},{6,7},{7,6},{8,9},{9,8},{10,11... | collective-permute-start | bytes 393224 | tf_op jit(solution)/shard_map/ppermute | solution.py:315
  17.8 1.9 %collective-permute-start.1 = (bf16[64,1024]{1,0:T(8,128)(2,1)S(1)}, bf16[64,1024]{1,0:T(8,128)(2,1)S(1)}, u32[]{:S(2)}, u32[]{:S(2)}) collective-permute-start(bf16[64,1024]{1,0:T(8,128)(2,1)S(1)} %get-tuple-element.38), channel_id=1, source_target_pairs={{1,2},{2,1},{3,4},{4,3},{5,6},{6,5},{7,8},{8,7},{9,10},{10,9},{11,... | collective-permute-start | bytes 393224 | tf_op jit(solution)/shard_map/ppermute | solution.py:311
  20.5 4.5 %collective-permute-done.1.refs_3_ = bf16[64,1024]{1,0:T(8,128)(2,1)S(1)} collective-permute-done((bf16[64,1024]{1,0:T(8,128)(2,1)S(1)}, bf16[64,1024]{1,0:T(8,128)(2,1)S(1)}, u32[]{:S(2)}, u32[]{:S(2)}) %collective-permute-start.1) | collective-permute-done | bytes 131104 | tf_op jit(solution)/shard_map/ppermute | solution.py:311
  25.0 11.8 %all-to-all-start.1 = ((bf16[32,16,128]{2,1,0:T(8,128)(2,1)}), bf16[32,16,128]{2,1,0:T(8,128)(2,1)S(1)}, u32[]{:S(2)}, u32[]{:S(2)}) async-start(bf16[32,16,128]{2,1,0:T(8,128)(2,1)} %shard_map.121), calls=%async_computation.1 | async-start | bytes 262144 | tf_op jit(solution)/shard_map/all_to_all | solution.py:319
  37.4 4.7 %collective-permute-start.2 = (bf16[100,448]{1,0:T(8,128)(2,1)S(1)}, bf16[100,448]{1,0:T(8,128)(2,1)S(1)}, u32[]{:S(2)}, u32[]{:S(2)}) collective-permute-start(bf16[100,448]{1,0:T(8,128)(2,1)S(1)} %shard_map.123.refs_4_), channel_id=1, source_target_pairs={{0,1},{1,0},{2,3},{3,2},{4,5},{5,4},{6,7},{7,6},{8,9},{9,8},{10,11... | collective-permute-start | bytes 268808 | tf_op jit(solution)/shard_map/ppermute | solution.py:315
  44.0 4.1 %all-to-all-done.1.refs_0_ = bf16[32,16,128]{2,1,0:T(8,128)(2,1)S(1)} async-done(((bf16[32,16,128]{2,1,0:T(8,128)(2,1)}), bf16[32,16,128]{2,1,0:T(8,128)(2,1)S(1)}, u32[]{:S(2)}, u32[]{:S(2)}) %all-to-all-start.1) | async-done | bytes 131104 | tf_op jit(solution)/shard_map/all_to_all | solution.py:319
  49.2 6.4 %all-to-all-start.2 = ((bf16[8,32,16,128]{3,2,1,0:T(8,128)(2,1)}), bf16[8,32,16,128]{3,2,1,0:T(8,128)(2,1)S(1)}, u32[]{:S(2)}, u32[]{:S(2)}) async-start(bf16[8,32,16,128]{3,2,1,0:T(8,128)(2,1)} %shard_map.125), calls=%async_computation.2 | async-start | bytes 2097152 | tf_op jit(solution)/shard_map/all_to_all | solution.py:323
  55.6 3.6 %shard_map.126 = (f32[448,128]{1,0:T(8,128)}, bf16[448,512]{1,0:T(8,128)(2,1)}, bf16[448,1536]{1,0:T(8,128)(2,1)}) custom-call(s32[1]{0:T(128)} %bitcast.refs_0_, bf16[448,1024]{1,0:T(8,128)(2,1)S(1)} %bitcast.9, bf16[64,1024]{1,0:T(8,128)(2,1)S(1)} %collective-permute-done.3.refs_2_, bf16[64,1024]{1,0:T(8,128)(2,1)S(1)} %collective-permute-done.1.refs_3_, ...), custom_call_target="tpu_custom_call" | custom-call | flops 528482304 | bytes 3760128 | tf_op jit(solution)/shard_map/pallas_call | solution.py:67
  59.2 4.7 %collective-permute-start.4 = (bf16[448,1536]{1,0:T(8,128)(2,1)}, bf16[448,1536]{1,0:T(8,128)(2,1)S(1)}, u32[]{:S(2)}, u32[]{:S(2)}) collective-permute-start(bf16[448,1536]{1,0:T(8,128)(2,1)} %get-tuple-element.23.refs_2_.refs_7_), channel_id=1, source_target_pairs={{0,1},{1,0},{2,3},{3,2},{4,5},{5,4},{6,7},{7,6},{8,9},{9,8},{10,11... | collective-permute-start | bytes 4128776 | tf_op jit(solution)/shard_map/ppermute | solution.py:315
  63.9 2.9 %collective-permute-done.4.refs_6_ = bf16[448,1536]{1,0:T(8,128)(2,1)S(1)} collective-permute-done((bf16[448,1536]{1,0:T(8,128)(2,1)}, bf16[448,1536]{1,0:T(8,128)(2,1)S(1)}, u32[]{:S(2)}, u32[]{:S(2)}) %collective-permute-start.4) | collective-permute-done | bytes 1376288 | tf_op jit(solution)/shard_map/ppermute | solution.py:315
  68.0 6.0 %shard_map.127 = (bf16[8,36,16,128]{3,2,1,0:T(8,128)(2,1)}, bf16[448,512]{1,0:T(8,128)(2,1)}, bf16[448,1024]{1,0:T(8,128)(2,1)}) custom-call(s32[1]{0:T(128)} %bitcast.refs_0_, bf16[8,32,16,128]{3,2,1,0:T(8,128)(2,1)S(1)} %all-to-all-done.2.refs_1_, bf16[448,1536]{1,0:T(8,128)(2,1)} %get-tuple-element.23.refs_2_.refs_7_, ...), custom_call_target="tpu_custom_call" | custom-call | flops 2348810240 | bytes 7199744 | tf_op jit(solution)/shard_map/pallas_call | solution.py:67
  74.0 5.9 %all-to-all-start.3 = ((bf16[8,36,16,128]{3,2,1,0:T(8,128)(2,1)}), bf16[8,36,16,128]{3,2,1,0:T(8,128)(2,1)S(1)}, u32[]{:S(2)}, u32[]{:S(2)}) async-start(bf16[8,36,16,128]{3,2,1,0:T(8,128)(2,1)} %get-tuple-element.32), calls=%async_computation.3 | async-start | bytes 2359296 | tf_op jit(solution)/shard_map/all_to_all | solution.py:323
  79.9 3.1 %collective-permute-start.5 = (bf16[448,1024]{1,0:T(8,128)(2,1)S(1)}, bf16[448,1024]{1,0:T(8,128)(2,1)S(1)}, u32[]{:S(2)}, u32[]{:S(2)}) collective-permute-start(bf16[448,1024]{1,0:T(8,128)(2,1)S(1)} %copy-done.11), channel_id=1, source_target_pairs={{0,1},{1,0},{2,3},{3,2},{4,5},{5,4},{6,7},{7,6},{8,9},{9,8},{10,11... | collective-permute-start | bytes 2752520 | tf_op jit(solution)/shard_map/ppermute | solution.py:315
  83.1 2.1 %collective-permute-done.5.refs_2_ = bf16[448,1024]{1,0:T(8,128)(2,1)S(1)} collective-permute-done((bf16[448,1024]{1,0:T(8,128)(2,1)S(1)}, bf16[448,1024]{1,0:T(8,128)(2,1)S(1)}, u32[]{:S(2)}, u32[]{:S(2)}) %collective-permute-start.5) | collective-permute-done | bytes 917536 | tf_op jit(solution)/shard_map/ppermute | solution.py:315
  85.1 4.6 %shard_map.128 = (bf16[448,1024]{1,0:T(8,128)(2,1)}, f32[128,1024]{1,0:T(8,128)}, bf16[64,1024]{1,0:T(8,128)(2,1)S(1)}, bf16[64,1024]{1,0:T(8,128)(2,1)S(1)}) custom-call(s32[1]{0:T(128)} %bitcast.refs_0_, bf16[8,32,16,128]{3,2,1,0:T(8,128)(2,1)S(1)} %all-to-all-done.2.refs_1_, bf16[448,1024]{1,0:T(8,128)(2,1)S(1)} %collective-permute-done.5.refs_2_, ...), custom_call_target="tpu_custom_call" | custom-call | flops 528482304 | bytes 6544896 | tf_op jit(solution)/shard_map/pallas_call | solution.py:67
  89.8 6.5 %all-to-all-done.3.refs_0_ = bf16[8,36,16,128]{3,2,1,0:T(8,128)(2,1)S(1)} async-done(((bf16[8,36,16,128]{3,2,1,0:T(8,128)(2,1)}), bf16[8,36,16,128]{3,2,1,0:T(8,128)(2,1)S(1)}, u32[]{:S(2)}, u32[]{:S(2)}) %all-to-all-start.3) | async-done | bytes 1179680 | tf_op jit(solution)/shard_map/all_to_all | solution.py:323
  97.2 6.9 %all-to-all-start.4 = ((bf16[32,5,16,128]{3,2,1,0:T(8,128)(2,1)}), bf16[32,5,16,128]{3,2,1,0:T(8,128)(2,1)S(1)}, u32[]{:S(2)}, u32[]{:S(2)}) async-start(bf16[32,5,16,128]{3,2,1,0:T(8,128)(2,1)} %shard_map.130), calls=%async_computation.4 | async-start | bytes 1310720 | tf_op jit(solution)/shard_map/all_to_all | solution.py:319
  104.2 5.3 %collective-permute-start.7 = (bf16[64,1024]{1,0:T(8,128)(2,1)S(1)}, bf16[64,1024]{1,0:T(8,128)(2,1)S(1)}, u32[]{:S(2)}, u32[]{:S(2)}) collective-permute-start(bf16[64,1024]{1,0:T(8,128)(2,1)S(1)} %get-tuple-element.29), channel_id=1, source_target_pairs={{1,2},{2,1},{3,4},{4,3},{5,6},{6,5},{7,8},{8,7},{9,10},{10,9},{11,... | collective-permute-start | bytes 393224 | tf_op jit(solution)/shard_map/ppermute | solution.py:311
  111.4 12.9 %collective-permute-done.7.refs_2_ = bf16[64,1024]{1,0:T(8,128)(2,1)S(1)} collective-permute-done((bf16[64,1024]{1,0:T(8,128)(2,1)S(1)}, bf16[64,1024]{1,0:T(8,128)(2,1)S(1)}, u32[]{:S(2)}, u32[]{:S(2)}) %collective-permute-start.7) | collective-permute-done | bytes 131104 | tf_op jit(solution)/shard_map/ppermute | solution.py:311
  125.2 10.5 %all-to-all-start.5 = ((bf16[16,5,16,128]{3,2,1,0:T(8,128)(2,1)}), bf16[16,5,16,128]{3,2,1,0:T(8,128)(2,1)S(1)}, u32[]{:S(2)}, u32[]{:S(2)}) async-start(bf16[16,5,16,128]{3,2,1,0:T(8,128)(2,1)} %shard_map.131), calls=%async_computation.5 | async-start | bytes 655360 | tf_op jit(solution)/shard_map/all_to_all | solution.py:455
  135.7 2.3 %shard_map.129 = bf16[1,448,1024]{2,1,0:T(8,128)(2,1)} custom-call(s32[1]{0:T(128)} %bitcast.refs_0_, bf16[64,1024]{1,0:T(8,128)(2,1)S(1)} %collective-permute-done.6.refs_1_, bf16[64,1024]{1,0:T(8,128)(2,1)S(1)} %collective-permute-done.7.refs_2_, bf16[448,1024]{1,0:T(8,128)(2,1)} %get-tuple-element.30.refs_3_, f32[128,1024]{1,0:T(8,128)} %get-tuple-element.31.refs_4_), custom_call_target="tpu_custom_call" | custom-call | bytes 2621440 | tf_op jit(solution)/shard_map/pallas_call | solution.py:67
  138.0 5.4 %all-to-all-done.5.refs_1_ = bf16[16,5,16,128]{3,2,1,0:T(8,128)(2,1)S(1)} async-done(((bf16[16,5,16,128]{3,2,1,0:T(8,128)(2,1)}), bf16[16,5,16,128]{3,2,1,0:T(8,128)(2,1)S(1)}, u32[]{:S(2)}, u32[]{:S(2)}) %all-to-all-start.5) | async-done | bytes 327712 | tf_op jit(solution)/shard_map/all_to_all | solution.py:455
  (46 shorter events, 12.6 us)
Async XLA Ops:
  1.5 14.3 %copy-start.4 = (bf16[1,448,1024]{2,1,0:T(8,128)(2,1)S(1)}, bf16[1,448,1024]{2,1,0:T(8,128)(2,1)}, u32[]{:S(2)}) copy-start(bf16[1,448,1024]{2,1,0:T(8,128)(2,1)} %param.10) | copy-start | bytes 2752516
  2.5 17.2 %copy-start.7 = (f32[448]{0:T(512)S(1)}, f32[448]{0:T(512)}, u32[]{:S(2)}) copy-start(f32[448]{0:T(512)} %param.13) | copy-start | bytes 5380
  2.5 17.2 %copy-start.8 = (s32[448]{0:T(512)S(1)}, s32[448]{0:T(512)}, u32[]{:S(2)}) copy-start(s32[448]{0:T(512)} %param.15) | copy-start | bytes 5380
  2.5 34.3 %copy-start.9 = (f32[100]{0:T(128)S(1)}, f32[100]{0:T(128)}, u32[]{:S(2)}) copy-start(f32[100]{0:T(128)} %param.14) | copy-start | bytes 1204
  2.6 34.3 %copy-start.1 = (bf16[1,100,448]{2,1,0:T(8,128)(2,1)S(1)}, bf16[1,100,448]{2,1,0:T(8,128)(2,1)}, u32[]{:S(2)}) copy-start(bf16[1,100,448]{2,1,0:T(8,128)(2,1)} %refs_1_.2) | copy-start | bytes 268804
  2.6 34.3 %copy-start.3 = (bf16[100,448]{1,0:T(8,128)(2,1)S(1)}, bf16[100,448]{1,0:T(8,128)(2,1)}, u32[]{:S(2)}) copy-start(bf16[100,448]{1,0:T(8,128)(2,1)} %refs_2_.1) | copy-start | bytes 268804
  2.6 22.4 %all-to-all-start = ((bf16[8,112,448]{2,1,0:T(8,128)(2,1)}), bf16[8,112,448]{2,1,0:T(8,128)(2,1)S(1)}, u32[]{:S(2)}, u32[]{:S(2)}) async-start(bf16[8,112,448]{2,1,0:T(8,128)(2,1)} %shard_map.122), calls=%async_computation | async-start | bytes 1835008 | tf_op jit(solution)/shard_map/all_to_all | solution.py:323
  8.6 33.5 %copy-start.5 = (s32[8,448]{1,0:T(8,128)S(1)}, s32[8,448]{1,0:T(8,128)}, u32[]{:S(2)}) copy-start(s32[8,448]{1,0:T(8,128)} %refs_0_.3) | copy-start | bytes 43012
  8.6 33.5 %copy-start.6 = (f32[8,448]{1,0:T(8,128)S(1)}, f32[8,448]{1,0:T(8,128)}, u32[]{:S(2)}) copy-start(f32[8,448]{1,0:T(8,128)} %refs_1_.3) | copy-start | bytes 43012
  9.3 10.4 %collective-permute-start = (bf16[16,128]{1,0:T(8,128)(2,1)S(1)}, bf16[16,128]{1,0:T(8,128)(2,1)S(1)}, u32[]{:S(2)}, u32[]{:S(2)}) collective-permute-start(bf16[16,128]{1,0:T(8,128)(2,1)S(1)} %get-tuple-element.39), channel_id=1, source_target_pairs={{0,1},{1,0},{2,3},{3,2},{4,5},{5,4},{6,7},{7,6},{8,9},{9,8},{10,11... | collective-permute-start | bytes 12296 | tf_op jit(solution)/shard_map/ppermute | solution.py:315
  15.9 28.1 %collective-permute-start.3 = (bf16[64,1024]{1,0:T(8,128)(2,1)S(1)}, bf16[64,1024]{1,0:T(8,128)(2,1)S(1)}, u32[]{:S(2)}, u32[]{:S(2)}) collective-permute-start(bf16[64,1024]{1,0:T(8,128)(2,1)S(1)} %get-tuple-element.37), channel_id=1, source_target_pairs={{0,1},{1,0},{2,3},{3,2},{4,5},{5,4},{6,7},{7,6},{8,9},{9,8},{10,11... | collective-permute-start | bytes 393224 | tf_op jit(solution)/shard_map/ppermute | solution.py:315
  17.8 7.2 %collective-permute-start.1 = (bf16[64,1024]{1,0:T(8,128)(2,1)S(1)}, bf16[64,1024]{1,0:T(8,128)(2,1)S(1)}, u32[]{:S(2)}, u32[]{:S(2)}) collective-permute-start(bf16[64,1024]{1,0:T(8,128)(2,1)S(1)} %get-tuple-element.38), channel_id=1, source_target_pairs={{1,2},{2,1},{3,4},{4,3},{5,6},{6,5},{7,8},{8,7},{9,10},{10,9},{11,... | collective-permute-start | bytes 393224 | tf_op jit(solution)/shard_map/ppermute | solution.py:311
  25.0 23.1 %all-to-all-start.1 = ((bf16[32,16,128]{2,1,0:T(8,128)(2,1)}), bf16[32,16,128]{2,1,0:T(8,128)(2,1)S(1)}, u32[]{:S(2)}, u32[]{:S(2)}) async-start(bf16[32,16,128]{2,1,0:T(8,128)(2,1)} %shard_map.121), calls=%async_computation.1 | async-start | bytes 262144 | tf_op jit(solution)/shard_map/all_to_all | solution.py:319
  37.4 11.8 %copy-start.2 = (bf16[100,448]{1,0:T(8,128)(2,1)}, bf16[100,448]{1,0:T(8,128)(2,1)S(1)}, u32[]{:S(2)}) copy-start(bf16[100,448]{1,0:T(8,128)(2,1)S(1)} %shard_map.123.refs_4_) | copy-start | bytes 268804
  37.4 6.6 %collective-permute-start.2 = (bf16[100,448]{1,0:T(8,128)(2,1)S(1)}, bf16[100,448]{1,0:T(8,128)(2,1)S(1)}, u32[]{:S(2)}, u32[]{:S(2)}) collective-permute-start(bf16[100,448]{1,0:T(8,128)(2,1)S(1)} %shard_map.123.refs_4_), channel_id=1, source_target_pairs={{0,1},{1,0},{2,3},{3,2},{4,5},{5,4},{6,7},{7,6},{8,9},{9,8},{10,11... | collective-permute-start | bytes 268808 | tf_op jit(solution)/shard_map/ppermute | solution.py:315
  49.2 17.7 %all-to-all-start.2 = ((bf16[8,32,16,128]{3,2,1,0:T(8,128)(2,1)}), bf16[8,32,16,128]{3,2,1,0:T(8,128)(2,1)S(1)}, u32[]{:S(2)}, u32[]{:S(2)}) async-start(bf16[8,32,16,128]{3,2,1,0:T(8,128)(2,1)} %shard_map.125), calls=%async_computation.2 | async-start | bytes 2097152 | tf_op jit(solution)/shard_map/all_to_all | solution.py:323
  59.2 7.7 %collective-permute-start.4 = (bf16[448,1536]{1,0:T(8,128)(2,1)}, bf16[448,1536]{1,0:T(8,128)(2,1)S(1)}, u32[]{:S(2)}, u32[]{:S(2)}) collective-permute-start(bf16[448,1536]{1,0:T(8,128)(2,1)} %get-tuple-element.23.refs_2_.refs_7_), channel_id=1, source_target_pairs={{0,1},{1,0},{2,3},{3,2},{4,5},{5,4},{6,7},{7,6},{8,9},{9,8},{10,11... | collective-permute-start | bytes 4128776 | tf_op jit(solution)/shard_map/ppermute | solution.py:315
  74.0 5.9 %copy-start.11 = (bf16[448,1024]{1,0:T(8,128)(2,1)S(1)}, bf16[448,1024]{1,0:T(8,128)(2,1)}, u32[]{:S(2)}) copy-start(bf16[448,1024]{1,0:T(8,128)(2,1)} %get-tuple-element.25) | copy-start | bytes 2752516
  74.0 22.2 %all-to-all-start.3 = ((bf16[8,36,16,128]{3,2,1,0:T(8,128)(2,1)}), bf16[8,36,16,128]{3,2,1,0:T(8,128)(2,1)S(1)}, u32[]{:S(2)}, u32[]{:S(2)}) async-start(bf16[8,36,16,128]{3,2,1,0:T(8,128)(2,1)} %get-tuple-element.32), calls=%async_computation.3 | async-start | bytes 2359296 | tf_op jit(solution)/shard_map/all_to_all | solution.py:323
  79.9 5.2 %collective-permute-start.5 = (bf16[448,1024]{1,0:T(8,128)(2,1)S(1)}, bf16[448,1024]{1,0:T(8,128)(2,1)S(1)}, u32[]{:S(2)}, u32[]{:S(2)}) collective-permute-start(bf16[448,1024]{1,0:T(8,128)(2,1)S(1)} %copy-done.11), channel_id=1, source_target_pairs={{0,1},{1,0},{2,3},{3,2},{4,5},{5,4},{6,7},{7,6},{8,9},{9,8},{10,11... | collective-permute-start | bytes 2752520 | tf_op jit(solution)/shard_map/ppermute | solution.py:315
  97.2 27.0 %all-to-all-start.4 = ((bf16[32,5,16,128]{3,2,1,0:T(8,128)(2,1)}), bf16[32,5,16,128]{3,2,1,0:T(8,128)(2,1)S(1)}, u32[]{:S(2)}, u32[]{:S(2)}) async-start(bf16[32,5,16,128]{3,2,1,0:T(8,128)(2,1)} %shard_map.130), calls=%async_computation.4 | async-start | bytes 1310720 | tf_op jit(solution)/shard_map/all_to_all | solution.py:319
  104.2 20.1 %collective-permute-start.7 = (bf16[64,1024]{1,0:T(8,128)(2,1)S(1)}, bf16[64,1024]{1,0:T(8,128)(2,1)S(1)}, u32[]{:S(2)}, u32[]{:S(2)}) collective-permute-start(bf16[64,1024]{1,0:T(8,128)(2,1)S(1)} %get-tuple-element.29), channel_id=1, source_target_pairs={{1,2},{2,1},{3,4},{4,3},{5,6},{6,5},{7,8},{8,7},{9,10},{10,9},{11,... | collective-permute-start | bytes 393224 | tf_op jit(solution)/shard_map/ppermute | solution.py:311
  109.5 14.8 %collective-permute-start.6 = (bf16[64,1024]{1,0:T(8,128)(2,1)S(1)}, bf16[64,1024]{1,0:T(8,128)(2,1)S(1)}, u32[]{:S(2)}, u32[]{:S(2)}) collective-permute-start(bf16[64,1024]{1,0:T(8,128)(2,1)S(1)} %get-tuple-element.28), channel_id=1, source_target_pairs={{0,1},{1,0},{2,3},{3,2},{4,5},{5,4},{6,7},{7,6},{8,9},{9,8},{10,11... | collective-permute-start | bytes 393224 | tf_op jit(solution)/shard_map/ppermute | solution.py:315
  125.2 18.2 %all-to-all-start.5 = ((bf16[16,5,16,128]{3,2,1,0:T(8,128)(2,1)}), bf16[16,5,16,128]{3,2,1,0:T(8,128)(2,1)S(1)}, u32[]{:S(2)}, u32[]{:S(2)}) async-start(bf16[16,5,16,128]{3,2,1,0:T(8,128)(2,1)} %shard_map.131), calls=%async_computation.5 | async-start | bytes 655360 | tf_op jit(solution)/shard_map/all_to_all | solution.py:455
  (3 other events, 7.2 us)

commit v3 on v2

--- a/solution.py
+++ b/solution.py
@@ -11,7 +11,10 @@
 KNB = 8
 LANES = 128
 TILE = 16
+DEC_TILES = 4
 MEMBERS = 8
+GRID = ("z", "y", "core")
+PAIR = ("z", "y")
 
 norm_eps = 1e-05
 alpha_fair = 0.95
@@ -269,22 +272,26 @@
     copies.start(mid_ref, out_hbm.at[0]).wait()
 
 
-def sum_mem_body(got_ref, out_hbm, out_ref, copies):
-    pairs, tiles = out_ref.shape[:2]
+def total_of(got_ref):
     total = got_ref[0].astype(f32)
-    for m in range(1, MEMBERS):
-        total += got_ref[m].astype(f32)
-    total = total.astype(bf16)
-    out_ref[:, 0] = total[0:pairs]
-    out_ref[:, 1:] = jnp.broadcast_to(total[pairs:][None], (pairs, tiles - 1, TILE, LANES))
+    for i in range(1, got_ref.shape[0]):
+        total += got_ref[i].astype(f32)
+    return total.astype(bf16)
+
+
+def sum_body(got_ref, out_hbm, out_ref, copies):
+    total = total_of(got_ref)
+    parts, tiles = out_ref.shape[:2]
+    dec = DEC_TILES
+    weights = got_ref.shape[1] - dec
+    each = weights // parts
+    out_ref[:, 0:each] = total[0:weights].reshape(parts, each, TILE, LANES)
+    out_ref[:, each:] = jnp.broadcast_to(total[weights:][None], (parts, dec, TILE, LANES))
     copies.start(out_ref, out_hbm).wait()
 
 
-def sum_grid_body(got_ref, out_hbm, out_ref, copies):
-    total = got_ref[0].astype(f32)
-    for g in range(1, got_ref.shape[0]):
-        total += got_ref[g].astype(f32)
-    out_ref[...] = total.astype(bf16)
+def sum_last_body(got_ref, out_hbm, out_ref, copies):
+    out_ref[...] = total_of(got_ref)
     for c in [copies.start(out_ref, out_hbm.at[m]) for m in range(out_hbm.shape[0])]:
         c.wait()
 
@@ -306,9 +313,9 @@
 
 
 def other_pair(a):
-    size = lax.axis_size(("pair", "core"))
+    size = lax.axis_size(GRID)
     pairs = [(i, i + (1 if i % 2 else -1)) for i in range(1, size - 1)]
-    return lax.ppermute(a, ("pair", "core"), pairs)
+    return lax.ppermute(a, GRID, pairs)
 
 
 def other_core(a):
@@ -316,7 +323,7 @@
 
 
 def over_pairs(a):
-    return lax.all_to_all(a, "pair", 0, 0, tiled=True)
+    return lax.all_to_all(a, PAIR, 0, 0, tiled=True)
 
 
 def over_mem(a):
@@ -326,7 +333,7 @@
 def on_device(
     hidden, predictions, target, area, var_weight, interior, sources, edge_weight, w_node, w_dec
 ):
-    pairs = lax.axis_size("pair")
+    pairs = lax.axis_size(PAIR)
     nodes, width = hidden.shape[1:]
     half = width // 2
     cols = half // LANES
@@ -366,7 +373,7 @@
         edges_body, [sent((nodes + 2 * K, nodes), bf16)], (sources, edge_weight),
         [vmem((nodes + 2 * K, nodes), bf16)], sems=1,
     )
-    shards = over_pairs(after(tiles, every_pred, far))
+    shards = over_pairs(after(tiles, every_pred))
     rstd, keep, send = call(
         norm_body,
         [sent((nodes, LANES), f32), sent((nodes, half), bf16), sent((nodes, width + half), bf16)],
@@ -391,7 +398,7 @@
     (spread,) = call(
         share_body,
         [sent((MEMBERS, pairs, TILE, LANES), bf16)],
-        (after(shards, pred_got, near, at),),
+        (after(shards, pred_got, near, far, at),),
         sems=MEMBERS,
     )
     weight = over_mem(spread)
@@ -428,14 +435,23 @@
     )
     from_near = other_core(to_near)
     from_far = other_pair(to_far)
-    (grid_out,) = call(
-        sum_mem_body,
-        [sent((pairs, 1 + cols, TILE, LANES), bf16)],
+    n_z, n_y = lax.axis_size("z"), lax.axis_size("y")
+    (z_out,) = call(
+        sum_body,
+        [sent((n_z, n_y + cols, TILE, LANES), bf16)],
         (after(mem_parts, to_near),),
-        [vmem((pairs, 1 + cols, TILE, LANES), bf16)],
+        [vmem((n_z, n_y + cols, TILE, LANES), bf16)],
         sems=1,
     )
-    grid_parts = over_pairs(grid_out)
+    z_parts = lax.all_to_all(z_out, "z", 0, 0, tiled=True)
+    (y_out,) = call(
+        sum_body,
+        [sent((n_y, 1 + cols, TILE, LANES), bf16)],
+        (after(z_parts, from_near),),
+        [vmem((n_y, 1 + cols, TILE, LANES), bf16)],
+        sems=1,
+    )
+    y_parts = lax.all_to_all(y_out, "y", 0, 0, tiled=True)
     (hidden_grad,) = call(
         join_body,
         [sent((1, nodes, width), bf16)],
@@ -446,9 +462,9 @@
         sems=3,
     )
     (last_out,) = call(
-        sum_grid_body,
+        sum_last_body,
         [sent((2 * MEMBERS, 1 + cols, TILE, LANES), bf16)],
-        (after(grid_parts, from_near, from_far),),
+        (after(y_parts, hidden_grad),),
         [vmem((1 + cols, TILE, LANES), bf16)],
         sems=2 * MEMBERS,
     )
@@ -464,10 +480,8 @@
 
 def solution(mesh):
     members, blocks = mesh.shape["mem"], mesh.shape["grid"]
-    split = jax.sharding.Mesh(
-        mesh.devices.reshape(members, blocks // 2, 2), ("mem", "pair", "core")
-    )
-    grid = ("pair", "core")
+    split = jax.sharding.Mesh(mesh.devices.reshape(members, blocks // 8, 4, 2), ("mem",) + GRID)
+    grid = GRID
     placed = (
         P("mem", grid, None),
         P("mem", None, grid),

time: 145 us -> 141 us (0.972)
  blocking collectives: 0 us -> 15.5 us
  waiting for transfers between devices: 38.4 us -> 26.2 us
  starting transfers between devices: 77.6 us -> 69.2 us
    ppermute x2, waiting for transfers between devices: 17.4 us -> 0.01 us  [other_pair(): return lax.ppermute(a, GRID, pairs)]
    all_to_all x0 -> x1, blocking collectives: none -> 15.5 us  [on_device(): last = lax.all_to_all(last_out, ('mem', 'core'), 0, 0, tiled=True)]
    all_to_all x3, starting transfers between devices: 29.2 us -> 23.7 us  [the longest x1 15.7 us: over_pairs(): return lax.all_to_all(a, PAIR, 0, 0, tiled=True)]
    all_to_all x3, waiting for transfers between devices: 9.46 us -> 14.1 us  [the longest x1 5.09 us: on_device(): z_parts = lax.all_to_all(z_out, 'z', 0, 0, tiled=True)]
    ppermute x2, starting transfers between devices: 7.22 us -> 4.7 us  [other_pair(): return lax.ppermute(a, GRID, pairs)]
    all_to_all x3, starting transfers between devices: 18.3 us -> 16.1 us  [over_mem(): return lax.all_to_all(a, 'mem', 0, 0, tiled=True)]
    ppermute x6, starting transfers between devices: 22.9 us -> 24.7 us  [other_core(): return lax.ppermute(a, 'core', [(0, 1), (1, 0)])]
    pallas_call x12 -> x13, Pallas kernels: 24.3 us -> 24.8 us  [call(): pl.pallas_call(kernel, out_shape=out, in_specs=[pl.BlockSpec(memory_space...]
  transfers between devices with their start and end apart: 14 -> 14, of which waited for: 7 -> 6; matrix products, arithmetic and copies ran while one was open for 1% -> 1% of each run, Pallas kernels for 9% -> 10%
where the time goes in v3:
time: 141 us; the launch traced here: 140 us
  starting transfers between devices  69.2 us (49%)
  waiting for transfers between devices  26.2 us (19%)
  Pallas kernels  24.8 us (18%)
  blocking collectives  15.5 us (11%)
  local copies, waits for them, and re-layouts  2.79 us (2%)
    pallas_call x13, Pallas kernels, call(): pl.pallas_call(kernel, out_shape=out, in_specs=[pl.BlockSpec(memory_space...  24.8 us
    ppermute x6, starting transfers between devices, other_core(): return lax.ppermute(a, 'core', [(0, 1), (1, 0)])  24.7 us
    all_to_all x3, starting transfers between devices, over_mem(): return lax.all_to_all(a, 'mem', 0, 0, tiled=True)  16.1 us
    all_to_all x1, starting transfers between devices, over_pairs(): return lax.all_to_all(a, PAIR, 0, 0, tiled=True)  15.7 us
    all_to_all x1, blocking collectives, on_device(): last = lax.all_to_all(last_out, ('mem', 'core'), 0, 0, tiled=True)  15.5 us
    all_to_all x3, waiting for transfers between devices, over_mem(): return lax.all_to_all(a, 'mem', 0, 0, tiled=True)  7.1 us
    all_to_all x1, waiting for transfers between devices, on_device(): z_parts = lax.all_to_all(z_out, 'z', 0, 0, tiled=True)  5.09 us
    all_to_all x1, waiting for transfers between devices, on_device(): y_parts = lax.all_to_all(y_out, 'y', 0, 0, tiled=True)  5.09 us
  transfers between devices with their start and end apart: 14, of which 6 were waited for; matrix products, arithmetic and copies ran while one was open for 1% of the time, Pallas kernels for 10%

profile of v3, /device:TPU:1, one launch (start us, length us, event | category | flops | bytes accessed | tf_op | source)
XLA Modules:
  0.0 139.7 jit_solution(17658758215918585645)
XLA Ops:
  2.6 6.0 %all-to-all-start = ((bf16[8,112,448]{2,1,0:T(8,128)(2,1)}), bf16[8,112,448]{2,1,0:T(8,128)(2,1)S(1)}, u32[]{:S(2)}, u32[]{:S(2)}) async-start(bf16[8,112,448]{2,1,0:T(8,128)(2,1)} %shard_map.122), calls=%async_computation | async-start | bytes 1835008 | tf_op jit(solution)/shard_map/all_to_all | solution.py:330
  9.3 6.5 %collective-permute-start = (bf16[16,128]{1,0:T(8,128)(2,1)S(1)}, bf16[16,128]{1,0:T(8,128)(2,1)S(1)}, u32[]{:S(2)}, u32[]{:S(2)}) collective-permute-start(bf16[16,128]{1,0:T(8,128)(2,1)S(1)} %get-tuple-element.41), channel_id=1, source_target_pairs={{0,1},{1,0},{2,3},{3,2},{4,5},{5,4},{6,7},{7,6},{8,9},{9,8},{10,11... | collective-permute-start | bytes 12296 | tf_op jit(solution)/shard_map/ppermute | solution.py:322
  15.9 1.9 %collective-permute-start.3 = (bf16[64,1024]{1,0:T(8,128)(2,1)S(1)}, bf16[64,1024]{1,0:T(8,128)(2,1)S(1)}, u32[]{:S(2)}, u32[]{:S(2)}) collective-permute-start(bf16[64,1024]{1,0:T(8,128)(2,1)S(1)} %get-tuple-element.39), channel_id=1, source_target_pairs={{1,2},{2,1},{3,4},{4,3},{5,6},{6,5},{7,8},{8,7},{9,10},{10,9},{11,... | collective-permute-start | bytes 393224 | tf_op jit(solution)/shard_map/ppermute | solution.py:318
  20.5 15.7 %all-to-all-start.1 = ((bf16[32,16,128]{2,1,0:T(8,128)(2,1)}), bf16[32,16,128]{2,1,0:T(8,128)(2,1)S(1)}, u32[]{:S(2)}, u32[]{:S(2)}) async-start(bf16[32,16,128]{2,1,0:T(8,128)(2,1)} %shard_map.121), calls=%async_computation.1 | async-start | bytes 262144 | tf_op jit(solution)/shard_map/all_to_all | solution.py:326
  36.8 4.8 %collective-permute-start.1 = (bf16[100,448]{1,0:T(8,128)(2,1)S(1)}, bf16[100,448]{1,0:T(8,128)(2,1)S(1)}, u32[]{:S(2)}, u32[]{:S(2)}) collective-permute-start(bf16[100,448]{1,0:T(8,128)(2,1)S(1)} %shard_map.123.refs_4_), channel_id=1, source_target_pairs={{0,1},{1,0},{2,3},{3,2},{4,5},{5,4},{6,7},{7,6},{8,9},{9,8},{10,11... | collective-permute-start | bytes 268808 | tf_op jit(solution)/shard_map/ppermute | solution.py:322
  43.5 3.9 %all-to-all-done.1.refs_0_ = bf16[32,16,128]{2,1,0:T(8,128)(2,1)S(1)} async-done(((bf16[32,16,128]{2,1,0:T(8,128)(2,1)}), bf16[32,16,128]{2,1,0:T(8,128)(2,1)S(1)}, u32[]{:S(2)}, u32[]{:S(2)}) %all-to-all-start.1) | async-done | bytes 131104 | tf_op jit(solution)/shard_map/all_to_all | solution.py:326
  48.5 4.5 %all-to-all-start.2 = ((bf16[8,32,16,128]{3,2,1,0:T(8,128)(2,1)}), bf16[8,32,16,128]{3,2,1,0:T(8,128)(2,1)S(1)}, u32[]{:S(2)}, u32[]{:S(2)}) async-start(bf16[8,32,16,128]{3,2,1,0:T(8,128)(2,1)} %shard_map.125), calls=%async_computation.2 | async-start | bytes 2097152 | tf_op jit(solution)/shard_map/all_to_all | solution.py:330
  53.1 3.6 %shard_map.126 = (f32[448,128]{1,0:T(8,128)}, bf16[448,512]{1,0:T(8,128)(2,1)}, bf16[448,1536]{1,0:T(8,128)(2,1)}) custom-call(s32[1]{0:T(128)} %bitcast.refs_0_, bf16[448,1024]{1,0:T(8,128)(2,1)S(1)} %bitcast.9, bf16[64,1024]{1,0:T(8,128)(2,1)S(1)} %collective-permute-done.2.refs_2_, bf16[64,1024]{1,0:T(8,128)(2,1)S(1)} %collective-permute-done.3.refs_3_, ...), custom_call_target="tpu_custom_call" | custom-call | flops 528482304 | bytes 3760128 | tf_op jit(solution)/shard_map/pallas_call | solution.py:70
  56.7 6.2 %collective-permute-start.4 = (bf16[448,1536]{1,0:T(8,128)(2,1)}, bf16[448,1536]{1,0:T(8,128)(2,1)S(1)}, u32[]{:S(2)}, u32[]{:S(2)}) collective-permute-start(bf16[448,1536]{1,0:T(8,128)(2,1)} %get-tuple-element.24.refs_2_.refs_7_), channel_id=1, source_target_pairs={{0,1},{1,0},{2,3},{3,2},{4,5},{5,4},{6,7},{7,6},{8,9},{9,8},{10,11... | collective-permute-start | bytes 4128776 | tf_op jit(solution)/shard_map/ppermute | solution.py:322
  62.9 2.9 %collective-permute-done.4.refs_6_ = bf16[448,1536]{1,0:T(8,128)(2,1)S(1)} collective-permute-done((bf16[448,1536]{1,0:T(8,128)(2,1)}, bf16[448,1536]{1,0:T(8,128)(2,1)S(1)}, u32[]{:S(2)}, u32[]{:S(2)}) %collective-permute-start.4) | collective-permute-done | bytes 1376288 | tf_op jit(solution)/shard_map/ppermute | solution.py:322
  66.9 6.0 %shard_map.127 = (bf16[8,36,16,128]{3,2,1,0:T(8,128)(2,1)}, bf16[448,512]{1,0:T(8,128)(2,1)}, bf16[448,1024]{1,0:T(8,128)(2,1)}) custom-call(s32[1]{0:T(128)} %bitcast.refs_0_, bf16[8,32,16,128]{3,2,1,0:T(8,128)(2,1)S(1)} %all-to-all-done.2.refs_1_, bf16[448,1536]{1,0:T(8,128)(2,1)} %get-tuple-element.24.refs_2_.refs_7_, ...), custom_call_target="tpu_custom_call" | custom-call | flops 2348810240 | bytes 7199744 | tf_op jit(solution)/shard_map/pallas_call | solution.py:70
  73.0 5.6 %all-to-all-start.3 = ((bf16[8,36,16,128]{3,2,1,0:T(8,128)(2,1)}), bf16[8,36,16,128]{3,2,1,0:T(8,128)(2,1)S(1)}, u32[]{:S(2)}, u32[]{:S(2)}) async-start(bf16[8,36,16,128]{3,2,1,0:T(8,128)(2,1)} %get-tuple-element.33), calls=%async_computation.3 | async-start | bytes 2359296 | tf_op jit(solution)/shard_map/all_to_all | solution.py:330
  78.5 2.6 %collective-permute-start.5 = (bf16[448,1024]{1,0:T(8,128)(2,1)S(1)}, bf16[448,1024]{1,0:T(8,128)(2,1)S(1)}, u32[]{:S(2)}, u32[]{:S(2)}) collective-permute-start(bf16[448,1024]{1,0:T(8,128)(2,1)S(1)} %copy-done.11), channel_id=1, source_target_pairs={{0,1},{1,0},{2,3},{3,2},{4,5},{5,4},{6,7},{7,6},{8,9},{9,8},{10,11... | collective-permute-start | bytes 2752520 | tf_op jit(solution)/shard_map/ppermute | solution.py:322
  81.1 2.1 %collective-permute-done.5.refs_2_ = bf16[448,1024]{1,0:T(8,128)(2,1)S(1)} collective-permute-done((bf16[448,1024]{1,0:T(8,128)(2,1)S(1)}, bf16[448,1024]{1,0:T(8,128)(2,1)S(1)}, u32[]{:S(2)}, u32[]{:S(2)}) %collective-permute-start.5) | collective-permute-done | bytes 917536 | tf_op jit(solution)/shard_map/ppermute | solution.py:322
  83.2 4.6 %shard_map.128 = (bf16[448,1024]{1,0:T(8,128)(2,1)}, f32[128,1024]{1,0:T(8,128)}, bf16[64,1024]{1,0:T(8,128)(2,1)S(1)}, bf16[64,1024]{1,0:T(8,128)(2,1)S(1)}) custom-call(s32[1]{0:T(128)} %bitcast.refs_0_, bf16[8,32,16,128]{3,2,1,0:T(8,128)(2,1)S(1)} %all-to-all-done.2.refs_1_, bf16[448,1024]{1,0:T(8,128)(2,1)S(1)} %collective-permute-done.5.refs_2_, ...), custom_call_target="tpu_custom_call" | custom-call | flops 528482304 | bytes 6544896 | tf_op jit(solution)/shard_map/pallas_call | solution.py:70
  87.8 7.1 %all-to-all-done.3.refs_0_ = bf16[8,36,16,128]{3,2,1,0:T(8,128)(2,1)S(1)} async-done(((bf16[8,36,16,128]{3,2,1,0:T(8,128)(2,1)}), bf16[8,36,16,128]{3,2,1,0:T(8,128)(2,1)S(1)}, u32[]{:S(2)}, u32[]{:S(2)}) %all-to-all-start.3) | async-done | bytes 1179680 | tf_op jit(solution)/shard_map/all_to_all | solution.py:330
  95.8 3.4 %all-to-all-start.4 = ((bf16[8,8,16,128]{3,2,1,0:T(8,128)(2,1)}), bf16[8,8,16,128]{3,2,1,0:T(8,128)(2,1)S(1)}, u32[]{:S(2)}, u32[]{:S(2)}) async-start(bf16[8,8,16,128]{3,2,1,0:T(8,128)(2,1)} %shard_map.130), calls=%async_computation.4 | async-start | bytes 524288 | tf_op jit(solution)/shard_map/all_to_all | solution.py:446
  99.2 2.7 %collective-permute-start.6 = (bf16[64,1024]{1,0:T(8,128)(2,1)S(1)}, bf16[64,1024]{1,0:T(8,128)(2,1)S(1)}, u32[]{:S(2)}, u32[]{:S(2)}) collective-permute-start(bf16[64,1024]{1,0:T(8,128)(2,1)S(1)} %get-tuple-element.29), channel_id=1, source_target_pairs={{0,1},{1,0},{2,3},{3,2},{4,5},{5,4},{6,7},{7,6},{8,9},{9,8},{10,11... | collective-permute-start | bytes 393224 | tf_op jit(solution)/shard_map/ppermute | solution.py:322
  101.9 2.8 %collective-permute-start.7 = (bf16[64,1024]{1,0:T(8,128)(2,1)S(1)}, bf16[64,1024]{1,0:T(8,128)(2,1)S(1)}, u32[]{:S(2)}, u32[]{:S(2)}) collective-permute-start(bf16[64,1024]{1,0:T(8,128)(2,1)S(1)} %get-tuple-element.30), channel_id=1, source_target_pairs={{1,2},{2,1},{3,4},{4,3},{5,6},{6,5},{7,8},{8,7},{9,10},{10,9},{11,... | collective-permute-start | bytes 393224 | tf_op jit(solution)/shard_map/ppermute | solution.py:318
  104.7 5.1 %all-to-all-done.4.refs_0_ = bf16[8,8,16,128]{3,2,1,0:T(8,128)(2,1)S(1)} async-done(((bf16[8,8,16,128]{3,2,1,0:T(8,128)(2,1)}), bf16[8,8,16,128]{3,2,1,0:T(8,128)(2,1)S(1)}, u32[]{:S(2)}, u32[]{:S(2)}) %all-to-all-start.4) | async-done | bytes 262176 | tf_op jit(solution)/shard_map/all_to_all | solution.py:446
  110.5 4.6 %all-to-all-start.5 = ((bf16[4,5,16,128]{3,2,1,0:T(8,128)(2,1)}), bf16[4,5,16,128]{3,2,1,0:T(8,128)(2,1)S(1)}, u32[]{:S(2)}, u32[]{:S(2)}) async-start(bf16[4,5,16,128]{3,2,1,0:T(8,128)(2,1)} %shard_map.131), calls=%async_computation.5 | async-start | bytes 163840 | tf_op jit(solution)/shard_map/all_to_all | solution.py:454
  115.1 2.3 %shard_map.129 = bf16[1,448,1024]{2,1,0:T(8,128)(2,1)} custom-call(s32[1]{0:T(128)} %bitcast.refs_0_, bf16[64,1024]{1,0:T(8,128)(2,1)S(1)} %collective-permute-done.6.refs_1_, bf16[64,1024]{1,0:T(8,128)(2,1)S(1)} %collective-permute-done.7.refs_2_, bf16[448,1024]{1,0:T(8,128)(2,1)} %get-tuple-element.31.refs_3_, f32[128,1024]{1,0:T(8,128)} %get-tuple-element.32.refs_4_), custom_call_target="tpu_custom_call" | custom-call | bytes 2621440 | tf_op jit(solution)/shard_map/pallas_call | solution.py:70
  117.4 5.1 %all-to-all-done.5.refs_0_ = bf16[4,5,16,128]{3,2,1,0:T(8,128)(2,1)S(1)} async-done(((bf16[4,5,16,128]{3,2,1,0:T(8,128)(2,1)}), bf16[4,5,16,128]{3,2,1,0:T(8,128)(2,1)S(1)}, u32[]{:S(2)}, u32[]{:S(2)}) %all-to-all-start.5) | async-done | bytes 81952 | tf_op jit(solution)/shard_map/all_to_all | solution.py:454
  123.4 15.5 %all_to_all.35.refs_1_ = bf16[16,5,16,128]{3,2,1,0:T(8,128)(2,1)S(1)} all-to-all(bf16[16,5,16,128]{3,2,1,0:T(8,128)(2,1)} %shard_map.132), channel_id=1, replica_groups=mesh['mem'=8,'z'=8,'y'=4,'core'=2] {'mem','core'}, dimensions={0} | all-to-all | bytes 655360 | tf_op jit(solution)/shard_map/all_to_all | solution.py:471
  (48 shorter events, 13.0 us)
Async XLA Ops:
  1.5 14.3 %copy-start.4 = (bf16[1,448,1024]{2,1,0:T(8,128)(2,1)S(1)}, bf16[1,448,1024]{2,1,0:T(8,128)(2,1)}, u32[]{:S(2)}) copy-start(bf16[1,448,1024]{2,1,0:T(8,128)(2,1)} %param.10) | copy-start | bytes 2752516
  2.5 17.2 %copy-start.7 = (f32[448]{0:T(512)S(1)}, f32[448]{0:T(512)}, u32[]{:S(2)}) copy-start(f32[448]{0:T(512)} %param.13) | copy-start | bytes 5380
  2.5 17.2 %copy-start.8 = (s32[448]{0:T(512)S(1)}, s32[448]{0:T(512)}, u32[]{:S(2)}) copy-start(s32[448]{0:T(512)} %param.15) | copy-start | bytes 5380
  2.5 33.7 %copy-start.9 = (f32[100]{0:T(128)S(1)}, f32[100]{0:T(128)}, u32[]{:S(2)}) copy-start(f32[100]{0:T(128)} %param.14) | copy-start | bytes 1204
  2.6 33.7 %copy-start.1 = (bf16[1,100,448]{2,1,0:T(8,128)(2,1)S(1)}, bf16[1,100,448]{2,1,0:T(8,128)(2,1)}, u32[]{:S(2)}) copy-start(bf16[1,100,448]{2,1,0:T(8,128)(2,1)} %refs_1_.2) | copy-start | bytes 268804
  2.6 33.7 %copy-start.3 = (bf16[100,448]{1,0:T(8,128)(2,1)S(1)}, bf16[100,448]{1,0:T(8,128)(2,1)}, u32[]{:S(2)}) copy-start(bf16[100,448]{1,0:T(8,128)(2,1)} %refs_2_.1) | copy-start | bytes 268804
  2.6 17.9 %all-to-all-start = ((bf16[8,112,448]{2,1,0:T(8,128)(2,1)}), bf16[8,112,448]{2,1,0:T(8,128)(2,1)S(1)}, u32[]{:S(2)}, u32[]{:S(2)}) async-start(bf16[8,112,448]{2,1,0:T(8,128)(2,1)} %shard_map.122), calls=%async_computation | async-start | bytes 1835008 | tf_op jit(solution)/shard_map/all_to_all | solution.py:330
  8.6 33.1 %copy-start.5 = (s32[8,448]{1,0:T(8,128)S(1)}, s32[8,448]{1,0:T(8,128)}, u32[]{:S(2)}) copy-start(s32[8,448]{1,0:T(8,128)} %refs_0_.3) | copy-start | bytes 43012
  8.6 33.1 %copy-start.6 = (f32[8,448]{1,0:T(8,128)S(1)}, f32[8,448]{1,0:T(8,128)}, u32[]{:S(2)}) copy-start(f32[8,448]{1,0:T(8,128)} %refs_1_.3) | copy-start | bytes 43012
  9.3 10.4 %collective-permute-start = (bf16[16,128]{1,0:T(8,128)(2,1)S(1)}, bf16[16,128]{1,0:T(8,128)(2,1)S(1)}, u32[]{:S(2)}, u32[]{:S(2)}) collective-permute-start(bf16[16,128]{1,0:T(8,128)(2,1)S(1)} %get-tuple-element.41), channel_id=1, source_target_pairs={{0,1},{1,0},{2,3},{3,2},{4,5},{5,4},{6,7},{7,6},{8,9},{9,8},{10,11... | collective-permute-start | bytes 12296 | tf_op jit(solution)/shard_map/ppermute | solution.py:322
  15.9 27.6 %collective-permute-start.3 = (bf16[64,1024]{1,0:T(8,128)(2,1)S(1)}, bf16[64,1024]{1,0:T(8,128)(2,1)S(1)}, u32[]{:S(2)}, u32[]{:S(2)}) collective-permute-start(bf16[64,1024]{1,0:T(8,128)(2,1)S(1)} %get-tuple-element.39), channel_id=1, source_target_pairs={{1,2},{2,1},{3,4},{4,3},{5,6},{6,5},{7,8},{8,7},{9,10},{10,9},{11,... | collective-permute-start | bytes 393224 | tf_op jit(solution)/shard_map/ppermute | solution.py:318
  17.8 25.7 %collective-permute-start.2 = (bf16[64,1024]{1,0:T(8,128)(2,1)S(1)}, bf16[64,1024]{1,0:T(8,128)(2,1)S(1)}, u32[]{:S(2)}, u32[]{:S(2)}) collective-permute-start(bf16[64,1024]{1,0:T(8,128)(2,1)S(1)} %get-tuple-element.40), channel_id=1, source_target_pairs={{0,1},{1,0},{2,3},{3,2},{4,5},{5,4},{6,7},{7,6},{8,9},{9,8},{10,11... | collective-permute-start | bytes 393224 | tf_op jit(solution)/shard_map/ppermute | solution.py:322
  20.5 26.9 %all-to-all-start.1 = ((bf16[32,16,128]{2,1,0:T(8,128)(2,1)}), bf16[32,16,128]{2,1,0:T(8,128)(2,1)S(1)}, u32[]{:S(2)}, u32[]{:S(2)}) async-start(bf16[32,16,128]{2,1,0:T(8,128)(2,1)} %shard_map.121), calls=%async_computation.1 | async-start | bytes 262144 | tf_op jit(solution)/shard_map/all_to_all | solution.py:326
  36.8 11.7 %copy-start.2 = (bf16[100,448]{1,0:T(8,128)(2,1)}, bf16[100,448]{1,0:T(8,128)(2,1)S(1)}, u32[]{:S(2)}) copy-start(bf16[100,448]{1,0:T(8,128)(2,1)S(1)} %shard_map.123.refs_4_) | copy-start | bytes 268804
  36.8 6.7 %collective-permute-start.1 = (bf16[100,448]{1,0:T(8,128)(2,1)S(1)}, bf16[100,448]{1,0:T(8,128)(2,1)S(1)}, u32[]{:S(2)}, u32[]{:S(2)}) collective-permute-start(bf16[100,448]{1,0:T(8,128)(2,1)S(1)} %shard_map.123.refs_4_), channel_id=1, source_target_pairs={{0,1},{1,0},{2,3},{3,2},{4,5},{5,4},{6,7},{7,6},{8,9},{9,8},{10,11... | collective-permute-start | bytes 268808 | tf_op jit(solution)/shard_map/ppermute | solution.py:322
  48.5 17.3 %all-to-all-start.2 = ((bf16[8,32,16,128]{3,2,1,0:T(8,128)(2,1)}), bf16[8,32,16,128]{3,2,1,0:T(8,128)(2,1)S(1)}, u32[]{:S(2)}, u32[]{:S(2)}) async-start(bf16[8,32,16,128]{3,2,1,0:T(8,128)(2,1)} %shard_map.125), calls=%async_computation.2 | async-start | bytes 2097152 | tf_op jit(solution)/shard_map/all_to_all | solution.py:330
  56.7 9.1 %collective-permute-start.4 = (bf16[448,1536]{1,0:T(8,128)(2,1)}, bf16[448,1536]{1,0:T(8,128)(2,1)S(1)}, u32[]{:S(2)}, u32[]{:S(2)}) collective-permute-start(bf16[448,1536]{1,0:T(8,128)(2,1)} %get-tuple-element.24.refs_2_.refs_7_), channel_id=1, source_target_pairs={{0,1},{1,0},{2,3},{3,2},{4,5},{5,4},{6,7},{7,6},{8,9},{9,8},{10,11... | collective-permute-start | bytes 4128776 | tf_op jit(solution)/shard_map/ppermute | solution.py:322
  73.0 5.6 %copy-start.11 = (bf16[448,1024]{1,0:T(8,128)(2,1)S(1)}, bf16[448,1024]{1,0:T(8,128)(2,1)}, u32[]{:S(2)}) copy-start(bf16[448,1024]{1,0:T(8,128)(2,1)} %get-tuple-element.26) | copy-start | bytes 2752516
  73.0 21.9 %all-to-all-start.3 = ((bf16[8,36,16,128]{3,2,1,0:T(8,128)(2,1)}), bf16[8,36,16,128]{3,2,1,0:T(8,128)(2,1)S(1)}, u32[]{:S(2)}, u32[]{:S(2)}) async-start(bf16[8,36,16,128]{3,2,1,0:T(8,128)(2,1)} %get-tuple-element.33), calls=%async_computation.3 | async-start | bytes 2359296 | tf_op jit(solution)/shard_map/all_to_all | solution.py:330
  78.5 4.6 %collective-permute-start.5 = (bf16[448,1024]{1,0:T(8,128)(2,1)S(1)}, bf16[448,1024]{1,0:T(8,128)(2,1)S(1)}, u32[]{:S(2)}, u32[]{:S(2)}) collective-permute-start(bf16[448,1024]{1,0:T(8,128)(2,1)S(1)} %copy-done.11), channel_id=1, source_target_pairs={{0,1},{1,0},{2,3},{3,2},{4,5},{5,4},{6,7},{7,6},{8,9},{9,8},{10,11... | collective-permute-start | bytes 2752520 | tf_op jit(solution)/shard_map/ppermute | solution.py:322
  95.8 14.0 %all-to-all-start.4 = ((bf16[8,8,16,128]{3,2,1,0:T(8,128)(2,1)}), bf16[8,8,16,128]{3,2,1,0:T(8,128)(2,1)S(1)}, u32[]{:S(2)}, u32[]{:S(2)}) async-start(bf16[8,8,16,128]{3,2,1,0:T(8,128)(2,1)} %shard_map.130), calls=%async_computation.4 | async-start | bytes 524288 | tf_op jit(solution)/shard_map/all_to_all | solution.py:446
  99.2 5.5 %collective-permute-start.6 = (bf16[64,1024]{1,0:T(8,128)(2,1)S(1)}, bf16[64,1024]{1,0:T(8,128)(2,1)S(1)}, u32[]{:S(2)}, u32[]{:S(2)}) collective-permute-start(bf16[64,1024]{1,0:T(8,128)(2,1)S(1)} %get-tuple-element.29), channel_id=1, source_target_pairs={{0,1},{1,0},{2,3},{3,2},{4,5},{5,4},{6,7},{7,6},{8,9},{9,8},{10,11... | collective-permute-start | bytes 393224 | tf_op jit(solution)/shard_map/ppermute | solution.py:322
  101.9 13.2 %collective-permute-start.7 = (bf16[64,1024]{1,0:T(8,128)(2,1)S(1)}, bf16[64,1024]{1,0:T(8,128)(2,1)S(1)}, u32[]{:S(2)}, u32[]{:S(2)}) collective-permute-start(bf16[64,1024]{1,0:T(8,128)(2,1)S(1)} %get-tuple-element.30), channel_id=1, source_target_pairs={{1,2},{2,1},{3,4},{4,3},{5,6},{6,5},{7,8},{8,7},{9,10},{10,9},{11,... | collective-permute-start | bytes 393224 | tf_op jit(solution)/shard_map/ppermute | solution.py:318
  110.5 12.0 %all-to-all-start.5 = ((bf16[4,5,16,128]{3,2,1,0:T(8,128)(2,1)}), bf16[4,5,16,128]{3,2,1,0:T(8,128)(2,1)S(1)}, u32[]{:S(2)}, u32[]{:S(2)}) async-start(bf16[4,5,16,128]{3,2,1,0:T(8,128)(2,1)} %shard_map.131), calls=%async_computation.5 | async-start | bytes 163840 | tf_op jit(solution)/shard_map/all_to_all | solution.py:454
  (3 other events, 7.0 us)

commit v4 on v3

--- a/solution.py
+++ b/solution.py
@@ -79,10 +79,28 @@
     )(*first, *args)
 
 
-def widen_body(pred_ref, out_hbm, wide_ref, copies):
-    variables, nodes = pred_ref.shape[1:]
-    pad = jnp.zeros((wide_ref.shape[0] - variables, nodes), f32)
-    wide_ref[...] = jnp.concatenate([pred_ref[0].astype(f32), pad], axis=0).astype(bf16)
+def packed(a):
+    a = jnp.concatenate([a, jnp.zeros((7 * TILE - a.shape[0], a.shape[1]), f32)], axis=0)
+    tail = a[:, 3 * LANES :]
+    left = jnp.concatenate([tail[i * TILE : (i + 1) * TILE] for i in (0, 2, 4, 6)], axis=0)
+    right = jnp.concatenate(
+        [tail[i * TILE : (i + 1) * TILE] for i in (1, 3, 5)] + [jnp.zeros((TILE, LANES // 2), f32)], axis=0
+    )
+    return jnp.concatenate(
+        [a[:, j * LANES : (j + 1) * LANES] for j in range(3)] + [jnp.concatenate([left, right], axis=1)], axis=0
+    )
+
+
+def unpacked(a, variables):
+    last, half = a[21 * TILE :], LANES // 2
+    tail = jnp.concatenate(
+        [last[i // 2 * TILE : (i // 2 + 1) * TILE, (i % 2) * half : (i % 2 + 1) * half] for i in range(7)], axis=0
+    )
+    return jnp.concatenate([a[7 * j * TILE : 7 * (j + 1) * TILE] for j in range(3)] + [tail], axis=1)[0:variables]
+
+
+def pack_body(pred_ref, out_hbm, wide_ref, copies):
+    wide_ref[...] = packed(pred_ref[0].astype(f32)).astype(bf16).reshape(wide_ref.shape)
     for c in [copies.start(wide_ref, out_hbm.at[m]) for m in range(MEMBERS)]:
         c.wait()
 
@@ -143,11 +161,12 @@
     def sign(a):
         return jnp.where(a > 0.0, 1.0, jnp.where(a < 0.0, -1.0, 0.0))
 
-    own = own_ref[0].astype(f32)
+    own = packed(own_ref[0].astype(f32))
     pair_sum = jnp.zeros(own.shape, f32)
     for k in range(members):
-        pair_sum += sign(own - all_ref[k].astype(f32)[0:variables])
-    to_target = sign(own - target_ref[...].astype(f32))
+        pair_sum += sign(own - all_ref[k].astype(f32).reshape(own.shape))
+    to_target = sign(own_ref[0].astype(f32) - target_ref[...].astype(f32))
+    pair_sum = unpacked(pair_sum, variables)
     out_ref[...] = (lw_ref[...] * (to_target / members - coef_pair * pair_sum)).astype(bf16)
 
 
@@ -360,10 +379,10 @@
     )
 
     (spread_pred,) = call(
-        widen_body,
-        [sent((MEMBERS, rows, nodes), bf16)],
+        pack_body,
+        [sent((MEMBERS, 25, TILE, LANES), bf16)],
         (predictions,),
-        [vmem((rows, nodes), bf16)],
+        [vmem((25, TILE, LANES), bf16)],
         sems=MEMBERS,
     )
     every_pred = over_mem(spread_pred)

time: 141 us -> 140 us (level)
  no operation moved by 1% of the time
where the time goes in v4:
time: 140 us; the launch traced here: 139 us
  starting transfers between devices  68.4 us (49%)
  waiting for transfers between devices  26 us (19%)
  Pallas kernels  24.9 us (18%)
  blocking collectives  15.5 us (11%)
  local copies, waits for them, and re-layouts  2.78 us (2%)
    pallas_call x13, Pallas kernels, call(): pl.pallas_call(kernel, out_shape=out, in_specs=[pl.BlockSpec(memory_space...  24.9 us
    ppermute x6, starting transfers between devices, other_core(): return lax.ppermute(a, 'core', [(0, 1), (1, 0)])  24.7 us
    all_to_all x3, starting transfers between devices, over_mem(): return lax.all_to_all(a, 'mem', 0, 0, tiled=True)  16.1 us
    all_to_all x1, blocking collectives, on_device(): last = lax.all_to_all(last_out, ('mem', 'core'), 0, 0, tiled=True)  15.5 us
    all_to_all x1, starting transfers between devices, over_pairs(): return lax.all_to_all(a, PAIR, 0, 0, tiled=True)  14.7 us
    all_to_all x3, waiting for transfers between devices, over_mem(): return lax.all_to_all(a, 'mem', 0, 0, tiled=True)  7.1 us
    all_to_all x1, waiting for transfers between devices, on_device(): y_parts = lax.all_to_all(y_out, 'y', 0, 0, tiled=True)  5.09 us
    ppermute x6, waiting for transfers between devices, other_core(): return lax.ppermute(a, 'core', [(0, 1), (1, 0)])  5.03 us
  transfers between devices with their start and end apart: 14, of which 6 were waited for; matrix products, arithmetic and copies ran while one was open for 1% of the time, Pallas kernels for 10%

profile of v4, /device:TPU:1, one launch (start us, length us, event | category | flops | bytes accessed | tf_op | source)
XLA Modules:
  0.0 138.7 jit_solution(15868085482672863911)
XLA Ops:
  2.6 6.0 %all-to-all-start = ((bf16[8,25,16,128]{3,2,1,0:T(8,128)(2,1)}), bf16[8,25,16,128]{3,2,1,0:T(8,128)(2,1)S(1)}, u32[]{:S(2)}, u32[]{:S(2)}) async-start(bf16[8,25,16,128]{3,2,1,0:T(8,128)(2,1)} %shard_map.122), calls=%async_computation | async-start | bytes 1638400 | tf_op jit(solution)/shard_map/all_to_all | solution.py:349
  9.4 6.5 %collective-permute-start = (bf16[16,128]{1,0:T(8,128)(2,1)S(1)}, bf16[16,128]{1,0:T(8,128)(2,1)S(1)}, u32[]{:S(2)}, u32[]{:S(2)}) collective-permute-start(bf16[16,128]{1,0:T(8,128)(2,1)S(1)} %get-tuple-element.41), channel_id=1, source_target_pairs={{0,1},{1,0},{2,3},{3,2},{4,5},{5,4},{6,7},{7,6},{8,9},{9,8},{10,11... | collective-permute-start | bytes 12296 | tf_op jit(solution)/shard_map/ppermute | solution.py:341
  15.9 1.9 %collective-permute-start.3 = (bf16[64,1024]{1,0:T(8,128)(2,1)S(1)}, bf16[64,1024]{1,0:T(8,128)(2,1)S(1)}, u32[]{:S(2)}, u32[]{:S(2)}) collective-permute-start(bf16[64,1024]{1,0:T(8,128)(2,1)S(1)} %get-tuple-element.39), channel_id=1, source_target_pairs={{1,2},{2,1},{3,4},{4,3},{5,6},{6,5},{7,8},{8,7},{9,10},{10,9},{11,... | collective-permute-start | bytes 393224 | tf_op jit(solution)/shard_map/ppermute | solution.py:337
  20.5 14.7 %all-to-all-start.1 = ((bf16[32,16,128]{2,1,0:T(8,128)(2,1)}), bf16[32,16,128]{2,1,0:T(8,128)(2,1)S(1)}, u32[]{:S(2)}, u32[]{:S(2)}) async-start(bf16[32,16,128]{2,1,0:T(8,128)(2,1)} %shard_map.121), calls=%async_computation.1 | async-start | bytes 262144 | tf_op jit(solution)/shard_map/all_to_all | solution.py:345
  35.9 4.9 %collective-permute-start.1 = (bf16[100,448]{1,0:T(8,128)(2,1)S(1)}, bf16[100,448]{1,0:T(8,128)(2,1)S(1)}, u32[]{:S(2)}, u32[]{:S(2)}) collective-permute-start(bf16[100,448]{1,0:T(8,128)(2,1)S(1)} %shard_map.123.refs_4_), channel_id=1, source_target_pairs={{0,1},{1,0},{2,3},{3,2},{4,5},{5,4},{6,7},{7,6},{8,9},{9,8},{10,11... | collective-permute-start | bytes 268808 | tf_op jit(solution)/shard_map/ppermute | solution.py:341
  42.7 3.8 %all-to-all-done.1.refs_0_ = bf16[32,16,128]{2,1,0:T(8,128)(2,1)S(1)} async-done(((bf16[32,16,128]{2,1,0:T(8,128)(2,1)}), bf16[32,16,128]{2,1,0:T(8,128)(2,1)S(1)}, u32[]{:S(2)}, u32[]{:S(2)}) %all-to-all-start.1) | async-done | bytes 131104 | tf_op jit(solution)/shard_map/all_to_all | solution.py:345
  47.6 4.6 %all-to-all-start.2 = ((bf16[8,32,16,128]{3,2,1,0:T(8,128)(2,1)}), bf16[8,32,16,128]{3,2,1,0:T(8,128)(2,1)S(1)}, u32[]{:S(2)}, u32[]{:S(2)}) async-start(bf16[8,32,16,128]{3,2,1,0:T(8,128)(2,1)} %shard_map.125), calls=%async_computation.2 | async-start | bytes 2097152 | tf_op jit(solution)/shard_map/all_to_all | solution.py:349
  52.1 3.6 %shard_map.126 = (f32[448,128]{1,0:T(8,128)}, bf16[448,512]{1,0:T(8,128)(2,1)}, bf16[448,1536]{1,0:T(8,128)(2,1)}) custom-call(s32[1]{0:T(128)} %bitcast.refs_0_, bf16[448,1024]{1,0:T(8,128)(2,1)S(1)} %bitcast.9, bf16[64,1024]{1,0:T(8,128)(2,1)S(1)} %collective-permute-done.2.refs_2_, bf16[64,1024]{1,0:T(8,128)(2,1)S(1)} %collective-permute-done.3.refs_3_, ...), custom_call_target="tpu_custom_call" | custom-call | flops 528482304 | bytes 3760128 | tf_op jit(solution)/shard_map/pallas_call | solution.py:70
  55.8 6.1 %collective-permute-start.4 = (bf16[448,1536]{1,0:T(8,128)(2,1)}, bf16[448,1536]{1,0:T(8,128)(2,1)S(1)}, u32[]{:S(2)}, u32[]{:S(2)}) collective-permute-start(bf16[448,1536]{1,0:T(8,128)(2,1)} %get-tuple-element.24.refs_2_.refs_7_), channel_id=1, source_target_pairs={{0,1},{1,0},{2,3},{3,2},{4,5},{5,4},{6,7},{7,6},{8,9},{9,8},{10,11... | collective-permute-start | bytes 4128776 | tf_op jit(solution)/shard_map/ppermute | solution.py:341
  61.9 2.9 %collective-permute-done.4.refs_6_ = bf16[448,1536]{1,0:T(8,128)(2,1)S(1)} collective-permute-done((bf16[448,1536]{1,0:T(8,128)(2,1)}, bf16[448,1536]{1,0:T(8,128)(2,1)S(1)}, u32[]{:S(2)}, u32[]{:S(2)}) %collective-permute-start.4) | collective-permute-done | bytes 1376288 | tf_op jit(solution)/shard_map/ppermute | solution.py:341
  65.9 6.0 %shard_map.127 = (bf16[8,36,16,128]{3,2,1,0:T(8,128)(2,1)}, bf16[448,512]{1,0:T(8,128)(2,1)}, bf16[448,1024]{1,0:T(8,128)(2,1)}) custom-call(s32[1]{0:T(128)} %bitcast.refs_0_, bf16[8,32,16,128]{3,2,1,0:T(8,128)(2,1)S(1)} %all-to-all-done.2.refs_1_, bf16[448,1536]{1,0:T(8,128)(2,1)} %get-tuple-element.24.refs_2_.refs_7_, ...), custom_call_target="tpu_custom_call" | custom-call | flops 2348810240 | bytes 7199744 | tf_op jit(solution)/shard_map/pallas_call | solution.py:70
  71.9 5.6 %all-to-all-start.3 = ((bf16[8,36,16,128]{3,2,1,0:T(8,128)(2,1)}), bf16[8,36,16,128]{3,2,1,0:T(8,128)(2,1)S(1)}, u32[]{:S(2)}, u32[]{:S(2)}) async-start(bf16[8,36,16,128]{3,2,1,0:T(8,128)(2,1)} %get-tuple-element.33), calls=%async_computation.3 | async-start | bytes 2359296 | tf_op jit(solution)/shard_map/all_to_all | solution.py:349
  77.5 2.6 %collective-permute-start.5 = (bf16[448,1024]{1,0:T(8,128)(2,1)S(1)}, bf16[448,1024]{1,0:T(8,128)(2,1)S(1)}, u32[]{:S(2)}, u32[]{:S(2)}) collective-permute-start(bf16[448,1024]{1,0:T(8,128)(2,1)S(1)} %copy-done.11), channel_id=1, source_target_pairs={{0,1},{1,0},{2,3},{3,2},{4,5},{5,4},{6,7},{7,6},{8,9},{9,8},{10,11... | collective-permute-start | bytes 2752520 | tf_op jit(solution)/shard_map/ppermute | solution.py:341
  80.1 2.1 %collective-permute-done.5.refs_2_ = bf16[448,1024]{1,0:T(8,128)(2,1)S(1)} collective-permute-done((bf16[448,1024]{1,0:T(8,128)(2,1)S(1)}, bf16[448,1024]{1,0:T(8,128)(2,1)S(1)}, u32[]{:S(2)}, u32[]{:S(2)}) %collective-permute-start.5) | collective-permute-done | bytes 917536 | tf_op jit(solution)/shard_map/ppermute | solution.py:341
  82.1 4.6 %shard_map.128 = (bf16[448,1024]{1,0:T(8,128)(2,1)}, f32[128,1024]{1,0:T(8,128)}, bf16[64,1024]{1,0:T(8,128)(2,1)S(1)}, bf16[64,1024]{1,0:T(8,128)(2,1)S(1)}) custom-call(s32[1]{0:T(128)} %bitcast.refs_0_, bf16[8,32,16,128]{3,2,1,0:T(8,128)(2,1)S(1)} %all-to-all-done.2.refs_1_, bf16[448,1024]{1,0:T(8,128)(2,1)S(1)} %collective-permute-done.5.refs_2_, ...), custom_call_target="tpu_custom_call" | custom-call | flops 528482304 | bytes 6544896 | tf_op jit(solution)/shard_map/pallas_call | solution.py:70
  86.8 7.1 %all-to-all-done.3.refs_0_ = bf16[8,36,16,128]{3,2,1,0:T(8,128)(2,1)S(1)} async-done(((bf16[8,36,16,128]{3,2,1,0:T(8,128)(2,1)}), bf16[8,36,16,128]{3,2,1,0:T(8,128)(2,1)S(1)}, u32[]{:S(2)}, u32[]{:S(2)}) %all-to-all-start.3) | async-done | bytes 1179680 | tf_op jit(solution)/shard_map/all_to_all | solution.py:349
  94.7 3.4 %all-to-all-start.4 = ((bf16[8,8,16,128]{3,2,1,0:T(8,128)(2,1)}), bf16[8,8,16,128]{3,2,1,0:T(8,128)(2,1)S(1)}, u32[]{:S(2)}, u32[]{:S(2)}) async-start(bf16[8,8,16,128]{3,2,1,0:T(8,128)(2,1)} %shard_map.130), calls=%async_computation.4 | async-start | bytes 524288 | tf_op jit(solution)/shard_map/all_to_all | solution.py:465
  98.2 2.7 %collective-permute-start.6 = (bf16[64,1024]{1,0:T(8,128)(2,1)S(1)}, bf16[64,1024]{1,0:T(8,128)(2,1)S(1)}, u32[]{:S(2)}, u32[]{:S(2)}) collective-permute-start(bf16[64,1024]{1,0:T(8,128)(2,1)S(1)} %get-tuple-element.29), channel_id=1, source_target_pairs={{0,1},{1,0},{2,3},{3,2},{4,5},{5,4},{6,7},{7,6},{8,9},{9,8},{10,11... | collective-permute-start | bytes 393224 | tf_op jit(solution)/shard_map/ppermute | solution.py:341
  100.9 2.9 %collective-permute-start.7 = (bf16[64,1024]{1,0:T(8,128)(2,1)S(1)}, bf16[64,1024]{1,0:T(8,128)(2,1)S(1)}, u32[]{:S(2)}, u32[]{:S(2)}) collective-permute-start(bf16[64,1024]{1,0:T(8,128)(2,1)S(1)} %get-tuple-element.30), channel_id=1, source_target_pairs={{1,2},{2,1},{3,4},{4,3},{5,6},{6,5},{7,8},{8,7},{9,10},{10,9},{11,... | collective-permute-start | bytes 393224 | tf_op jit(solution)/shard_map/ppermute | solution.py:337
  103.8 5.0 %all-to-all-done.4.refs_0_ = bf16[8,8,16,128]{3,2,1,0:T(8,128)(2,1)S(1)} async-done(((bf16[8,8,16,128]{3,2,1,0:T(8,128)(2,1)}), bf16[8,8,16,128]{3,2,1,0:T(8,128)(2,1)S(1)}, u32[]{:S(2)}, u32[]{:S(2)}) %all-to-all-start.4) | async-done | bytes 262176 | tf_op jit(solution)/shard_map/all_to_all | solution.py:465
  109.4 4.7 %all-to-all-start.5 = ((bf16[4,5,16,128]{3,2,1,0:T(8,128)(2,1)}), bf16[4,5,16,128]{3,2,1,0:T(8,128)(2,1)S(1)}, u32[]{:S(2)}, u32[]{:S(2)}) async-start(bf16[4,5,16,128]{3,2,1,0:T(8,128)(2,1)} %shard_map.131), calls=%async_computation.5 | async-start | bytes 163840 | tf_op jit(solution)/shard_map/all_to_all | solution.py:473
  114.1 2.3 %shard_map.129 = bf16[1,448,1024]{2,1,0:T(8,128)(2,1)} custom-call(s32[1]{0:T(128)} %bitcast.refs_0_, bf16[64,1024]{1,0:T(8,128)(2,1)S(1)} %collective-permute-done.6.refs_1_, bf16[64,1024]{1,0:T(8,128)(2,1)S(1)} %collective-permute-done.7.refs_2_, bf16[448,1024]{1,0:T(8,128)(2,1)} %get-tuple-element.31.refs_3_, f32[128,1024]{1,0:T(8,128)} %get-tuple-element.32.refs_4_), custom_call_target="tpu_custom_call" | custom-call | bytes 2621440 | tf_op jit(solution)/shard_map/pallas_call | solution.py:70
  116.4 5.1 %all-to-all-done.5.refs_0_ = bf16[4,5,16,128]{3,2,1,0:T(8,128)(2,1)S(1)} async-done(((bf16[4,5,16,128]{3,2,1,0:T(8,128)(2,1)}), bf16[4,5,16,128]{3,2,1,0:T(8,128)(2,1)S(1)}, u32[]{:S(2)}, u32[]{:S(2)}) %all-to-all-start.5) | async-done | bytes 81952 | tf_op jit(solution)/shard_map/all_to_all | solution.py:473
  122.4 15.5 %all_to_all.35.refs_1_ = bf16[16,5,16,128]{3,2,1,0:T(8,128)(2,1)S(1)} all-to-all(bf16[16,5,16,128]{3,2,1,0:T(8,128)(2,1)} %shard_map.132), channel_id=1, replica_groups=mesh['mem'=8,'z'=8,'y'=4,'core'=2] {'mem','core'}, dimensions={0} | all-to-all | bytes 655360 | tf_op jit(solution)/shard_map/all_to_all | solution.py:490
  (48 shorter events, 13.1 us)
Async XLA Ops:
  1.5 14.3 %copy-start.4 = (bf16[1,448,1024]{2,1,0:T(8,128)(2,1)S(1)}, bf16[1,448,1024]{2,1,0:T(8,128)(2,1)}, u32[]{:S(2)}) copy-start(bf16[1,448,1024]{2,1,0:T(8,128)(2,1)} %param.10) | copy-start | bytes 2752516
  1.5 18.2 %copy-start.7 = (f32[448]{0:T(512)S(1)}, f32[448]{0:T(512)}, u32[]{:S(2)}) copy-start(f32[448]{0:T(512)} %param.13) | copy-start | bytes 5380
  1.5 18.2 %copy-start.8 = (s32[448]{0:T(512)S(1)}, s32[448]{0:T(512)}, u32[]{:S(2)}) copy-start(s32[448]{0:T(512)} %param.15) | copy-start | bytes 5380
  2.6 32.7 %copy-start.9 = (f32[100]{0:T(128)S(1)}, f32[100]{0:T(128)}, u32[]{:S(2)}) copy-start(f32[100]{0:T(128)} %param.14) | copy-start | bytes 1204
  2.6 32.8 %copy-start.1 = (bf16[1,100,448]{2,1,0:T(8,128)(2,1)S(1)}, bf16[1,100,448]{2,1,0:T(8,128)(2,1)}, u32[]{:S(2)}) copy-start(bf16[1,100,448]{2,1,0:T(8,128)(2,1)} %refs_1_.2) | copy-start | bytes 268804
  2.6 32.7 %copy-start.3 = (bf16[100,448]{1,0:T(8,128)(2,1)S(1)}, bf16[100,448]{1,0:T(8,128)(2,1)}, u32[]{:S(2)}) copy-start(bf16[100,448]{1,0:T(8,128)(2,1)} %refs_2_.1) | copy-start | bytes 268804
  2.6 17.9 %all-to-all-start = ((bf16[8,25,16,128]{3,2,1,0:T(8,128)(2,1)}), bf16[8,25,16,128]{3,2,1,0:T(8,128)(2,1)S(1)}, u32[]{:S(2)}, u32[]{:S(2)}) async-start(bf16[8,25,16,128]{3,2,1,0:T(8,128)(2,1)} %shard_map.122), calls=%async_computation | async-start | bytes 1638400 | tf_op jit(solution)/shard_map/all_to_all | solution.py:349
  8.6 32.2 %copy-start.5 = (s32[8,448]{1,0:T(8,128)S(1)}, s32[8,448]{1,0:T(8,128)}, u32[]{:S(2)}) copy-start(s32[8,448]{1,0:T(8,128)} %refs_0_.3) | copy-start | bytes 43012
  8.6 32.2 %copy-start.6 = (f32[8,448]{1,0:T(8,128)S(1)}, f32[8,448]{1,0:T(8,128)}, u32[]{:S(2)}) copy-start(f32[8,448]{1,0:T(8,128)} %refs_1_.3) | copy-start | bytes 43012
  9.4 10.4 %collective-permute-start = (bf16[16,128]{1,0:T(8,128)(2,1)S(1)}, bf16[16,128]{1,0:T(8,128)(2,1)S(1)}, u32[]{:S(2)}, u32[]{:S(2)}) collective-permute-start(bf16[16,128]{1,0:T(8,128)(2,1)S(1)} %get-tuple-element.41), channel_id=1, source_target_pairs={{0,1},{1,0},{2,3},{3,2},{4,5},{5,4},{6,7},{7,6},{8,9},{9,8},{10,11... | collective-permute-start | bytes 12296 | tf_op jit(solution)/shard_map/ppermute | solution.py:341
  15.9 26.8 %collective-permute-start.3 = (bf16[64,1024]{1,0:T(8,128)(2,1)S(1)}, bf16[64,1024]{1,0:T(8,128)(2,1)S(1)}, u32[]{:S(2)}, u32[]{:S(2)}) collective-permute-start(bf16[64,1024]{1,0:T(8,128)(2,1)S(1)} %get-tuple-element.39), channel_id=1, source_target_pairs={{1,2},{2,1},{3,4},{4,3},{5,6},{6,5},{7,8},{8,7},{9,10},{10,9},{11,... | collective-permute-start | bytes 393224 | tf_op jit(solution)/shard_map/ppermute | solution.py:337
  17.8 24.9 %collective-permute-start.2 = (bf16[64,1024]{1,0:T(8,128)(2,1)S(1)}, bf16[64,1024]{1,0:T(8,128)(2,1)S(1)}, u32[]{:S(2)}, u32[]{:S(2)}) collective-permute-start(bf16[64,1024]{1,0:T(8,128)(2,1)S(1)} %get-tuple-element.40), channel_id=1, source_target_pairs={{0,1},{1,0},{2,3},{3,2},{4,5},{5,4},{6,7},{7,6},{8,9},{9,8},{10,11... | collective-permute-start | bytes 393224 | tf_op jit(solution)/shard_map/ppermute | solution.py:341
  20.5 26.0 %all-to-all-start.1 = ((bf16[32,16,128]{2,1,0:T(8,128)(2,1)}), bf16[32,16,128]{2,1,0:T(8,128)(2,1)S(1)}, u32[]{:S(2)}, u32[]{:S(2)}) async-start(bf16[32,16,128]{2,1,0:T(8,128)(2,1)} %shard_map.121), calls=%async_computation.1 | async-start | bytes 262144 | tf_op jit(solution)/shard_map/all_to_all | solution.py:345
  35.9 11.6 %copy-start.2 = (bf16[100,448]{1,0:T(8,128)(2,1)}, bf16[100,448]{1,0:T(8,128)(2,1)S(1)}, u32[]{:S(2)}) copy-start(bf16[100,448]{1,0:T(8,128)(2,1)S(1)} %shard_map.123.refs_4_) | copy-start | bytes 268804
  35.9 6.8 %collective-permute-start.1 = (bf16[100,448]{1,0:T(8,128)(2,1)S(1)}, bf16[100,448]{1,0:T(8,128)(2,1)S(1)}, u32[]{:S(2)}, u32[]{:S(2)}) collective-permute-start(bf16[100,448]{1,0:T(8,128)(2,1)S(1)} %shard_map.123.refs_4_), channel_id=1, source_target_pairs={{0,1},{1,0},{2,3},{3,2},{4,5},{5,4},{6,7},{7,6},{8,9},{9,8},{10,11... | collective-permute-start | bytes 268808 | tf_op jit(solution)/shard_map/ppermute | solution.py:341
  47.6 17.3 %all-to-all-start.2 = ((bf16[8,32,16,128]{3,2,1,0:T(8,128)(2,1)}), bf16[8,32,16,128]{3,2,1,0:T(8,128)(2,1)S(1)}, u32[]{:S(2)}, u32[]{:S(2)}) async-start(bf16[8,32,16,128]{3,2,1,0:T(8,128)(2,1)} %shard_map.125), calls=%async_computation.2 | async-start | bytes 2097152 | tf_op jit(solution)/shard_map/all_to_all | solution.py:349
  55.8 9.0 %collective-permute-start.4 = (bf16[448,1536]{1,0:T(8,128)(2,1)}, bf16[448,1536]{1,0:T(8,128)(2,1)S(1)}, u32[]{:S(2)}, u32[]{:S(2)}) collective-permute-start(bf16[448,1536]{1,0:T(8,128)(2,1)} %get-tuple-element.24.refs_2_.refs_7_), channel_id=1, source_target_pairs={{0,1},{1,0},{2,3},{3,2},{4,5},{5,4},{6,7},{7,6},{8,9},{9,8},{10,11... | collective-permute-start | bytes 4128776 | tf_op jit(solution)/shard_map/ppermute | solution.py:341
  71.9 5.6 %copy-start.11 = (bf16[448,1024]{1,0:T(8,128)(2,1)S(1)}, bf16[448,1024]{1,0:T(8,128)(2,1)}, u32[]{:S(2)}) copy-start(bf16[448,1024]{1,0:T(8,128)(2,1)} %get-tuple-element.26) | copy-start | bytes 2752516
  71.9 21.9 %all-to-all-start.3 = ((bf16[8,36,16,128]{3,2,1,0:T(8,128)(2,1)}), bf16[8,36,16,128]{3,2,1,0:T(8,128)(2,1)S(1)}, u32[]{:S(2)}, u32[]{:S(2)}) async-start(bf16[8,36,16,128]{3,2,1,0:T(8,128)(2,1)} %get-tuple-element.33), calls=%async_computation.3 | async-start | bytes 2359296 | tf_op jit(solution)/shard_map/all_to_all | solution.py:349
  77.5 4.6 %collective-permute-start.5 = (bf16[448,1024]{1,0:T(8,128)(2,1)S(1)}, bf16[448,1024]{1,0:T(8,128)(2,1)S(1)}, u32[]{:S(2)}, u32[]{:S(2)}) collective-permute-start(bf16[448,1024]{1,0:T(8,128)(2,1)S(1)} %copy-done.11), channel_id=1, source_target_pairs={{0,1},{1,0},{2,3},{3,2},{4,5},{5,4},{6,7},{7,6},{8,9},{9,8},{10,11... | collective-permute-start | bytes 2752520 | tf_op jit(solution)/shard_map/ppermute | solution.py:341
  94.7 14.0 %all-to-all-start.4 = ((bf16[8,8,16,128]{3,2,1,0:T(8,128)(2,1)}), bf16[8,8,16,128]{3,2,1,0:T(8,128)(2,1)S(1)}, u32[]{:S(2)}, u32[]{:S(2)}) async-start(bf16[8,8,16,128]{3,2,1,0:T(8,128)(2,1)} %shard_map.130), calls=%async_computation.4 | async-start | bytes 524288 | tf_op jit(solution)/shard_map/all_to_all | solution.py:465
  98.2 5.6 %collective-permute-start.6 = (bf16[64,1024]{1,0:T(8,128)(2,1)S(1)}, bf16[64,1024]{1,0:T(8,128)(2,1)S(1)}, u32[]{:S(2)}, u32[]{:S(2)}) collective-permute-start(bf16[64,1024]{1,0:T(8,128)(2,1)S(1)} %get-tuple-element.29), channel_id=1, source_target_pairs={{0,1},{1,0},{2,3},{3,2},{4,5},{5,4},{6,7},{7,6},{8,9},{9,8},{10,11... | collective-permute-start | bytes 393224 | tf_op jit(solution)/shard_map/ppermute | solution.py:341
  100.9 13.2 %collective-permute-start.7 = (bf16[64,1024]{1,0:T(8,128)(2,1)S(1)}, bf16[64,1024]{1,0:T(8,128)(2,1)S(1)}, u32[]{:S(2)}, u32[]{:S(2)}) collective-permute-start(bf16[64,1024]{1,0:T(8,128)(2,1)S(1)} %get-tuple-element.30), channel_id=1, source_target_pairs={{1,2},{2,1},{3,4},{4,3},{5,6},{6,5},{7,8},{8,7},{9,10},{10,9},{11,... | collective-permute-start | bytes 393224 | tf_op jit(solution)/shard_map/ppermute | solution.py:337
  109.4 12.1 %all-to-all-start.5 = ((bf16[4,5,16,128]{3,2,1,0:T(8,128)(2,1)}), bf16[4,5,16,128]{3,2,1,0:T(8,128)(2,1)S(1)}, u32[]{:S(2)}, u32[]{:S(2)}) async-start(bf16[4,5,16,128]{3,2,1,0:T(8,128)(2,1)} %shard_map.131), calls=%async_computation.5 | async-start | bytes 163840 | tf_op jit(solution)/shard_map/all_to_all | solution.py:473
  (3 other events, 6.8 us)

commit v5 on v4

--- a/solution.py
+++ b/solution.py
@@ -50,6 +50,10 @@
 
 def sent(dims, dtype):
     return pltpu.HBM(dims, dtype)
+
+
+def staged(dims, dtype):
+    return pltpu.VMEM(dims, dtype)
 
 
 def call(body, out, args, scratch=(), core=None, sems=0, hbm_args=(), flops=0, trans=0, mib=24):
@@ -80,23 +84,21 @@
 
 
 def packed(a):
-    a = jnp.concatenate([a, jnp.zeros((7 * TILE - a.shape[0], a.shape[1]), f32)], axis=0)
+    rows, half = a.shape[0], a.shape[0] // 2
     tail = a[:, 3 * LANES :]
-    left = jnp.concatenate([tail[i * TILE : (i + 1) * TILE] for i in (0, 2, 4, 6)], axis=0)
-    right = jnp.concatenate(
-        [tail[i * TILE : (i + 1) * TILE] for i in (1, 3, 5)] + [jnp.zeros((TILE, LANES // 2), f32)], axis=0
-    )
-    return jnp.concatenate(
-        [a[:, j * LANES : (j + 1) * LANES] for j in range(3)] + [jnp.concatenate([left, right], axis=1)], axis=0
-    )
-
-
-def unpacked(a, variables):
-    last, half = a[21 * TILE :], LANES // 2
-    tail = jnp.concatenate(
-        [last[i // 2 * TILE : (i // 2 + 1) * TILE, (i % 2) * half : (i % 2 + 1) * half] for i in range(7)], axis=0
-    )
-    return jnp.concatenate([a[7 * j * TILE : 7 * (j + 1) * TILE] for j in range(3)] + [tail], axis=1)[0:variables]
+    parts = [a[:, j * LANES : (j + 1) * LANES] for j in range(3)]
+    parts.append(jnp.concatenate([tail[0:half], tail[half:]], axis=1))
+    fill = -(3 * rows + half) % TILE
+    if fill:
+        parts.append(jnp.zeros((fill, LANES), f32))
+    return jnp.concatenate(parts, axis=0)
+
+
+def unpacked(a, rows):
+    half = rows // 2
+    last = a[3 * rows : 3 * rows + half]
+    tail = jnp.concatenate([last[:, 0 : LANES // 2], last[:, LANES // 2 :]], axis=0)
+    return jnp.concatenate([a[j * rows : (j + 1) * rows] for j in range(3)] + [tail], axis=1)
 
 
 def pack_body(pred_ref, out_hbm, wide_ref, copies):
@@ -106,7 +108,9 @@
 
 
 def tile_body(pick_ref, own_ref, got_ref, out_hbm, out_ref, copies):
-    tile = jnp.where(pick_ref[0] == 1, own_ref[...].astype(f32), got_ref[...].astype(f32)).astype(bf16)
+    at = pl.ds(pl.multiple_of(pick_ref[1] * LANES, LANES), LANES)
+    own, got = own_ref[:, at].astype(f32), got_ref[K:, at].astype(f32)
+    tile = jnp.where(pick_ref[0] == 1, own, got).astype(bf16)
     out_ref[...] = jnp.broadcast_to(tile[None], out_ref.shape)
     copies.start(out_ref, out_hbm).wait()
 
@@ -123,7 +127,7 @@
 
 
 def norm_body(
-    core_ref, own_ref, near_ref, far_ref, at_hbm, rstd_hbm, keep_hbm, send_hbm, at_ref, li_ref, normed_ref, rstd_ref, copies
+    core_ref, own_ref, near_ref, far_ref, at_hbm, rstd_hbm, keep_hbm, normed_ref, send_hbm, at_ref, li_ref, rstd_ref, copies
 ):
     copies.start(at_hbm, at_ref).wait()
     core = core_ref[0]
@@ -131,7 +135,7 @@
     half = width // 2
     near_at = pl.multiple_of((1 - core) * (K + nodes), K)
     far_at = pl.multiple_of(core * (K + nodes), K)
-    agg = dot(at_ref[pl.ds(near_at, K), :], near_ref[...], 0, 0)
+    agg = dot(at_ref[pl.ds(near_at, K), :], near_ref[0:K, :], 0, 0)
     agg += dot(at_ref[K : K + nodes, :], own_ref[...], 0, 0)
     agg += dot(at_ref[pl.ds(far_at, K), :], far_ref[...], 0, 0)
     li = own_ref[...].astype(f32) + agg
@@ -185,8 +189,8 @@
 
 
 def main_body(
-    core_ref, wg_ref, own_hbm, keep_hbm, po_hbm, wd_hbm, got_hbm, pp_hbm, send_hbm, pre_hbm, ng_hbm,
-    no_ref, keep_ref, po_ref, wd_ref, got_ref, pp_ref, w_ref, lo_ref, pre_ref, parts_ref, ng_ref, copies,
+    core_ref, wg_ref, no_ref, keep_hbm, po_hbm, wd_hbm, got_hbm, pp_hbm, send_hbm, pre_hbm, ng_hbm,
+    keep_ref, po_ref, wd_ref, got_ref, pp_ref, w_ref, lo_ref, pre_ref, parts_ref, ng_ref, copies,
 ):
     core = core_ref[0]
     nodes, width = no_ref.shape
@@ -194,8 +198,7 @@
     cols = half // LANES
     pairs = parts_ref.shape[1] - cols
     loads = [
-        [copies.start(own_hbm.at[:, pl.ds(0, width)], no_ref), copies.start(keep_hbm, keep_ref),
-         copies.start(po_hbm, po_ref), copies.start(wd_hbm, wd_ref)],
+        [copies.start(po_hbm, po_ref), copies.start(wd_hbm, wd_ref), copies.start(keep_hbm, keep_ref)],
         [copies.start(got_hbm, got_ref), copies.start(pp_hbm, pp_ref)],
     ]
     fill_weight(wg_ref, w_ref)
@@ -365,40 +368,39 @@
     vmem = pltpu.VMEM
 
     row_half, col_block = member // cols, member % cols
-    tile_own = lax.dynamic_slice(w_node, (0, core * half + col_block * LANES), (TILE, LANES))
-    tile_out = lax.dynamic_slice(w_node, (0, (1 - core) * half + col_block * LANES), (TILE, LANES))
-    tile_got = other_core(tile_out)
-    own_half = (core == row_half).astype(jnp.int32).reshape(1)
+    edge = lax.dynamic_slice(own, ((1 - core) * (nodes - K), 0), (K, width))
+    near = other_core(jnp.concatenate([edge, w_node]))
+    pick = jnp.stack([(core == row_half).astype(jnp.int32), (core * cols + col_block).astype(jnp.int32)])
     (tiles,) = call(
         tile_body,
         [sent((pairs, TILE, LANES), bf16)],
-        (tile_own, tile_got),
+        (w_node, near),
         [vmem((pairs, TILE, LANES), bf16)],
-        core=own_half,
+        core=pick,
         sems=1,
     )
 
+    pred_tiles = -(-variables * nodes // (TILE * LANES))
     (spread_pred,) = call(
         pack_body,
-        [sent((MEMBERS, 25, TILE, LANES), bf16)],
+        [sent((MEMBERS, pred_tiles, TILE, LANES), bf16)],
         (predictions,),
-        [vmem((25, TILE, LANES), bf16)],
+        [vmem((pred_tiles, TILE, LANES), bf16)],
         sems=MEMBERS,
     )
     every_pred = over_mem(spread_pred)
-    near = other_core(lax.dynamic_slice(own, ((1 - core) * (nodes - K), 0), (K, width)))
     far = other_pair(lax.dynamic_slice(own, (core * (nodes - K), 0), (K, width)))
     (at,) = call(
         edges_body, [sent((nodes + 2 * K, nodes), bf16)], (sources, edge_weight),
         [vmem((nodes + 2 * K, nodes), bf16)], sems=1,
     )
     shards = over_pairs(after(tiles, every_pred))
-    rstd, keep, send = call(
+    rstd, keep, normed, send = call(
         norm_body,
-        [sent((nodes, LANES), f32), sent((nodes, half), bf16), sent((nodes, width + half), bf16)],
+        [sent((nodes, LANES), f32), sent((nodes, half), bf16), staged((nodes, width), bf16),
+         sent((nodes, width + half), bf16)],
         (after(own, shards), near, far),
-        [vmem((nodes + 2 * K, nodes), bf16), vmem((nodes, width), bf16), vmem((nodes, width), bf16),
-         vmem((nodes, LANES), f32)],
+        [vmem((nodes + 2 * K, nodes), bf16), vmem((nodes, width), bf16), vmem((nodes, LANES), f32)],
         core=core_arg,
         hbm_args=(at,),
         sems=5,
@@ -417,7 +419,7 @@
     (spread,) = call(
         share_body,
         [sent((MEMBERS, pairs, TILE, LANES), bf16)],
-        (after(shards, pred_got, near, far, at),),
+        (after(shards, pred_got, far, at),),
         sems=MEMBERS,
     )
     weight = over_mem(spread)
@@ -427,12 +429,12 @@
     parts, pre_grad, ng_send = call(
         main_body,
         [sent(part_shape, bf16), sent((nodes, half), bf16), sent((nodes, width), bf16)],
-        (weight,),
-        [vmem((nodes, width), bf16), vmem((nodes, half), bf16), vmem((variables, nodes), bf16),
+        (weight, normed),
+        [vmem((nodes, half), bf16), vmem((variables, nodes), bf16),
          vmem((variables, width), bf16), vmem((nodes, width + half), bf16), vmem((variables, nodes), bf16), weight_shape, vmem((2 * nodes, half), bf16),
          vmem((2 * nodes, half), bf16), vmem(part_shape, bf16), vmem((nodes, width), bf16)],
         core=core_arg,
-        hbm_args=(send, keep, pred_grad, dec_t, got, pred_got),
+        hbm_args=(keep, pred_grad, dec_t, got, pred_got),
         sems=16,
         flops=5 * 2 * nodes * width * half,
         trans=4 * nodes * half,

time: 140 us -> 138 us (0.986)
  local copies, waits for them, and re-layouts: 2.78 us -> 0.98 us
    ppermute x6 -> x5, starting transfers between devices: 24.7 us -> 18.9 us  [other_core(): return lax.ppermute(a, 'core', [(0, 1), (1, 0)])]
    ppermute x2, starting transfers between devices: 4.78 us -> 8.83 us  [other_pair(): return lax.ppermute(a, GRID, pairs)]
    ppermute x6 -> x5, waiting for transfers between devices: 5.03 us -> 6.21 us  [other_core(): return lax.ppermute(a, 'core', [(0, 1), (1, 0)])]
  transfers between devices with their start and end apart: 14 -> 13, of which waited for: 6 -> 7; matrix products, arithmetic and copies ran while one was open for 1% -> 0% of each run, Pallas kernels for 10% -> 11%
where the time goes in v5:
time: 138 us; the launch traced here: 137 us
  starting transfers between devices  68.7 us (50%)
  waiting for transfers between devices  25.8 us (19%)
  Pallas kernels  25.2 us (18%)
  blocking collectives  15.5 us (11%)
    pallas_call x13, Pallas kernels, call(): pl.pallas_call(kernel, out_shape=out, in_specs=[pl.BlockSpec(memory_space...  25.2 us
    ppermute x5, starting transfers between devices, other_core(): return lax.ppermute(a, 'core', [(0, 1), (1, 0)])  18.9 us
    all_to_all x1, starting transfers between devices, over_pairs(): return lax.all_to_all(a, PAIR, 0, 0, tiled=True)  15.9 us
    all_to_all x3, starting transfers between devices, over_mem(): return lax.all_to_all(a, 'mem', 0, 0, tiled=True)  15.9 us
    all_to_all x1, blocking collectives, on_device(): last = lax.all_to_all(last_out, ('mem', 'core'), 0, 0, tiled=True)  15.5 us
    ppermute x2, starting transfers between devices, other_pair(): return lax.ppermute(a, GRID, pairs)  8.83 us
    all_to_all x3, waiting for transfers between devices, over_mem(): return lax.all_to_all(a, 'mem', 0, 0, tiled=True)  6.72 us
    ppermute x5, waiting for transfers between devices, other_core(): return lax.ppermute(a, 'core', [(0, 1), (1, 0)])  6.21 us
  transfers between devices with their start and end apart: 13, of which 7 were waited for; matrix products, arithmetic and copies ran while one was open for 0% of the time, Pallas kernels for 11%

profile of v5, /device:TPU:1, one launch (start us, length us, event | category | flops | bytes accessed | tf_op | source)
XLA Modules:
  0.0 137.5 jit_solution(14103315229082416830)
XLA Ops:
  2.6 6.0 %all-to-all-start = ((bf16[8,22,16,128]{3,2,1,0:T(8,128)(2,1)}), bf16[8,22,16,128]{3,2,1,0:T(8,128)(2,1)S(1)}, u32[]{:S(2)}, u32[]{:S(2)}) async-start(bf16[8,22,16,128]{3,2,1,0:T(8,128)(2,1)} %shard_map.122), calls=%async_computation | async-start | bytes 1441792 | tf_op jit(solution)/shard_map/all_to_all | solution.py:352
  8.7 5.1 %collective-permute-start.2 = (bf16[64,1024]{1,0:T(8,128)(2,1)S(1)}, bf16[64,1024]{1,0:T(8,128)(2,1)S(1)}, u32[]{:S(2)}, u32[]{:S(2)}) collective-permute-start(bf16[64,1024]{1,0:T(8,128)(2,1)S(1)} %get-tuple-element.41), channel_id=1, source_target_pairs={{1,2},{2,1},{3,4},{4,3},{5,6},{6,5},{7,8},{8,7},{9,10},{10,9},{11,... | collective-permute-start | bytes 393224 | tf_op jit(solution)/shard_map/ppermute | solution.py:340
  13.7 2.1 %collective-permute-start = (bf16[80,1024]{1,0:T(8,128)(2,1)S(1)}, bf16[80,1024]{1,0:T(8,128)(2,1)S(1)}, u32[]{:S(2)}, u32[]{:S(2)}) collective-permute-start(bf16[80,1024]{1,0:T(8,128)(2,1)S(1)} %pad_maximum_fusion), channel_id=1, source_target_pairs={{0,1},{1,0},{2,3},{3,2},{4,5},{5,4},{6,7},{7,6},{8,9},{9,8},{10,11... | collective-permute-start | bytes 491528 | tf_op jit(solution)/shard_map/ppermute | solution.py:344
  18.3 15.9 %all-to-all-start.1 = ((bf16[32,16,128]{2,1,0:T(8,128)(2,1)}), bf16[32,16,128]{2,1,0:T(8,128)(2,1)S(1)}, u32[]{:S(2)}, u32[]{:S(2)}) async-start(bf16[32,16,128]{2,1,0:T(8,128)(2,1)} %shard_map.121), calls=%async_computation.1 | async-start | bytes 262144 | tf_op jit(solution)/shard_map/all_to_all | solution.py:348
  34.9 5.0 %collective-permute-start.1 = (bf16[100,448]{1,0:T(8,128)(2,1)S(1)}, bf16[100,448]{1,0:T(8,128)(2,1)S(1)}, u32[]{:S(2)}, u32[]{:S(2)}) collective-permute-start(bf16[100,448]{1,0:T(8,128)(2,1)S(1)} %shard_map.123.refs_4_), channel_id=1, source_target_pairs={{0,1},{1,0},{2,3},{3,2},{4,5},{5,4},{6,7},{7,6},{8,9},{9,8},{10,11... | collective-permute-start | bytes 268808 | tf_op jit(solution)/shard_map/ppermute | solution.py:344
  41.7 3.8 %all-to-all-done.1.refs_0_ = bf16[32,16,128]{2,1,0:T(8,128)(2,1)S(1)} async-done(((bf16[32,16,128]{2,1,0:T(8,128)(2,1)}), bf16[32,16,128]{2,1,0:T(8,128)(2,1)S(1)}, u32[]{:S(2)}, u32[]{:S(2)}) %all-to-all-start.1) | async-done | bytes 131104 | tf_op jit(solution)/shard_map/all_to_all | solution.py:348
  46.7 4.3 %all-to-all-start.2 = ((bf16[8,32,16,128]{3,2,1,0:T(8,128)(2,1)}), bf16[8,32,16,128]{3,2,1,0:T(8,128)(2,1)S(1)}, u32[]{:S(2)}, u32[]{:S(2)}) async-start(bf16[8,32,16,128]{3,2,1,0:T(8,128)(2,1)} %shard_map.125), calls=%async_computation.2 | async-start | bytes 2097152 | tf_op jit(solution)/shard_map/all_to_all | solution.py:352
  50.9 3.7 %shard_map.126 = (f32[448,128]{1,0:T(8,128)}, bf16[448,512]{1,0:T(8,128)(2,1)}, bf16[448,1024]{1,0:T(8,128)(2,1)S(1)}, bf16[448,1536]{1,0:T(8,128)(2,1)}) custom-call(s32[1]{0:T(128)} %bitcast.refs_0_, bf16[448,1024]{1,0:T(8,128)(2,1)S(1)} %bitcast.10, bf16[80,1024]{1,0:T(8,128)(2,1)S(1)} %collective-permute-done.refs_2_, ...), custom_call_target="tpu_custom_call" | custom-call | flops 528482304 | bytes 4710400 | tf_op jit(solution)/shard_map/pallas_call | solution.py:74
  54.6 6.2 %collective-permute-start.3 = (bf16[448,1536]{1,0:T(8,128)(2,1)}, bf16[448,1536]{1,0:T(8,128)(2,1)}, u32[]{:S(2)}, u32[]{:S(2)}) collective-permute-start(bf16[448,1536]{1,0:T(8,128)(2,1)} %get-tuple-element.27.refs_7_), channel_id=1, source_target_pairs={{0,1},{1,0},{2,3},{3,2},{4,5},{5,4},{6,7},{7,6},{8,9},{9,8},{10,11... | collective-permute-start | bytes 4128776 | tf_op jit(solution)/shard_map/ppermute | solution.py:344
  60.8 3.1 %collective-permute-done.3.refs_6_ = bf16[448,1536]{1,0:T(8,128)(2,1)} collective-permute-done((bf16[448,1536]{1,0:T(8,128)(2,1)}, bf16[448,1536]{1,0:T(8,128)(2,1)}, u32[]{:S(2)}, u32[]{:S(2)}) %collective-permute-start.3) | collective-permute-done | bytes 1376288 | tf_op jit(solution)/shard_map/ppermute | solution.py:344
  63.9 5.8 %shard_map.127 = (bf16[8,36,16,128]{3,2,1,0:T(8,128)(2,1)}, bf16[448,512]{1,0:T(8,128)(2,1)}, bf16[448,1024]{1,0:T(8,128)(2,1)}) custom-call(s32[1]{0:T(128)} %bitcast.refs_0_, bf16[8,32,16,128]{3,2,1,0:T(8,128)(2,1)S(1)} %all-to-all-done.2.refs_1_, bf16[448,1024]{1,0:T(8,128)(2,1)S(1)} %get-tuple-element.25.refs_2_, ...), custom_call_target="tpu_custom_call" | custom-call | flops 2348810240 | bytes 6740992 | tf_op jit(solution)/shard_map/pallas_call | solution.py:74
  69.7 5.6 %all-to-all-start.3 = ((bf16[8,36,16,128]{3,2,1,0:T(8,128)(2,1)}), bf16[8,36,16,128]{3,2,1,0:T(8,128)(2,1)S(1)}, u32[]{:S(2)}, u32[]{:S(2)}) async-start(bf16[8,36,16,128]{3,2,1,0:T(8,128)(2,1)} %get-tuple-element.35), calls=%async_computation.3 | async-start | bytes 2359296 | tf_op jit(solution)/shard_map/all_to_all | solution.py:352
  75.3 2.9 %collective-permute-start.4 = (bf16[448,1024]{1,0:T(8,128)(2,1)S(1)}, bf16[448,1024]{1,0:T(8,128)(2,1)S(1)}, u32[]{:S(2)}, u32[]{:S(2)}) collective-permute-start(bf16[448,1024]{1,0:T(8,128)(2,1)S(1)} %copy-done.11), channel_id=1, source_target_pairs={{0,1},{1,0},{2,3},{3,2},{4,5},{5,4},{6,7},{7,6},{8,9},{9,8},{10,11... | collective-permute-start | bytes 2752520 | tf_op jit(solution)/shard_map/ppermute | solution.py:344
  78.2 2.1 %collective-permute-done.4.refs_2_ = bf16[448,1024]{1,0:T(8,128)(2,1)S(1)} collective-permute-done((bf16[448,1024]{1,0:T(8,128)(2,1)S(1)}, bf16[448,1024]{1,0:T(8,128)(2,1)S(1)}, u32[]{:S(2)}, u32[]{:S(2)}) %collective-permute-start.4) | collective-permute-done | bytes 917536 | tf_op jit(solution)/shard_map/ppermute | solution.py:344
  80.3 4.6 %shard_map.128 = (bf16[448,1024]{1,0:T(8,128)(2,1)}, f32[128,1024]{1,0:T(8,128)}, bf16[64,1024]{1,0:T(8,128)(2,1)S(1)}, bf16[64,1024]{1,0:T(8,128)(2,1)S(1)}) custom-call(s32[1]{0:T(128)} %bitcast.refs_0_, bf16[8,32,16,128]{3,2,1,0:T(8,128)(2,1)S(1)} %all-to-all-done.2.refs_1_, bf16[448,1024]{1,0:T(8,128)(2,1)S(1)} %collective-permute-done.4.refs_2_, ...), custom_call_target="tpu_custom_call" | custom-call | flops 528482304 | bytes 6544896 | tf_op jit(solution)/shard_map/pallas_call | solution.py:74
  84.9 6.7 %all-to-all-done.3.refs_0_ = bf16[8,36,16,128]{3,2,1,0:T(8,128)(2,1)S(1)} async-done(((bf16[8,36,16,128]{3,2,1,0:T(8,128)(2,1)}), bf16[8,36,16,128]{3,2,1,0:T(8,128)(2,1)S(1)}, u32[]{:S(2)}, u32[]{:S(2)}) %all-to-all-start.3) | async-done | bytes 1179680 | tf_op jit(solution)/shard_map/all_to_all | solution.py:352
  92.5 3.4 %all-to-all-start.4 = ((bf16[8,8,16,128]{3,2,1,0:T(8,128)(2,1)}), bf16[8,8,16,128]{3,2,1,0:T(8,128)(2,1)S(1)}, u32[]{:S(2)}, u32[]{:S(2)}) async-start(bf16[8,8,16,128]{3,2,1,0:T(8,128)(2,1)} %shard_map.130), calls=%async_computation.4 | async-start | bytes 524288 | tf_op jit(solution)/shard_map/all_to_all | solution.py:467
  95.9 2.8 %collective-permute-start.5 = (bf16[64,1024]{1,0:T(8,128)(2,1)S(1)}, bf16[64,1024]{1,0:T(8,128)(2,1)S(1)}, u32[]{:S(2)}, u32[]{:S(2)}) collective-permute-start(bf16[64,1024]{1,0:T(8,128)(2,1)S(1)} %get-tuple-element.31), channel_id=1, source_target_pairs={{0,1},{1,0},{2,3},{3,2},{4,5},{5,4},{6,7},{7,6},{8,9},{9,8},{10,11... | collective-permute-start | bytes 393224 | tf_op jit(solution)/shard_map/ppermute | solution.py:344
  98.7 3.8 %collective-permute-start.6 = (bf16[64,1024]{1,0:T(8,128)(2,1)S(1)}, bf16[64,1024]{1,0:T(8,128)(2,1)S(1)}, u32[]{:S(2)}, u32[]{:S(2)}) collective-permute-start(bf16[64,1024]{1,0:T(8,128)(2,1)S(1)} %get-tuple-element.32), channel_id=1, source_target_pairs={{1,2},{2,1},{3,4},{4,3},{5,6},{6,5},{7,8},{8,7},{9,10},{10,9},{11,... | collective-permute-start | bytes 393224 | tf_op jit(solution)/shard_map/ppermute | solution.py:340
  102.5 4.0 %all-to-all-done.4.refs_0_ = bf16[8,8,16,128]{3,2,1,0:T(8,128)(2,1)S(1)} async-done(((bf16[8,8,16,128]{3,2,1,0:T(8,128)(2,1)}), bf16[8,8,16,128]{3,2,1,0:T(8,128)(2,1)S(1)}, u32[]{:S(2)}, u32[]{:S(2)}) %all-to-all-start.4) | async-done | bytes 262176 | tf_op jit(solution)/shard_map/all_to_all | solution.py:467
  107.1 5.7 %all-to-all-start.5 = ((bf16[4,5,16,128]{3,2,1,0:T(8,128)(2,1)}), bf16[4,5,16,128]{3,2,1,0:T(8,128)(2,1)S(1)}, u32[]{:S(2)}, u32[]{:S(2)}) async-start(bf16[4,5,16,128]{3,2,1,0:T(8,128)(2,1)} %shard_map.131), calls=%async_computation.5 | async-start | bytes 163840 | tf_op jit(solution)/shard_map/all_to_all | solution.py:475
  112.8 2.3 %shard_map.129 = bf16[1,448,1024]{2,1,0:T(8,128)(2,1)} custom-call(s32[1]{0:T(128)} %bitcast.refs_0_, bf16[64,1024]{1,0:T(8,128)(2,1)S(1)} %collective-permute-done.5.refs_1_, bf16[64,1024]{1,0:T(8,128)(2,1)S(1)} %collective-permute-done.6.refs_2_, bf16[448,1024]{1,0:T(8,128)(2,1)} %get-tuple-element.33.refs_3_, f32[128,1024]{1,0:T(8,128)} %get-tuple-element.34.refs_4_), custom_call_target="tpu_custom_call" | custom-call | bytes 2621440 | tf_op jit(solution)/shard_map/pallas_call | solution.py:74
  115.2 5.1 %all-to-all-done.5.refs_0_ = bf16[4,5,16,128]{3,2,1,0:T(8,128)(2,1)S(1)} async-done(((bf16[4,5,16,128]{3,2,1,0:T(8,128)(2,1)}), bf16[4,5,16,128]{3,2,1,0:T(8,128)(2,1)S(1)}, u32[]{:S(2)}, u32[]{:S(2)}) %all-to-all-start.5) | async-done | bytes 81952 | tf_op jit(solution)/shard_map/all_to_all | solution.py:475
  121.1 15.5 %all_to_all.35.refs_1_ = bf16[16,5,16,128]{3,2,1,0:T(8,128)(2,1)S(1)} all-to-all(bf16[16,5,16,128]{3,2,1,0:T(8,128)(2,1)} %shard_map.132), channel_id=1, replica_groups=mesh['mem'=8,'z'=8,'y'=4,'core'=2] {'mem','core'}, dimensions={0} | all-to-all | bytes 655360 | tf_op jit(solution)/shard_map/all_to_all | solution.py:492
  (47 shorter events, 11.1 us)
Async XLA Ops:
  1.5 7.1 %copy-start.5 = (bf16[1,448,1024]{2,1,0:T(8,128)(2,1)S(1)}, bf16[1,448,1024]{2,1,0:T(8,128)(2,1)}, u32[]{:S(2)}) copy-start(bf16[1,448,1024]{2,1,0:T(8,128)(2,1)} %param.10) | copy-start | bytes 2752516
  1.5 12.2 %copy-start.3 = (bf16[16,1024]{1,0:T(8,128)(2,1)S(1)}, bf16[16,1024]{1,0:T(8,128)(2,1)}, u32[]{:S(2)}) copy-start(bf16[16,1024]{1,0:T(8,128)(2,1)} %refs_1_.3) | copy-start | bytes 98308
  1.5 14.3 %copy-start.8 = (f32[448]{0:T(512)S(1)}, f32[448]{0:T(512)}, u32[]{:S(2)}) copy-start(f32[448]{0:T(512)} %param.13) | copy-start | bytes 5380
  1.5 14.3 %copy-start.9 = (s32[448]{0:T(512)S(1)}, s32[448]{0:T(512)}, u32[]{:S(2)}) copy-start(s32[448]{0:T(512)} %param.15) | copy-start | bytes 5380
  2.5 31.7 %copy-start.10 = (f32[100]{0:T(128)S(1)}, f32[100]{0:T(128)}, u32[]{:S(2)}) copy-start(f32[100]{0:T(128)} %param.14) | copy-start | bytes 1204
  2.6 31.8 %copy-start.1 = (bf16[1,100,448]{2,1,0:T(8,128)(2,1)S(1)}, bf16[1,100,448]{2,1,0:T(8,128)(2,1)}, u32[]{:S(2)}) copy-start(bf16[1,100,448]{2,1,0:T(8,128)(2,1)} %refs_1_.4) | copy-start | bytes 268804
  2.6 31.8 %copy-start.4 = (bf16[100,448]{1,0:T(8,128)(2,1)S(1)}, bf16[100,448]{1,0:T(8,128)(2,1)}, u32[]{:S(2)}) copy-start(bf16[100,448]{1,0:T(8,128)(2,1)} %refs_2_.1) | copy-start | bytes 268804
  2.6 15.7 %all-to-all-start = ((bf16[8,22,16,128]{3,2,1,0:T(8,128)(2,1)}), bf16[8,22,16,128]{3,2,1,0:T(8,128)(2,1)S(1)}, u32[]{:S(2)}, u32[]{:S(2)}) async-start(bf16[8,22,16,128]{3,2,1,0:T(8,128)(2,1)} %shard_map.122), calls=%async_computation | async-start | bytes 1441792 | tf_op jit(solution)/shard_map/all_to_all | solution.py:352
  8.6 31.3 %copy-start.6 = (s32[8,448]{1,0:T(8,128)S(1)}, s32[8,448]{1,0:T(8,128)}, u32[]{:S(2)}) copy-start(s32[8,448]{1,0:T(8,128)} %refs_0_.3) | copy-start | bytes 43012
  8.6 31.3 %copy-start.7 = (f32[8,448]{1,0:T(8,128)S(1)}, f32[8,448]{1,0:T(8,128)}, u32[]{:S(2)}) copy-start(f32[8,448]{1,0:T(8,128)} %refs_1_.5) | copy-start | bytes 43012
  8.7 33.1 %collective-permute-start.2 = (bf16[64,1024]{1,0:T(8,128)(2,1)S(1)}, bf16[64,1024]{1,0:T(8,128)(2,1)S(1)}, u32[]{:S(2)}, u32[]{:S(2)}) collective-permute-start(bf16[64,1024]{1,0:T(8,128)(2,1)S(1)} %get-tuple-element.41), channel_id=1, source_target_pairs={{1,2},{2,1},{3,4},{4,3},{5,6},{6,5},{7,8},{8,7},{9,10},{10,9},{11,... | collective-permute-start | bytes 393224 | tf_op jit(solution)/shard_map/ppermute | solution.py:340
  13.7 3.3 %collective-permute-start = (bf16[80,1024]{1,0:T(8,128)(2,1)S(1)}, bf16[80,1024]{1,0:T(8,128)(2,1)S(1)}, u32[]{:S(2)}, u32[]{:S(2)}) collective-permute-start(bf16[80,1024]{1,0:T(8,128)(2,1)S(1)} %pad_maximum_fusion), channel_id=1, source_target_pairs={{0,1},{1,0},{2,3},{3,2},{4,5},{5,4},{6,7},{7,6},{8,9},{9,8},{10,11... | collective-permute-start | bytes 491528 | tf_op jit(solution)/shard_map/ppermute | solution.py:344
  18.3 27.3 %all-to-all-start.1 = ((bf16[32,16,128]{2,1,0:T(8,128)(2,1)}), bf16[32,16,128]{2,1,0:T(8,128)(2,1)S(1)}, u32[]{:S(2)}, u32[]{:S(2)}) async-start(bf16[32,16,128]{2,1,0:T(8,128)(2,1)} %shard_map.121), calls=%async_computation.1 | async-start | bytes 262144 | tf_op jit(solution)/shard_map/all_to_all | solution.py:348
  34.9 11.8 %copy-start.2 = (bf16[100,448]{1,0:T(8,128)(2,1)}, bf16[100,448]{1,0:T(8,128)(2,1)S(1)}, u32[]{:S(2)}) copy-start(bf16[100,448]{1,0:T(8,128)(2,1)S(1)} %shard_map.123.refs_4_) | copy-start | bytes 268804
  34.9 6.8 %collective-permute-start.1 = (bf16[100,448]{1,0:T(8,128)(2,1)S(1)}, bf16[100,448]{1,0:T(8,128)(2,1)S(1)}, u32[]{:S(2)}, u32[]{:S(2)}) collective-permute-start(bf16[100,448]{1,0:T(8,128)(2,1)S(1)} %shard_map.123.refs_4_), channel_id=1, source_target_pairs={{0,1},{1,0},{2,3},{3,2},{4,5},{5,4},{6,7},{7,6},{8,9},{9,8},{10,11... | collective-permute-start | bytes 268808 | tf_op jit(solution)/shard_map/ppermute | solution.py:344
  46.7 17.2 %all-to-all-start.2 = ((bf16[8,32,16,128]{3,2,1,0:T(8,128)(2,1)}), bf16[8,32,16,128]{3,2,1,0:T(8,128)(2,1)S(1)}, u32[]{:S(2)}, u32[]{:S(2)}) async-start(bf16[8,32,16,128]{3,2,1,0:T(8,128)(2,1)} %shard_map.125), calls=%async_computation.2 | async-start | bytes 2097152 | tf_op jit(solution)/shard_map/all_to_all | solution.py:352
  54.6 9.3 %collective-permute-start.3 = (bf16[448,1536]{1,0:T(8,128)(2,1)}, bf16[448,1536]{1,0:T(8,128)(2,1)}, u32[]{:S(2)}, u32[]{:S(2)}) collective-permute-start(bf16[448,1536]{1,0:T(8,128)(2,1)} %get-tuple-element.27.refs_7_), channel_id=1, source_target_pairs={{0,1},{1,0},{2,3},{3,2},{4,5},{5,4},{6,7},{7,6},{8,9},{9,8},{10,11... | collective-permute-start | bytes 4128776 | tf_op jit(solution)/shard_map/ppermute | solution.py:344
  69.7 5.6 %copy-start.11 = (bf16[448,1024]{1,0:T(8,128)(2,1)S(1)}, bf16[448,1024]{1,0:T(8,128)(2,1)}, u32[]{:S(2)}) copy-start(bf16[448,1024]{1,0:T(8,128)(2,1)} %get-tuple-element.28) | copy-start | bytes 2752516
  69.7 21.9 %all-to-all-start.3 = ((bf16[8,36,16,128]{3,2,1,0:T(8,128)(2,1)}), bf16[8,36,16,128]{3,2,1,0:T(8,128)(2,1)S(1)}, u32[]{:S(2)}, u32[]{:S(2)}) async-start(bf16[8,36,16,128]{3,2,1,0:T(8,128)(2,1)} %get-tuple-element.35), calls=%async_computation.3 | async-start | bytes 2359296 | tf_op jit(solution)/shard_map/all_to_all | solution.py:352
  75.3 5.0 %collective-permute-start.4 = (bf16[448,1024]{1,0:T(8,128)(2,1)S(1)}, bf16[448,1024]{1,0:T(8,128)(2,1)S(1)}, u32[]{:S(2)}, u32[]{:S(2)}) collective-permute-start(bf16[448,1024]{1,0:T(8,128)(2,1)S(1)} %copy-done.11), channel_id=1, source_target_pairs={{0,1},{1,0},{2,3},{3,2},{4,5},{5,4},{6,7},{7,6},{8,9},{9,8},{10,11... | collective-permute-start | bytes 2752520 | tf_op jit(solution)/shard_map/ppermute | solution.py:344
  92.5 13.9 %all-to-all-start.4 = ((bf16[8,8,16,128]{3,2,1,0:T(8,128)(2,1)}), bf16[8,8,16,128]{3,2,1,0:T(8,128)(2,1)S(1)}, u32[]{:S(2)}, u32[]{:S(2)}) async-start(bf16[8,8,16,128]{3,2,1,0:T(8,128)(2,1)} %shard_map.130), calls=%async_computation.4 | async-start | bytes 524288 | tf_op jit(solution)/shard_map/all_to_all | solution.py:467
  95.9 6.5 %collective-permute-start.5 = (bf16[64,1024]{1,0:T(8,128)(2,1)S(1)}, bf16[64,1024]{1,0:T(8,128)(2,1)S(1)}, u32[]{:S(2)}, u32[]{:S(2)}) collective-permute-start(bf16[64,1024]{1,0:T(8,128)(2,1)S(1)} %get-tuple-element.31), channel_id=1, source_target_pairs={{0,1},{1,0},{2,3},{3,2},{4,5},{5,4},{6,7},{7,6},{8,9},{9,8},{10,11... | collective-permute-start | bytes 393224 | tf_op jit(solution)/shard_map/ppermute | solution.py:344
  98.7 14.2 %collective-permute-start.6 = (bf16[64,1024]{1,0:T(8,128)(2,1)S(1)}, bf16[64,1024]{1,0:T(8,128)(2,1)S(1)}, u32[]{:S(2)}, u32[]{:S(2)}) collective-permute-start(bf16[64,1024]{1,0:T(8,128)(2,1)S(1)} %get-tuple-element.32), channel_id=1, source_target_pairs={{1,2},{2,1},{3,4},{4,3},{5,6},{6,5},{7,8},{8,7},{9,10},{10,9},{11,... | collective-permute-start | bytes 393224 | tf_op jit(solution)/shard_map/ppermute | solution.py:340
  107.1 13.1 %all-to-all-start.5 = ((bf16[4,5,16,128]{3,2,1,0:T(8,128)(2,1)}), bf16[4,5,16,128]{3,2,1,0:T(8,128)(2,1)S(1)}, u32[]{:S(2)}, u32[]{:S(2)}) async-start(bf16[4,5,16,128]{3,2,1,0:T(8,128)(2,1)} %shard_map.131), calls=%async_computation.5 | async-start | bytes 163840 | tf_op jit(solution)/shard_map/all_to_all | solution.py:475
  (2 other events, 5.8 us)

commit v6 on v5

--- a/solution.py
+++ b/solution.py
@@ -102,7 +102,7 @@
 
 
 def pack_body(pred_ref, out_hbm, wide_ref, copies):
-    wide_ref[...] = packed(pred_ref[0].astype(f32)).astype(bf16).reshape(wide_ref.shape)
+    wide_ref[...] = packed(pred_ref[...]).astype(bf16).reshape(wide_ref.shape)
     for c in [copies.start(wide_ref, out_hbm.at[m]) for m in range(MEMBERS)]:
         c.wait()
 
@@ -159,19 +159,21 @@
 
 def pred_body(all_ref, own_ref, target_ref, lw_ref, out_ref):
     members = all_ref.shape[0]
-    variables = out_ref.shape[0]
+    variables = own_ref.shape[0]
     coef_pair = (1.0 - (1.0 - alpha_fair) / members) / (members * (members - 1))
 
     def sign(a):
         return jnp.where(a > 0.0, 1.0, jnp.where(a < 0.0, -1.0, 0.0))
 
-    own = packed(own_ref[0].astype(f32))
+    own = packed(own_ref[...])
     pair_sum = jnp.zeros(own.shape, f32)
     for k in range(members):
         pair_sum += sign(own - all_ref[k].astype(f32).reshape(own.shape))
-    to_target = sign(own_ref[0].astype(f32) - target_ref[...].astype(f32))
+    to_target = sign(own_ref[...] - target_ref[...])
     pair_sum = unpacked(pair_sum, variables)
-    out_ref[...] = (lw_ref[...] * (to_target / members - coef_pair * pair_sum)).astype(bf16)
+    grad = lw_ref[...] * (to_target / members - coef_pair * pair_sum)
+    fill = jnp.zeros((out_ref.shape[0] - variables, grad.shape[1]), f32)
+    out_ref[...] = jnp.concatenate([grad, fill], axis=0).astype(bf16)
 
 
 def share_body(got_ref, out_hbm, copies):
@@ -380,11 +382,12 @@
         sems=1,
     )
 
+    own_pred = predictions[0].astype(f32)
     pred_tiles = -(-variables * nodes // (TILE * LANES))
     (spread_pred,) = call(
         pack_body,
         [sent((MEMBERS, pred_tiles, TILE, LANES), bf16)],
-        (predictions,),
+        (own_pred,),
         [vmem((pred_tiles, TILE, LANES), bf16)],
         sems=MEMBERS,
     )
@@ -410,11 +413,11 @@
     loss_weight = var_weight[:, None] * (area * interior.astype(f32))[None, :]
     (pred_grad,) = call(
         pred_body,
-        [shape((variables, nodes), bf16)],
-        (every_pred, predictions, target, loss_weight),
+        [shape((rows, nodes), bf16)],
+        (every_pred, own_pred, target.astype(f32), loss_weight),
     )
     pred_got = other_core(pred_grad)
-    dec_t = w_dec.T
+    dec_t = jnp.pad(w_dec.T, ((0, rows - variables), (0, 0)))
 
     (spread,) = call(
         share_body,
@@ -430,8 +433,8 @@
         main_body,
         [sent(part_shape, bf16), sent((nodes, half), bf16), sent((nodes, width), bf16)],
         (weight, normed),
-        [vmem((nodes, half), bf16), vmem((variables, nodes), bf16),
-         vmem((variables, width), bf16), vmem((nodes, width + half), bf16), vmem((variables, nodes), bf16), weight_shape, vmem((2 * nodes, half), bf16),
+        [vmem((nodes, half), bf16), vmem((rows, nodes), bf16),
+         vmem((rows, width), bf16), vmem((nodes, width + half), bf16), vmem((rows, nodes), bf16), weight_shape, vmem((2 * nodes, half), bf16),
          vmem((2 * nodes, half), bf16), vmem(part_shape, bf16), vmem((nodes, width), bf16)],
         core=core_arg,
         hbm_args=(keep, pred_grad, dec_t, got, pred_got),
@@ -446,7 +449,7 @@
         scatter_body,
         [sent((nodes, width), bf16), sent((2 * K, width), f32), shape((K, width), bf16), shape((K, width), bf16)],
         (weight, ng_got),
-        [weight_shape, vmem((nodes, LANES), f32), vmem((variables, nodes), bf16), vmem((variables, width), bf16),
+        [weight_shape, vmem((nodes, LANES), f32), vmem((rows, nodes), bf16), vmem((rows, width), bf16),
          vmem((nodes, half), bf16), vmem((nodes, width), bf16), vmem((nodes + 2 * K, nodes), bf16),
          vmem((nodes, width), bf16), vmem((nodes, width), bf16), vmem((2 * K, width), f32)],
         core=core_arg,

time: 138 us -> 139 us (level)
  transfers between devices with their start and end apart: 13 -> 13, of which waited for: 7 -> 7; matrix products, arithmetic and copies ran while one was open for 0% -> 1% of each run, Pallas kernels for 11% -> 11%
where the time goes in v6:
time: 139 us; the launch traced here: 138 us
  starting transfers between devices  68.8 us (49%)
  Pallas kernels  25.2 us (18%)
  waiting for transfers between devices  25 us (18%)
  blocking collectives  15.5 us (11%)
    pallas_call x13, Pallas kernels, call(): pl.pallas_call(kernel, out_shape=out, in_specs=[pl.BlockSpec(memory_space...  25.2 us
    ppermute x5, starting transfers between devices, other_core(): return lax.ppermute(a, 'core', [(0, 1), (1, 0)])  19 us
    all_to_all x1, starting transfers between devices, over_pairs(): return lax.all_to_all(a, PAIR, 0, 0, tiled=True)  15.9 us
    all_to_all x3, starting transfers between devices, over_mem(): return lax.all_to_all(a, 'mem', 0, 0, tiled=True)  15.8 us
    all_to_all x1, blocking collectives, on_device(): last = lax.all_to_all(last_out, ('mem', 'core'), 0, 0, tiled=True)  15.5 us
    ppermute x2, starting transfers between devices, other_pair(): return lax.ppermute(a, GRID, pairs)  8.84 us
    all_to_all x3, waiting for transfers between devices, over_mem(): return lax.all_to_all(a, 'mem', 0, 0, tiled=True)  6.71 us
    all_to_all x1, starting transfers between devices, on_device(): y_parts = lax.all_to_all(y_out, 'y', 0, 0, tiled=True)  5.75 us
  transfers between devices with their start and end apart: 13, of which 7 were waited for; matrix products, arithmetic and copies ran while one was open for 1% of the time, Pallas kernels for 11%

profile of v6, /device:TPU:1, one launch (start us, length us, event | category | flops | bytes accessed | tf_op | source)
XLA Modules:
  0.0 137.6 jit_solution(2567851229139914620)
XLA Ops:
  2.7 6.0 %all-to-all-start = ((bf16[8,22,16,128]{3,2,1,0:T(8,128)(2,1)}), bf16[8,22,16,128]{3,2,1,0:T(8,128)(2,1)S(1)}, u32[]{:S(2)}, u32[]{:S(2)}) async-start(bf16[8,22,16,128]{3,2,1,0:T(8,128)(2,1)} %shard_map.122), calls=%async_computation | async-start | bytes 1441792 | tf_op jit(solution)/shard_map/all_to_all | solution.py:354
  8.7 5.1 %collective-permute-start.2 = (bf16[64,1024]{1,0:T(8,128)(2,1)S(1)}, bf16[64,1024]{1,0:T(8,128)(2,1)S(1)}, u32[]{:S(2)}, u32[]{:S(2)}) collective-permute-start(bf16[64,1024]{1,0:T(8,128)(2,1)S(1)} %get-tuple-element.41), channel_id=1, source_target_pairs={{1,2},{2,1},{3,4},{4,3},{5,6},{6,5},{7,8},{8,7},{9,10},{10,9},{11,... | collective-permute-start | bytes 393224 | tf_op jit(solution)/shard_map/ppermute | solution.py:342
  13.9 2.1 %collective-permute-start = (bf16[80,1024]{1,0:T(8,128)(2,1)S(1)}, bf16[80,1024]{1,0:T(8,128)(2,1)S(1)}, u32[]{:S(2)}, u32[]{:S(2)}) collective-permute-start(bf16[80,1024]{1,0:T(8,128)(2,1)S(1)} %pad_maximum_fusion), channel_id=1, source_target_pairs={{0,1},{1,0},{2,3},{3,2},{4,5},{5,4},{6,7},{7,6},{8,9},{9,8},{10,11... | collective-permute-start | bytes 491528 | tf_op jit(solution)/shard_map/ppermute | solution.py:346
  18.4 15.9 %all-to-all-start.1 = ((bf16[32,16,128]{2,1,0:T(8,128)(2,1)}), bf16[32,16,128]{2,1,0:T(8,128)(2,1)S(1)}, u32[]{:S(2)}, u32[]{:S(2)}) async-start(bf16[32,16,128]{2,1,0:T(8,128)(2,1)} %shard_map.121), calls=%async_computation.1 | async-start | bytes 262144 | tf_op jit(solution)/shard_map/all_to_all | solution.py:350
  35.0 5.0 %collective-permute-start.1 = (bf16[112,448]{1,0:T(8,128)(2,1)S(1)}, bf16[112,448]{1,0:T(8,128)(2,1)S(1)}, u32[]{:S(2)}, u32[]{:S(2)}) collective-permute-start(bf16[112,448]{1,0:T(8,128)(2,1)S(1)} %shard_map.123.refs_4_), channel_id=1, source_target_pairs={{0,1},{1,0},{2,3},{3,2},{4,5},{5,4},{6,7},{7,6},{8,9},{9,8},{10,11... | collective-permute-start | bytes 301064 | tf_op jit(solution)/shard_map/ppermute | solution.py:346
  41.9 3.8 %all-to-all-done.1.refs_0_ = bf16[32,16,128]{2,1,0:T(8,128)(2,1)S(1)} async-done(((bf16[32,16,128]{2,1,0:T(8,128)(2,1)}), bf16[32,16,128]{2,1,0:T(8,128)(2,1)S(1)}, u32[]{:S(2)}, u32[]{:S(2)}) %all-to-all-start.1) | async-done | bytes 131104 | tf_op jit(solution)/shard_map/all_to_all | solution.py:350
  46.8 4.3 %all-to-all-start.2 = ((bf16[8,32,16,128]{3,2,1,0:T(8,128)(2,1)}), bf16[8,32,16,128]{3,2,1,0:T(8,128)(2,1)S(1)}, u32[]{:S(2)}, u32[]{:S(2)}) async-start(bf16[8,32,16,128]{3,2,1,0:T(8,128)(2,1)} %shard_map.125), calls=%async_computation.2 | async-start | bytes 2097152 | tf_op jit(solution)/shard_map/all_to_all | solution.py:354
  51.0 3.7 %shard_map.126 = (f32[448,128]{1,0:T(8,128)}, bf16[448,512]{1,0:T(8,128)(2,1)}, bf16[448,1024]{1,0:T(8,128)(2,1)S(1)}, bf16[448,1536]{1,0:T(8,128)(2,1)}) custom-call(s32[1]{0:T(128)} %bitcast.refs_0_, bf16[448,1024]{1,0:T(8,128)(2,1)S(1)} %bitcast.13, bf16[80,1024]{1,0:T(8,128)(2,1)S(1)} %collective-permute-done.refs_2_, ...), custom_call_target="tpu_custom_call" | custom-call | flops 528482304 | bytes 4710400 | tf_op jit(solution)/shard_map/pallas_call | solution.py:74
  54.7 6.2 %collective-permute-start.3 = (bf16[448,1536]{1,0:T(8,128)(2,1)}, bf16[448,1536]{1,0:T(8,128)(2,1)}, u32[]{:S(2)}, u32[]{:S(2)}) collective-permute-start(bf16[448,1536]{1,0:T(8,128)(2,1)} %get-tuple-element.27.refs_7_), channel_id=1, source_target_pairs={{0,1},{1,0},{2,3},{3,2},{4,5},{5,4},{6,7},{7,6},{8,9},{9,8},{10,11... | collective-permute-start | bytes 4128776 | tf_op jit(solution)/shard_map/ppermute | solution.py:346
  61.7 2.3 %collective-permute-done.3.refs_6_ = bf16[448,1536]{1,0:T(8,128)(2,1)} collective-permute-done((bf16[448,1536]{1,0:T(8,128)(2,1)}, bf16[448,1536]{1,0:T(8,128)(2,1)}, u32[]{:S(2)}, u32[]{:S(2)}) %collective-permute-start.3) | collective-permute-done | bytes 1376288 | tf_op jit(solution)/shard_map/ppermute | solution.py:346
  64.0 5.8 %shard_map.127 = (bf16[8,36,16,128]{3,2,1,0:T(8,128)(2,1)}, bf16[448,512]{1,0:T(8,128)(2,1)}, bf16[448,1024]{1,0:T(8,128)(2,1)}) custom-call(s32[1]{0:T(128)} %bitcast.refs_0_, bf16[8,32,16,128]{3,2,1,0:T(8,128)(2,1)S(1)} %all-to-all-done.2.refs_1_, bf16[448,1024]{1,0:T(8,128)(2,1)S(1)} %get-tuple-element.25.refs_2_, ...), custom_call_target="tpu_custom_call" | custom-call | flops 2348810240 | bytes 6787072 | tf_op jit(solution)/shard_map/pallas_call | solution.py:74
  69.9 5.6 %all-to-all-start.3 = ((bf16[8,36,16,128]{3,2,1,0:T(8,128)(2,1)}), bf16[8,36,16,128]{3,2,1,0:T(8,128)(2,1)S(1)}, u32[]{:S(2)}, u32[]{:S(2)}) async-start(bf16[8,36,16,128]{3,2,1,0:T(8,128)(2,1)} %get-tuple-element.35), calls=%async_computation.3 | async-start | bytes 2359296 | tf_op jit(solution)/shard_map/all_to_all | solution.py:354
  75.4 2.9 %collective-permute-start.4 = (bf16[448,1024]{1,0:T(8,128)(2,1)S(1)}, bf16[448,1024]{1,0:T(8,128)(2,1)S(1)}, u32[]{:S(2)}, u32[]{:S(2)}) collective-permute-start(bf16[448,1024]{1,0:T(8,128)(2,1)S(1)} %copy-done.10), channel_id=1, source_target_pairs={{0,1},{1,0},{2,3},{3,2},{4,5},{5,4},{6,7},{7,6},{8,9},{9,8},{10,11... | collective-permute-start | bytes 2752520 | tf_op jit(solution)/shard_map/ppermute | solution.py:346
  78.4 2.1 %collective-permute-done.4.refs_2_ = bf16[448,1024]{1,0:T(8,128)(2,1)S(1)} collective-permute-done((bf16[448,1024]{1,0:T(8,128)(2,1)S(1)}, bf16[448,1024]{1,0:T(8,128)(2,1)S(1)}, u32[]{:S(2)}, u32[]{:S(2)}) %collective-permute-start.4) | collective-permute-done | bytes 917536 | tf_op jit(solution)/shard_map/ppermute | solution.py:346
  80.4 4.6 %shard_map.128 = (bf16[448,1024]{1,0:T(8,128)(2,1)}, f32[128,1024]{1,0:T(8,128)}, bf16[64,1024]{1,0:T(8,128)(2,1)S(1)}, bf16[64,1024]{1,0:T(8,128)(2,1)S(1)}) custom-call(s32[1]{0:T(128)} %bitcast.refs_0_, bf16[8,32,16,128]{3,2,1,0:T(8,128)(2,1)S(1)} %all-to-all-done.2.refs_1_, bf16[448,1024]{1,0:T(8,128)(2,1)S(1)} %collective-permute-done.4.refs_2_, ...), custom_call_target="tpu_custom_call" | custom-call | flops 528482304 | bytes 6580224 | tf_op jit(solution)/shard_map/pallas_call | solution.py:74
  85.0 6.7 %all-to-all-done.3.refs_0_ = bf16[8,36,16,128]{3,2,1,0:T(8,128)(2,1)S(1)} async-done(((bf16[8,36,16,128]{3,2,1,0:T(8,128)(2,1)}), bf16[8,36,16,128]{3,2,1,0:T(8,128)(2,1)S(1)}, u32[]{:S(2)}, u32[]{:S(2)}) %all-to-all-start.3) | async-done | bytes 1179680 | tf_op jit(solution)/shard_map/all_to_all | solution.py:354
  92.6 3.4 %all-to-all-start.4 = ((bf16[8,8,16,128]{3,2,1,0:T(8,128)(2,1)}), bf16[8,8,16,128]{3,2,1,0:T(8,128)(2,1)S(1)}, u32[]{:S(2)}, u32[]{:S(2)}) async-start(bf16[8,8,16,128]{3,2,1,0:T(8,128)(2,1)} %shard_map.130), calls=%async_computation.4 | async-start | bytes 524288 | tf_op jit(solution)/shard_map/all_to_all | solution.py:470
  96.0 2.8 %collective-permute-start.5 = (bf16[64,1024]{1,0:T(8,128)(2,1)S(1)}, bf16[64,1024]{1,0:T(8,128)(2,1)S(1)}, u32[]{:S(2)}, u32[]{:S(2)}) collective-permute-start(bf16[64,1024]{1,0:T(8,128)(2,1)S(1)} %get-tuple-element.31), channel_id=1, source_target_pairs={{0,1},{1,0},{2,3},{3,2},{4,5},{5,4},{6,7},{7,6},{8,9},{9,8},{10,11... | collective-permute-start | bytes 393224 | tf_op jit(solution)/shard_map/ppermute | solution.py:346
  98.8 3.8 %collective-permute-start.6 = (bf16[64,1024]{1,0:T(8,128)(2,1)S(1)}, bf16[64,1024]{1,0:T(8,128)(2,1)S(1)}, u32[]{:S(2)}, u32[]{:S(2)}) collective-permute-start(bf16[64,1024]{1,0:T(8,128)(2,1)S(1)} %get-tuple-element.32), channel_id=1, source_target_pairs={{1,2},{2,1},{3,4},{4,3},{5,6},{6,5},{7,8},{8,7},{9,10},{10,9},{11,... | collective-permute-start | bytes 393224 | tf_op jit(solution)/shard_map/ppermute | solution.py:342
  102.6 3.9 %all-to-all-done.4.refs_0_ = bf16[8,8,16,128]{3,2,1,0:T(8,128)(2,1)S(1)} async-done(((bf16[8,8,16,128]{3,2,1,0:T(8,128)(2,1)}), bf16[8,8,16,128]{3,2,1,0:T(8,128)(2,1)S(1)}, u32[]{:S(2)}, u32[]{:S(2)}) %all-to-all-start.4) | async-done | bytes 262176 | tf_op jit(solution)/shard_map/all_to_all | solution.py:470
  107.2 5.8 %all-to-all-start.5 = ((bf16[4,5,16,128]{3,2,1,0:T(8,128)(2,1)}), bf16[4,5,16,128]{3,2,1,0:T(8,128)(2,1)S(1)}, u32[]{:S(2)}, u32[]{:S(2)}) async-start(bf16[4,5,16,128]{3,2,1,0:T(8,128)(2,1)} %shard_map.131), calls=%async_computation.5 | async-start | bytes 163840 | tf_op jit(solution)/shard_map/all_to_all | solution.py:478
  113.0 2.3 %shard_map.129 = bf16[1,448,1024]{2,1,0:T(8,128)(2,1)} custom-call(s32[1]{0:T(128)} %bitcast.refs_0_, bf16[64,1024]{1,0:T(8,128)(2,1)S(1)} %collective-permute-done.5.refs_1_, bf16[64,1024]{1,0:T(8,128)(2,1)S(1)} %collective-permute-done.6.refs_2_, bf16[448,1024]{1,0:T(8,128)(2,1)} %get-tuple-element.33.refs_3_, f32[128,1024]{1,0:T(8,128)} %get-tuple-element.34.refs_4_), custom_call_target="tpu_custom_call" | custom-call | bytes 2621440 | tf_op jit(solution)/shard_map/pallas_call | solution.py:74
  115.3 5.1 %all-to-all-done.5.refs_0_ = bf16[4,5,16,128]{3,2,1,0:T(8,128)(2,1)S(1)} async-done(((bf16[4,5,16,128]{3,2,1,0:T(8,128)(2,1)}), bf16[4,5,16,128]{3,2,1,0:T(8,128)(2,1)S(1)}, u32[]{:S(2)}, u32[]{:S(2)}) %all-to-all-start.5) | async-done | bytes 81952 | tf_op jit(solution)/shard_map/all_to_all | solution.py:478
  121.3 15.5 %all_to_all.35.refs_1_ = bf16[16,5,16,128]{3,2,1,0:T(8,128)(2,1)S(1)} all-to-all(bf16[16,5,16,128]{3,2,1,0:T(8,128)(2,1)} %shard_map.132), channel_id=1, replica_groups=mesh['mem'=8,'z'=8,'y'=4,'core'=2] {'mem','core'}, dimensions={0} | all-to-all | bytes 655360 | tf_op jit(solution)/shard_map/all_to_all | solution.py:495
  (48 shorter events, 11.9 us)
Async XLA Ops:
  0.6 8.1 %copy-start.2 = (bf16[1,448,1024]{2,1,0:T(8,128)(2,1)S(1)}, bf16[1,448,1024]{2,1,0:T(8,128)(2,1)}, u32[]{:S(2)}) copy-start(bf16[1,448,1024]{2,1,0:T(8,128)(2,1)} %param.10) | copy-start | bytes 2752516
  1.6 12.2 %copy-start.1 = (bf16[16,1024]{1,0:T(8,128)(2,1)S(1)}, bf16[16,1024]{1,0:T(8,128)(2,1)}, u32[]{:S(2)}) copy-start(bf16[16,1024]{1,0:T(8,128)(2,1)} %refs_1_.2) | copy-start | bytes 98308
  2.7 13.3 %copy-start.7 = (f32[448]{0:T(512)S(1)}, f32[448]{0:T(512)}, u32[]{:S(2)}) copy-start(f32[448]{0:T(512)} %param.13) | copy-start | bytes 5380
  2.7 13.3 %copy-start.8 = (s32[448]{0:T(512)S(1)}, s32[448]{0:T(512)}, u32[]{:S(2)}) copy-start(s32[448]{0:T(512)} %param.15) | copy-start | bytes 5380
  2.7 31.7 %copy-start.9 = (f32[100]{0:T(128)S(1)}, f32[100]{0:T(128)}, u32[]{:S(2)}) copy-start(f32[100]{0:T(128)} %param.14) | copy-start | bytes 1204
  2.7 31.8 %copy-start.6 = (bf16[100,448]{1,0:T(8,128)(2,1)S(1)}, bf16[100,448]{1,0:T(8,128)(2,1)}, u32[]{:S(2)}) copy-start(bf16[100,448]{1,0:T(8,128)(2,1)} %param.12) | copy-start | bytes 268804
  2.7 15.7 %all-to-all-start = ((bf16[8,22,16,128]{3,2,1,0:T(8,128)(2,1)}), bf16[8,22,16,128]{3,2,1,0:T(8,128)(2,1)S(1)}, u32[]{:S(2)}, u32[]{:S(2)}) async-start(bf16[8,22,16,128]{3,2,1,0:T(8,128)(2,1)} %shard_map.122), calls=%async_computation | async-start | bytes 1441792 | tf_op jit(solution)/shard_map/all_to_all | solution.py:354
  8.7 33.1 %collective-permute-start.2 = (bf16[64,1024]{1,0:T(8,128)(2,1)S(1)}, bf16[64,1024]{1,0:T(8,128)(2,1)S(1)}, u32[]{:S(2)}, u32[]{:S(2)}) collective-permute-start(bf16[64,1024]{1,0:T(8,128)(2,1)S(1)} %get-tuple-element.41), channel_id=1, source_target_pairs={{1,2},{2,1},{3,4},{4,3},{5,6},{6,5},{7,8},{8,7},{9,10},{10,9},{11,... | collective-permute-start | bytes 393224 | tf_op jit(solution)/shard_map/ppermute | solution.py:342
  13.8 26.2 %copy-start.3 = (s32[8,448]{1,0:T(8,128)S(1)}, s32[8,448]{1,0:T(8,128)}, u32[]{:S(2)}) copy-start(s32[8,448]{1,0:T(8,128)} %refs_0_.1) | copy-start | bytes 43012
  13.9 26.2 %copy-start.4 = (f32[8,448]{1,0:T(8,128)S(1)}, f32[8,448]{1,0:T(8,128)}, u32[]{:S(2)}) copy-start(f32[8,448]{1,0:T(8,128)} %refs_1_.3) | copy-start | bytes 43012
  13.9 3.3 %collective-permute-start = (bf16[80,1024]{1,0:T(8,128)(2,1)S(1)}, bf16[80,1024]{1,0:T(8,128)(2,1)S(1)}, u32[]{:S(2)}, u32[]{:S(2)}) collective-permute-start(bf16[80,1024]{1,0:T(8,128)(2,1)S(1)} %pad_maximum_fusion), channel_id=1, source_target_pairs={{0,1},{1,0},{2,3},{3,2},{4,5},{5,4},{6,7},{7,6},{8,9},{9,8},{10,11... | collective-permute-start | bytes 491528 | tf_op jit(solution)/shard_map/ppermute | solution.py:346
  18.4 27.3 %all-to-all-start.1 = ((bf16[32,16,128]{2,1,0:T(8,128)(2,1)}), bf16[32,16,128]{2,1,0:T(8,128)(2,1)S(1)}, u32[]{:S(2)}, u32[]{:S(2)}) async-start(bf16[32,16,128]{2,1,0:T(8,128)(2,1)} %shard_map.121), calls=%async_computation.1 | async-start | bytes 262144 | tf_op jit(solution)/shard_map/all_to_all | solution.py:350
  35.0 11.7 %copy-start = (bf16[112,448]{1,0:T(8,128)(2,1)}, bf16[112,448]{1,0:T(8,128)(2,1)S(1)}, u32[]{:S(2)}) copy-start(bf16[112,448]{1,0:T(8,128)(2,1)S(1)} %shard_map.123.refs_4_) | copy-start | bytes 301060
  35.0 6.8 %collective-permute-start.1 = (bf16[112,448]{1,0:T(8,128)(2,1)S(1)}, bf16[112,448]{1,0:T(8,128)(2,1)S(1)}, u32[]{:S(2)}, u32[]{:S(2)}) collective-permute-start(bf16[112,448]{1,0:T(8,128)(2,1)S(1)} %shard_map.123.refs_4_), channel_id=1, source_target_pairs={{0,1},{1,0},{2,3},{3,2},{4,5},{5,4},{6,7},{7,6},{8,9},{9,8},{10,11... | collective-permute-start | bytes 301064 | tf_op jit(solution)/shard_map/ppermute | solution.py:346
  46.8 17.3 %all-to-all-start.2 = ((bf16[8,32,16,128]{3,2,1,0:T(8,128)(2,1)}), bf16[8,32,16,128]{3,2,1,0:T(8,128)(2,1)S(1)}, u32[]{:S(2)}, u32[]{:S(2)}) async-start(bf16[8,32,16,128]{3,2,1,0:T(8,128)(2,1)} %shard_map.125), calls=%async_computation.2 | async-start | bytes 2097152 | tf_op jit(solution)/shard_map/all_to_all | solution.py:354
  51.0 9.9 %copy-start.5 = (bf16[1024,100]{0,1:T(8,128)(2,1)S(1)}, bf16[1024,100]{0,1:T(8,128)(2,1)}, u32[]{:S(2)}) copy-start(bf16[1024,100]{0,1:T(8,128)(2,1)} %param.19) | copy-start | bytes 614404
  54.7 9.3 %collective-permute-start.3 = (bf16[448,1536]{1,0:T(8,128)(2,1)}, bf16[448,1536]{1,0:T(8,128)(2,1)}, u32[]{:S(2)}, u32[]{:S(2)}) collective-permute-start(bf16[448,1536]{1,0:T(8,128)(2,1)} %get-tuple-element.27.refs_7_), channel_id=1, source_target_pairs={{0,1},{1,0},{2,3},{3,2},{4,5},{5,4},{6,7},{7,6},{8,9},{9,8},{10,11... | collective-permute-start | bytes 4128776 | tf_op jit(solution)/shard_map/ppermute | solution.py:346
  69.9 5.6 %copy-start.10 = (bf16[448,1024]{1,0:T(8,128)(2,1)S(1)}, bf16[448,1024]{1,0:T(8,128)(2,1)}, u32[]{:S(2)}) copy-start(bf16[448,1024]{1,0:T(8,128)(2,1)} %get-tuple-element.28) | copy-start | bytes 2752516
  69.9 21.9 %all-to-all-start.3 = ((bf16[8,36,16,128]{3,2,1,0:T(8,128)(2,1)}), bf16[8,36,16,128]{3,2,1,0:T(8,128)(2,1)S(1)}, u32[]{:S(2)}, u32[]{:S(2)}) async-start(bf16[8,36,16,128]{3,2,1,0:T(8,128)(2,1)} %get-tuple-element.35), calls=%async_computation.3 | async-start | bytes 2359296 | tf_op jit(solution)/shard_map/all_to_all | solution.py:354
  75.4 5.0 %collective-permute-start.4 = (bf16[448,1024]{1,0:T(8,128)(2,1)S(1)}, bf16[448,1024]{1,0:T(8,128)(2,1)S(1)}, u32[]{:S(2)}, u32[]{:S(2)}) collective-permute-start(bf16[448,1024]{1,0:T(8,128)(2,1)S(1)} %copy-done.10), channel_id=1, source_target_pairs={{0,1},{1,0},{2,3},{3,2},{4,5},{5,4},{6,7},{7,6},{8,9},{9,8},{10,11... | collective-permute-start | bytes 2752520 | tf_op jit(solution)/shard_map/ppermute | solution.py:346
  92.6 13.9 %all-to-all-start.4 = ((bf16[8,8,16,128]{3,2,1,0:T(8,128)(2,1)}), bf16[8,8,16,128]{3,2,1,0:T(8,128)(2,1)S(1)}, u32[]{:S(2)}, u32[]{:S(2)}) async-start(bf16[8,8,16,128]{3,2,1,0:T(8,128)(2,1)} %shard_map.130), calls=%async_computation.4 | async-start | bytes 524288 | tf_op jit(solution)/shard_map/all_to_all | solution.py:470
  96.0 6.6 %collective-permute-start.5 = (bf16[64,1024]{1,0:T(8,128)(2,1)S(1)}, bf16[64,1024]{1,0:T(8,128)(2,1)S(1)}, u32[]{:S(2)}, u32[]{:S(2)}) collective-permute-start(bf16[64,1024]{1,0:T(8,128)(2,1)S(1)} %get-tuple-element.31), channel_id=1, source_target_pairs={{0,1},{1,0},{2,3},{3,2},{4,5},{5,4},{6,7},{7,6},{8,9},{9,8},{10,11... | collective-permute-start | bytes 393224 | tf_op jit(solution)/shard_map/ppermute | solution.py:346
  98.8 14.2 %collective-permute-start.6 = (bf16[64,1024]{1,0:T(8,128)(2,1)S(1)}, bf16[64,1024]{1,0:T(8,128)(2,1)S(1)}, u32[]{:S(2)}, u32[]{:S(2)}) collective-permute-start(bf16[64,1024]{1,0:T(8,128)(2,1)S(1)} %get-tuple-element.32), channel_id=1, source_target_pairs={{1,2},{2,1},{3,4},{4,3},{5,6},{6,5},{7,8},{8,7},{9,10},{10,9},{11,... | collective-permute-start | bytes 393224 | tf_op jit(solution)/shard_map/ppermute | solution.py:342
  107.2 13.2 %all-to-all-start.5 = ((bf16[4,5,16,128]{3,2,1,0:T(8,128)(2,1)}), bf16[4,5,16,128]{3,2,1,0:T(8,128)(2,1)S(1)}, u32[]{:S(2)}, u32[]{:S(2)}) async-start(bf16[4,5,16,128]{3,2,1,0:T(8,128)(2,1)} %shard_map.131), calls=%async_computation.5 | async-start | bytes 163840 | tf_op jit(solution)/shard_map/all_to_all | solution.py:478
  (1 other events, 4.9 us)

commit v7 on v6

--- a/solution.py
+++ b/solution.py
@@ -463,7 +463,7 @@
     (z_out,) = call(
         sum_body,
         [sent((n_z, n_y + cols, TILE, LANES), bf16)],
-        (after(mem_parts, to_near),),
+        (after(mem_parts, from_near),),
         [vmem((n_z, n_y + cols, TILE, LANES), bf16)],
         sems=1,
     )
@@ -471,7 +471,7 @@
     (y_out,) = call(
         sum_body,
         [sent((n_y, 1 + cols, TILE, LANES), bf16)],
-        (after(z_parts, from_near),),
+        (after(z_parts, to_far),),
         [vmem((n_y, 1 + cols, TILE, LANES), bf16)],
         sems=1,
     )

time: 139 us -> 139 us (level)
    all_to_all x3, waiting for transfers between devices: 6.71 us -> 3.46 us  [over_mem(): return lax.all_to_all(a, 'mem', 0, 0, tiled=True)]
    all_to_all x1, waiting for transfers between devices: 3.92 us -> 5.86 us  [on_device(): z_parts = lax.all_to_all(z_out, 'z', 0, 0, tiled=True)]
  transfers between devices with their start and end apart: 13 -> 13, of which waited for: 7 -> 8; matrix products, arithmetic and copies ran while one was open for 1% -> 1% of each run, Pallas kernels for 11% -> 11%
where the time goes in v7:
time: 139 us; the launch traced here: 138 us
  starting transfers between devices  69.1 us (50%)
  Pallas kernels  25.2 us (18%)
  waiting for transfers between devices  24.7 us (18%)
  blocking collectives  15.5 us (11%)
    pallas_call x13, Pallas kernels, call(): pl.pallas_call(kernel, out_shape=out, in_specs=[pl.BlockSpec(memory_space...  25.2 us
    ppermute x5, starting transfers between devices, other_core(): return lax.ppermute(a, 'core', [(0, 1), (1, 0)])  18.5 us
    all_to_all x1, starting transfers between devices, over_pairs(): return lax.all_to_all(a, PAIR, 0, 0, tiled=True)  15.9 us
    all_to_all x3, starting transfers between devices, over_mem(): return lax.all_to_all(a, 'mem', 0, 0, tiled=True)  15.8 us
    all_to_all x1, blocking collectives, on_device(): last = lax.all_to_all(last_out, ('mem', 'core'), 0, 0, tiled=True)  15.5 us
    ppermute x2, starting transfers between devices, other_pair(): return lax.ppermute(a, GRID, pairs)  9.69 us
    ppermute x5, waiting for transfers between devices, other_core(): return lax.ppermute(a, 'core', [(0, 1), (1, 0)])  6.44 us
    all_to_all x1, waiting for transfers between devices, on_device(): z_parts = lax.all_to_all(z_out, 'z', 0, 0, tiled=True)  5.86 us
  transfers between devices with their start and end apart: 13, of which 8 were waited for; matrix products, arithmetic and copies ran while one was open for 1% of the time, Pallas kernels for 11%

profile of v7, /device:TPU:1, one launch (start us, length us, event | category | flops | bytes accessed | tf_op | source)
XLA Modules:
  0.0 137.6 jit_solution(5761863005750347411)
XLA Ops:
  2.7 6.0 %all-to-all-start = ((bf16[8,22,16,128]{3,2,1,0:T(8,128)(2,1)}), bf16[8,22,16,128]{3,2,1,0:T(8,128)(2,1)S(1)}, u32[]{:S(2)}, u32[]{:S(2)}) async-start(bf16[8,22,16,128]{3,2,1,0:T(8,128)(2,1)} %shard_map.122), calls=%async_computation | async-start | bytes 1441792 | tf_op jit(solution)/shard_map/all_to_all | solution.py:354
  8.7 5.1 %collective-permute-start.2 = (bf16[64,1024]{1,0:T(8,128)(2,1)S(1)}, bf16[64,1024]{1,0:T(8,128)(2,1)S(1)}, u32[]{:S(2)}, u32[]{:S(2)}) collective-permute-start(bf16[64,1024]{1,0:T(8,128)(2,1)S(1)} %get-tuple-element.41), channel_id=1, source_target_pairs={{1,2},{2,1},{3,4},{4,3},{5,6},{6,5},{7,8},{8,7},{9,10},{10,9},{11,... | collective-permute-start | bytes 393224 | tf_op jit(solution)/shard_map/ppermute | solution.py:342
  13.9 2.1 %collective-permute-start = (bf16[80,1024]{1,0:T(8,128)(2,1)S(1)}, bf16[80,1024]{1,0:T(8,128)(2,1)S(1)}, u32[]{:S(2)}, u32[]{:S(2)}) collective-permute-start(bf16[80,1024]{1,0:T(8,128)(2,1)S(1)} %pad_maximum_fusion), channel_id=1, source_target_pairs={{0,1},{1,0},{2,3},{3,2},{4,5},{5,4},{6,7},{7,6},{8,9},{9,8},{10,11... | collective-permute-start | bytes 491528 | tf_op jit(solution)/shard_map/ppermute | solution.py:346
  18.4 15.9 %all-to-all-start.1 = ((bf16[32,16,128]{2,1,0:T(8,128)(2,1)}), bf16[32,16,128]{2,1,0:T(8,128)(2,1)S(1)}, u32[]{:S(2)}, u32[]{:S(2)}) async-start(bf16[32,16,128]{2,1,0:T(8,128)(2,1)} %shard_map.121), calls=%async_computation.1 | async-start | bytes 262144 | tf_op jit(solution)/shard_map/all_to_all | solution.py:350
  35.0 5.0 %collective-permute-start.1 = (bf16[112,448]{1,0:T(8,128)(2,1)S(1)}, bf16[112,448]{1,0:T(8,128)(2,1)S(1)}, u32[]{:S(2)}, u32[]{:S(2)}) collective-permute-start(bf16[112,448]{1,0:T(8,128)(2,1)S(1)} %shard_map.123.refs_4_), channel_id=1, source_target_pairs={{0,1},{1,0},{2,3},{3,2},{4,5},{5,4},{6,7},{7,6},{8,9},{9,8},{10,11... | collective-permute-start | bytes 301064 | tf_op jit(solution)/shard_map/ppermute | solution.py:346
  41.9 3.8 %all-to-all-done.1.refs_0_ = bf16[32,16,128]{2,1,0:T(8,128)(2,1)S(1)} async-done(((bf16[32,16,128]{2,1,0:T(8,128)(2,1)}), bf16[32,16,128]{2,1,0:T(8,128)(2,1)S(1)}, u32[]{:S(2)}, u32[]{:S(2)}) %all-to-all-start.1) | async-done | bytes 131104 | tf_op jit(solution)/shard_map/all_to_all | solution.py:350
  46.8 4.3 %all-to-all-start.2 = ((bf16[8,32,16,128]{3,2,1,0:T(8,128)(2,1)}), bf16[8,32,16,128]{3,2,1,0:T(8,128)(2,1)S(1)}, u32[]{:S(2)}, u32[]{:S(2)}) async-start(bf16[8,32,16,128]{3,2,1,0:T(8,128)(2,1)} %shard_map.125), calls=%async_computation.2 | async-start | bytes 2097152 | tf_op jit(solution)/shard_map/all_to_all | solution.py:354
  51.0 3.7 %shard_map.126 = (f32[448,128]{1,0:T(8,128)}, bf16[448,512]{1,0:T(8,128)(2,1)}, bf16[448,1024]{1,0:T(8,128)(2,1)S(1)}, bf16[448,1536]{1,0:T(8,128)(2,1)}) custom-call(s32[1]{0:T(128)} %bitcast.refs_0_, bf16[448,1024]{1,0:T(8,128)(2,1)S(1)} %bitcast.13, bf16[80,1024]{1,0:T(8,128)(2,1)S(1)} %collective-permute-done.refs_2_, ...), custom_call_target="tpu_custom_call" | custom-call | flops 528482304 | bytes 4710400 | tf_op jit(solution)/shard_map/pallas_call | solution.py:74
  54.7 6.2 %collective-permute-start.3 = (bf16[448,1536]{1,0:T(8,128)(2,1)}, bf16[448,1536]{1,0:T(8,128)(2,1)}, u32[]{:S(2)}, u32[]{:S(2)}) collective-permute-start(bf16[448,1536]{1,0:T(8,128)(2,1)} %get-tuple-element.27.refs_7_), channel_id=1, source_target_pairs={{0,1},{1,0},{2,3},{3,2},{4,5},{5,4},{6,7},{7,6},{8,9},{9,8},{10,11... | collective-permute-start | bytes 4128776 | tf_op jit(solution)/shard_map/ppermute | solution.py:346
  61.7 2.3 %collective-permute-done.3.refs_6_ = bf16[448,1536]{1,0:T(8,128)(2,1)} collective-permute-done((bf16[448,1536]{1,0:T(8,128)(2,1)}, bf16[448,1536]{1,0:T(8,128)(2,1)}, u32[]{:S(2)}, u32[]{:S(2)}) %collective-permute-start.3) | collective-permute-done | bytes 1376288 | tf_op jit(solution)/shard_map/ppermute | solution.py:346
  64.0 5.8 %shard_map.127 = (bf16[8,36,16,128]{3,2,1,0:T(8,128)(2,1)}, bf16[448,512]{1,0:T(8,128)(2,1)}, bf16[448,1024]{1,0:T(8,128)(2,1)}) custom-call(s32[1]{0:T(128)} %bitcast.refs_0_, bf16[8,32,16,128]{3,2,1,0:T(8,128)(2,1)S(1)} %all-to-all-done.2.refs_1_, bf16[448,1024]{1,0:T(8,128)(2,1)S(1)} %get-tuple-element.25.refs_2_, ...), custom_call_target="tpu_custom_call" | custom-call | flops 2348810240 | bytes 6787072 | tf_op jit(solution)/shard_map/pallas_call | solution.py:74
  69.9 5.6 %all-to-all-start.3 = ((bf16[8,36,16,128]{3,2,1,0:T(8,128)(2,1)}), bf16[8,36,16,128]{3,2,1,0:T(8,128)(2,1)S(1)}, u32[]{:S(2)}, u32[]{:S(2)}) async-start(bf16[8,36,16,128]{3,2,1,0:T(8,128)(2,1)} %get-tuple-element.35), calls=%async_computation.3 | async-start | bytes 2359296 | tf_op jit(solution)/shard_map/all_to_all | solution.py:354
  75.4 2.9 %collective-permute-start.4 = (bf16[448,1024]{1,0:T(8,128)(2,1)S(1)}, bf16[448,1024]{1,0:T(8,128)(2,1)S(1)}, u32[]{:S(2)}, u32[]{:S(2)}) collective-permute-start(bf16[448,1024]{1,0:T(8,128)(2,1)S(1)} %copy-done.10), channel_id=1, source_target_pairs={{0,1},{1,0},{2,3},{3,2},{4,5},{5,4},{6,7},{7,6},{8,9},{9,8},{10,11... | collective-permute-start | bytes 2752520 | tf_op jit(solution)/shard_map/ppermute | solution.py:346
  78.4 2.1 %collective-permute-done.4.refs_2_ = bf16[448,1024]{1,0:T(8,128)(2,1)S(1)} collective-permute-done((bf16[448,1024]{1,0:T(8,128)(2,1)S(1)}, bf16[448,1024]{1,0:T(8,128)(2,1)S(1)}, u32[]{:S(2)}, u32[]{:S(2)}) %collective-permute-start.4) | collective-permute-done | bytes 917536 | tf_op jit(solution)/shard_map/ppermute | solution.py:346
  80.4 4.6 %shard_map.128 = (bf16[448,1024]{1,0:T(8,128)(2,1)}, f32[128,1024]{1,0:T(8,128)}, bf16[64,1024]{1,0:T(8,128)(2,1)S(1)}, bf16[64,1024]{1,0:T(8,128)(2,1)S(1)}) custom-call(s32[1]{0:T(128)} %bitcast.refs_0_, bf16[8,32,16,128]{3,2,1,0:T(8,128)(2,1)S(1)} %all-to-all-done.2.refs_1_, bf16[448,1024]{1,0:T(8,128)(2,1)S(1)} %collective-permute-done.4.refs_2_, ...), custom_call_target="tpu_custom_call" | custom-call | flops 528482304 | bytes 6580224 | tf_op jit(solution)/shard_map/pallas_call | solution.py:74
  85.0 2.3 %collective-permute-start.5 = (bf16[64,1024]{1,0:T(8,128)(2,1)S(1)}, bf16[64,1024]{1,0:T(8,128)(2,1)S(1)}, u32[]{:S(2)}, u32[]{:S(2)}) collective-permute-start(bf16[64,1024]{1,0:T(8,128)(2,1)S(1)} %get-tuple-element.31), channel_id=1, source_target_pairs={{0,1},{1,0},{2,3},{3,2},{4,5},{5,4},{6,7},{7,6},{8,9},{9,8},{10,11... | collective-permute-start | bytes 393224 | tf_op jit(solution)/shard_map/ppermute | solution.py:346
  88.3 3.5 %all-to-all-done.3.refs_0_ = bf16[8,36,16,128]{3,2,1,0:T(8,128)(2,1)S(1)} async-done(((bf16[8,36,16,128]{3,2,1,0:T(8,128)(2,1)}), bf16[8,36,16,128]{3,2,1,0:T(8,128)(2,1)S(1)}, u32[]{:S(2)}, u32[]{:S(2)}) %all-to-all-start.3) | async-done | bytes 1179680 | tf_op jit(solution)/shard_map/all_to_all | solution.py:354
  92.6 3.4 %all-to-all-start.4 = ((bf16[8,8,16,128]{3,2,1,0:T(8,128)(2,1)}), bf16[8,8,16,128]{3,2,1,0:T(8,128)(2,1)S(1)}, u32[]{:S(2)}, u32[]{:S(2)}) async-start(bf16[8,8,16,128]{3,2,1,0:T(8,128)(2,1)} %shard_map.130), calls=%async_computation.4 | async-start | bytes 524288 | tf_op jit(solution)/shard_map/all_to_all | solution.py:470
  96.0 4.6 %collective-permute-start.6 = (bf16[64,1024]{1,0:T(8,128)(2,1)S(1)}, bf16[64,1024]{1,0:T(8,128)(2,1)S(1)}, u32[]{:S(2)}, u32[]{:S(2)}) collective-permute-start(bf16[64,1024]{1,0:T(8,128)(2,1)S(1)} %get-tuple-element.32), channel_id=1, source_target_pairs={{1,2},{2,1},{3,4},{4,3},{5,6},{6,5},{7,8},{8,7},{9,10},{10,9},{11,... | collective-permute-start | bytes 393224 | tf_op jit(solution)/shard_map/ppermute | solution.py:342
  100.7 5.9 %all-to-all-done.4.refs_0_ = bf16[8,8,16,128]{3,2,1,0:T(8,128)(2,1)S(1)} async-done(((bf16[8,8,16,128]{3,2,1,0:T(8,128)(2,1)}), bf16[8,8,16,128]{3,2,1,0:T(8,128)(2,1)S(1)}, u32[]{:S(2)}, u32[]{:S(2)}) %all-to-all-start.4) | async-done | bytes 262176 | tf_op jit(solution)/shard_map/all_to_all | solution.py:470
  107.2 5.8 %all-to-all-start.5 = ((bf16[4,5,16,128]{3,2,1,0:T(8,128)(2,1)}), bf16[4,5,16,128]{3,2,1,0:T(8,128)(2,1)S(1)}, u32[]{:S(2)}, u32[]{:S(2)}) async-start(bf16[4,5,16,128]{3,2,1,0:T(8,128)(2,1)} %shard_map.131), calls=%async_computation.5 | async-start | bytes 163840 | tf_op jit(solution)/shard_map/all_to_all | solution.py:478
  113.0 2.3 %shard_map.129 = bf16[1,448,1024]{2,1,0:T(8,128)(2,1)} custom-call(s32[1]{0:T(128)} %bitcast.refs_0_, bf16[64,1024]{1,0:T(8,128)(2,1)S(1)} %collective-permute-done.5.refs_1_, bf16[64,1024]{1,0:T(8,128)(2,1)S(1)} %collective-permute-done.6.refs_2_, bf16[448,1024]{1,0:T(8,128)(2,1)} %get-tuple-element.33.refs_3_, f32[128,1024]{1,0:T(8,128)} %get-tuple-element.34.refs_4_), custom_call_target="tpu_custom_call" | custom-call | bytes 2621440 | tf_op jit(solution)/shard_map/pallas_call | solution.py:74
  115.3 5.1 %all-to-all-done.5.refs_0_ = bf16[4,5,16,128]{3,2,1,0:T(8,128)(2,1)S(1)} async-done(((bf16[4,5,16,128]{3,2,1,0:T(8,128)(2,1)}), bf16[4,5,16,128]{3,2,1,0:T(8,128)(2,1)S(1)}, u32[]{:S(2)}, u32[]{:S(2)}) %all-to-all-start.5) | async-done | bytes 81952 | tf_op jit(solution)/shard_map/all_to_all | solution.py:478
  121.3 15.5 %all_to_all.35.refs_1_ = bf16[16,5,16,128]{3,2,1,0:T(8,128)(2,1)S(1)} all-to-all(bf16[16,5,16,128]{3,2,1,0:T(8,128)(2,1)} %shard_map.132), channel_id=1, replica_groups=mesh['mem'=8,'z'=8,'y'=4,'core'=2] {'mem','core'}, dimensions={0} | all-to-all | bytes 655360 | tf_op jit(solution)/shard_map/all_to_all | solution.py:495
  (48 shorter events, 12.8 us)
Async XLA Ops:
  0.6 8.1 %copy-start.2 = (bf16[1,448,1024]{2,1,0:T(8,128)(2,1)S(1)}, bf16[1,448,1024]{2,1,0:T(8,128)(2,1)}, u32[]{:S(2)}) copy-start(bf16[1,448,1024]{2,1,0:T(8,128)(2,1)} %param.10) | copy-start | bytes 2752516
  1.6 12.2 %copy-start.1 = (bf16[16,1024]{1,0:T(8,128)(2,1)S(1)}, bf16[16,1024]{1,0:T(8,128)(2,1)}, u32[]{:S(2)}) copy-start(bf16[16,1024]{1,0:T(8,128)(2,1)} %refs_1_.2) | copy-start | bytes 98308
  2.7 13.3 %copy-start.7 = (f32[448]{0:T(512)S(1)}, f32[448]{0:T(512)}, u32[]{:S(2)}) copy-start(f32[448]{0:T(512)} %param.13) | copy-start | bytes 5380
  2.7 13.3 %copy-start.8 = (s32[448]{0:T(512)S(1)}, s32[448]{0:T(512)}, u32[]{:S(2)}) copy-start(s32[448]{0:T(512)} %param.15) | copy-start | bytes 5380
  2.7 31.7 %copy-start.9 = (f32[100]{0:T(128)S(1)}, f32[100]{0:T(128)}, u32[]{:S(2)}) copy-start(f32[100]{0:T(128)} %param.14) | copy-start | bytes 1204
  2.7 31.8 %copy-start.6 = (bf16[100,448]{1,0:T(8,128)(2,1)S(1)}, bf16[100,448]{1,0:T(8,128)(2,1)}, u32[]{:S(2)}) copy-start(bf16[100,448]{1,0:T(8,128)(2,1)} %param.12) | copy-start | bytes 268804
  2.7 15.7 %all-to-all-start = ((bf16[8,22,16,128]{3,2,1,0:T(8,128)(2,1)}), bf16[8,22,16,128]{3,2,1,0:T(8,128)(2,1)S(1)}, u32[]{:S(2)}, u32[]{:S(2)}) async-start(bf16[8,22,16,128]{3,2,1,0:T(8,128)(2,1)} %shard_map.122), calls=%async_computation | async-start | bytes 1441792 | tf_op jit(solution)/shard_map/all_to_all | solution.py:354
  8.7 33.1 %collective-permute-start.2 = (bf16[64,1024]{1,0:T(8,128)(2,1)S(1)}, bf16[64,1024]{1,0:T(8,128)(2,1)S(1)}, u32[]{:S(2)}, u32[]{:S(2)}) collective-permute-start(bf16[64,1024]{1,0:T(8,128)(2,1)S(1)} %get-tuple-element.41), channel_id=1, source_target_pairs={{1,2},{2,1},{3,4},{4,3},{5,6},{6,5},{7,8},{8,7},{9,10},{10,9},{11,... | collective-permute-start | bytes 393224 | tf_op jit(solution)/shard_map/ppermute | solution.py:342
  13.8 26.2 %copy-start.3 = (s32[8,448]{1,0:T(8,128)S(1)}, s32[8,448]{1,0:T(8,128)}, u32[]{:S(2)}) copy-start(s32[8,448]{1,0:T(8,128)} %refs_0_.1) | copy-start | bytes 43012
  13.9 26.2 %copy-start.4 = (f32[8,448]{1,0:T(8,128)S(1)}, f32[8,448]{1,0:T(8,128)}, u32[]{:S(2)}) copy-start(f32[8,448]{1,0:T(8,128)} %refs_1_.3) | copy-start | bytes 43012
  13.9 3.3 %collective-permute-start = (bf16[80,1024]{1,0:T(8,128)(2,1)S(1)}, bf16[80,1024]{1,0:T(8,128)(2,1)S(1)}, u32[]{:S(2)}, u32[]{:S(2)}) collective-permute-start(bf16[80,1024]{1,0:T(8,128)(2,1)S(1)} %pad_maximum_fusion), channel_id=1, source_target_pairs={{0,1},{1,0},{2,3},{3,2},{4,5},{5,4},{6,7},{7,6},{8,9},{9,8},{10,11... | collective-permute-start | bytes 491528 | tf_op jit(solution)/shard_map/ppermute | solution.py:346
  18.4 27.3 %all-to-all-start.1 = ((bf16[32,16,128]{2,1,0:T(8,128)(2,1)}), bf16[32,16,128]{2,1,0:T(8,128)(2,1)S(1)}, u32[]{:S(2)}, u32[]{:S(2)}) async-start(bf16[32,16,128]{2,1,0:T(8,128)(2,1)} %shard_map.121), calls=%async_computation.1 | async-start | bytes 262144 | tf_op jit(solution)/shard_map/all_to_all | solution.py:350
  35.0 11.7 %copy-start = (bf16[112,448]{1,0:T(8,128)(2,1)}, bf16[112,448]{1,0:T(8,128)(2,1)S(1)}, u32[]{:S(2)}) copy-start(bf16[112,448]{1,0:T(8,128)(2,1)S(1)} %shard_map.123.refs_4_) | copy-start | bytes 301060
  35.0 6.8 %collective-permute-start.1 = (bf16[112,448]{1,0:T(8,128)(2,1)S(1)}, bf16[112,448]{1,0:T(8,128)(2,1)S(1)}, u32[]{:S(2)}, u32[]{:S(2)}) collective-permute-start(bf16[112,448]{1,0:T(8,128)(2,1)S(1)} %shard_map.123.refs_4_), channel_id=1, source_target_pairs={{0,1},{1,0},{2,3},{3,2},{4,5},{5,4},{6,7},{7,6},{8,9},{9,8},{10,11... | collective-permute-start | bytes 301064 | tf_op jit(solution)/shard_map/ppermute | solution.py:346
  46.8 17.3 %all-to-all-start.2 = ((bf16[8,32,16,128]{3,2,1,0:T(8,128)(2,1)}), bf16[8,32,16,128]{3,2,1,0:T(8,128)(2,1)S(1)}, u32[]{:S(2)}, u32[]{:S(2)}) async-start(bf16[8,32,16,128]{3,2,1,0:T(8,128)(2,1)} %shard_map.125), calls=%async_computation.2 | async-start | bytes 2097152 | tf_op jit(solution)/shard_map/all_to_all | solution.py:354
  51.0 9.9 %copy-start.5 = (bf16[1024,100]{0,1:T(8,128)(2,1)S(1)}, bf16[1024,100]{0,1:T(8,128)(2,1)}, u32[]{:S(2)}) copy-start(bf16[1024,100]{0,1:T(8,128)(2,1)} %param.19) | copy-start | bytes 614404
  54.7 9.3 %collective-permute-start.3 = (bf16[448,1536]{1,0:T(8,128)(2,1)}, bf16[448,1536]{1,0:T(8,128)(2,1)}, u32[]{:S(2)}, u32[]{:S(2)}) collective-permute-start(bf16[448,1536]{1,0:T(8,128)(2,1)} %get-tuple-element.27.refs_7_), channel_id=1, source_target_pairs={{0,1},{1,0},{2,3},{3,2},{4,5},{5,4},{6,7},{7,6},{8,9},{9,8},{10,11... | collective-permute-start | bytes 4128776 | tf_op jit(solution)/shard_map/ppermute | solution.py:346
  69.9 5.6 %copy-start.10 = (bf16[448,1024]{1,0:T(8,128)(2,1)S(1)}, bf16[448,1024]{1,0:T(8,128)(2,1)}, u32[]{:S(2)}) copy-start(bf16[448,1024]{1,0:T(8,128)(2,1)} %get-tuple-element.28) | copy-start | bytes 2752516
  69.9 21.9 %all-to-all-start.3 = ((bf16[8,36,16,128]{3,2,1,0:T(8,128)(2,1)}), bf16[8,36,16,128]{3,2,1,0:T(8,128)(2,1)S(1)}, u32[]{:S(2)}, u32[]{:S(2)}) async-start(bf16[8,36,16,128]{3,2,1,0:T(8,128)(2,1)} %get-tuple-element.35), calls=%async_computation.3 | async-start | bytes 2359296 | tf_op jit(solution)/shard_map/all_to_all | solution.py:354
  75.4 5.0 %collective-permute-start.4 = (bf16[448,1024]{1,0:T(8,128)(2,1)S(1)}, bf16[448,1024]{1,0:T(8,128)(2,1)S(1)}, u32[]{:S(2)}, u32[]{:S(2)}) collective-permute-start(bf16[448,1024]{1,0:T(8,128)(2,1)S(1)} %copy-done.10), channel_id=1, source_target_pairs={{0,1},{1,0},{2,3},{3,2},{4,5},{5,4},{6,7},{7,6},{8,9},{9,8},{10,11... | collective-permute-start | bytes 2752520 | tf_op jit(solution)/shard_map/ppermute | solution.py:346
  85.0 3.3 %collective-permute-start.5 = (bf16[64,1024]{1,0:T(8,128)(2,1)S(1)}, bf16[64,1024]{1,0:T(8,128)(2,1)S(1)}, u32[]{:S(2)}, u32[]{:S(2)}) collective-permute-start(bf16[64,1024]{1,0:T(8,128)(2,1)S(1)} %get-tuple-element.31), channel_id=1, source_target_pairs={{0,1},{1,0},{2,3},{3,2},{4,5},{5,4},{6,7},{7,6},{8,9},{9,8},{10,11... | collective-permute-start | bytes 393224 | tf_op jit(solution)/shard_map/ppermute | solution.py:346
  92.6 13.9 %all-to-all-start.4 = ((bf16[8,8,16,128]{3,2,1,0:T(8,128)(2,1)}), bf16[8,8,16,128]{3,2,1,0:T(8,128)(2,1)S(1)}, u32[]{:S(2)}, u32[]{:S(2)}) async-start(bf16[8,8,16,128]{3,2,1,0:T(8,128)(2,1)} %shard_map.130), calls=%async_computation.4 | async-start | bytes 524288 | tf_op jit(solution)/shard_map/all_to_all | solution.py:470
  96.0 16.9 %collective-permute-start.6 = (bf16[64,1024]{1,0:T(8,128)(2,1)S(1)}, bf16[64,1024]{1,0:T(8,128)(2,1)S(1)}, u32[]{:S(2)}, u32[]{:S(2)}) collective-permute-start(bf16[64,1024]{1,0:T(8,128)(2,1)S(1)} %get-tuple-element.32), channel_id=1, source_target_pairs={{1,2},{2,1},{3,4},{4,3},{5,6},{6,5},{7,8},{8,7},{9,10},{10,9},{11,... | collective-permute-start | bytes 393224 | tf_op jit(solution)/shard_map/ppermute | solution.py:342
  107.2 13.2 %all-to-all-start.5 = ((bf16[4,5,16,128]{3,2,1,0:T(8,128)(2,1)}), bf16[4,5,16,128]{3,2,1,0:T(8,128)(2,1)S(1)}, u32[]{:S(2)}, u32[]{:S(2)}) async-start(bf16[4,5,16,128]{3,2,1,0:T(8,128)(2,1)} %shard_map.131), calls=%async_computation.5 | async-start | bytes 163840 | tf_op jit(solution)/shard_map/all_to_all | solution.py:478
  (1 other events, 4.9 us)
